TPU v7x, 32 devices: a whole 2x2x4 slice. The times are simulated.
32 devices in a mesh: dp: 8 (over y, x, core), mp: 4 (over z).
Axes of the slice: x: 2, y: 2, z: 4, core: 2. Of those that a mesh axis runs over, the one named last changes fastest.
Arguments:
- tokens: bfloat16 [8, 1536, 768], P('dp'), may hold values from -6 to 6
- lengths: int32 [8, 8], P('dp'), may hold values from 1 to 512, 1536 in all within a row
- query_weight: float32 [768, 768], P('dp', 'mp'), may hold values from -0.3125 to 0.3125
- key_weight: float32 [768, 768], P('dp', 'mp'), may hold values from -0.3125 to 0.3125
- value_weight: float32 [768, 768], P('dp', 'mp'), may hold values from -0.21875 to 0.21875
- out_weight: float32 [768, 768], P('mp', 'dp'), may hold values from -0.875 to 0.875
- attn_gain: float32 [768], P('dp'), may hold values from 0.1 to 1.9
- gate_weight: float32 [768, 2048], P('dp', 'mp'), may hold values from -0.21875 to 0.21875
- up_weight: float32 [768, 2048], P('dp', 'mp'), may hold values from -0.21875 to 0.21875
- down_weight: float32 [2048, 768], P('mp', 'dp'), may hold values from -0.1875 to 0.1875
- ffn_gain: float32 [768], P('dp'), may hold values from 0.1 to 1.9
- cotangent: bfloat16 [8, 1536, 768], P('dp'), may hold values from -6 to 6
Outputs:
- output: bfloat16 [8, 1536, 768], P('dp')
- grad_tokens: float32 [8, 1536, 768], P('dp')
- grad_query: float32 [768, 768], P('dp', 'mp')
- grad_key: float32 [768, 768], P('dp', 'mp')
- grad_value: float32 [768, 768], P('dp', 'mp')
- grad_out: float32 [768, 768], P('mp', 'dp')
- grad_attn_gain: float32 [768], P('dp')
- grad_gate: float32 [768, 2048], P('dp', 'mp')
- grad_up: float32 [768, 2048], P('dp', 'mp')
- grad_down: float32 [2048, 768], P('mp', 'dp')
- grad_ffn_gain: float32 [768], P('dp')
Inputs may be any that keep to these rules, and one draw needn't show every extreme that they name: Each row's lengths add up to 1536; the longest segment of a row has 512 positions.
All inputs are finite; a program needn't handle non-finite values.
Results may differ from a plain program's by a relative error of at most 0.014.
The roundings to bfloat16 on the way count: a program that leaves them out, or rounds other values in their place, can miss the bound.
Values may be sent and summed in bfloat16 or wider, within the bound.
A program may use at most 192 MiB of HBM per device.

v0:
```python
import jax
import jax.numpy as jnp
from jax import lax
from jax.sharding import PartitionSpec as P

HD = 64


EPSILON = 1e-06
GELU_COEF = 0.7978845608028654


def rms_scale(values, gain):
    return values * lax.rsqrt(jnp.mean(values * values, axis=-1, keepdims=True) + EPSILON) * gain


def gelu_tanh(values):
    return (
        0.5 * values * (1.0 + jnp.tanh(GELU_COEF * (values + 0.044715 * values * values * values)))
    )


def gated_unit(gate, upward):
    return gelu_tanh(gate) * upward


def matmul(left, right):
    return jnp.dot(left, right, preferred_element_type=jnp.float32)


def matmul_right_t(left, right):
    return lax.dot_general(
        left, right, (((1,), (1,)), ((), ())), preferred_element_type=jnp.float32
    )


def matmul_left_t(left, right):
    return lax.dot_general(
        left, right, (((0,), (0,)), ((), ())), preferred_element_type=jnp.float32
    )


def segment_numbers(lengths, seq):
    ends = jnp.cumsum(lengths, axis=1)
    places = jnp.arange(seq, dtype=jnp.int32)
    return jnp.sum((ends[:, None, :] <= places[None, :, None]).astype(jnp.int32), axis=2)


def per_device(
    tokens,
    lengths,
    query_weight,
    key_weight,
    value_weight,
    out_weight,
    attn_gain,
    gate_weight,
    up_weight,
    down_weight,
    ffn_gain,
    cotangent,
):
    rows, seq, width = tokens.shape
    count = rows * seq
    block = min(512, seq)
    blocks_row = seq // block
    total_blocks = rows * blocks_row
    scale = HD ** (-0.5)
    low_type = jnp.bfloat16
    gathered = (
        lax.all_gather(query_weight.astype(low_type), "dp", axis=0, tiled=True),
        lax.all_gather(key_weight.astype(low_type), "dp", axis=0, tiled=True),
        lax.all_gather(value_weight.astype(low_type), "dp", axis=0, tiled=True),
        lax.all_gather(out_weight.astype(low_type), "dp", axis=1, tiled=True),
        lax.all_gather(attn_gain.astype(low_type), "dp", axis=0, tiled=True),
        lax.all_gather(gate_weight.astype(low_type), "dp", axis=0, tiled=True),
        lax.all_gather(up_weight.astype(low_type), "dp", axis=0, tiled=True),
        lax.all_gather(down_weight.astype(low_type), "dp", axis=1, tiled=True),
        lax.all_gather(ffn_gain.astype(low_type), "dp", axis=0, tiled=True),
    )
    (
        full_query,
        full_key,
        full_value,
        full_out,
        gain_attn,
        full_gate,
        full_up,
        full_down,
        gain_ffn,
    ) = gathered
    segment = segment_numbers(lengths, seq)
    flat = tokens.reshape(count, width).astype(jnp.float32)
    normed_attn, attn_norm_back = jax.vjp(rms_scale, flat, gain_attn.astype(jnp.float32))
    normed_low = normed_attn.astype(low_type)
    query = matmul(normed_low, full_query).astype(low_type)
    keys = matmul(normed_low, full_key).astype(low_type)
    values = matmul(normed_low, full_value).astype(low_type)
    heads = query.shape[1] // HD
    query4 = query.reshape(rows, seq, heads, HD)
    keys4 = keys.reshape(rows, seq, heads, HD)
    values4 = values.reshape(rows, seq, heads, HD)

    def block_scores(index):
        row = index // blocks_row
        begin = index % blocks_row * block
        query_block = lax.dynamic_slice(query4, (row, begin, 0, 0), (1, block, heads, HD))[0]
        keys_row = lax.dynamic_index_in_dim(keys4, row, 0, keepdims=False)
        values_row = lax.dynamic_index_in_dim(values4, row, 0, keepdims=False)
        segment_row = lax.dynamic_index_in_dim(segment, row, 0, keepdims=False)
        segment_block = lax.dynamic_slice_in_dim(segment_row, begin, block, 0)
        scores = (
            jnp.einsum("qhd,khd->hqk", query_block, keys_row, preferred_element_type=jnp.float32)
            * scale
        )
        same = segment_block[:, None] == segment_row[None, :]
        scores = jnp.where(same[None], scores, -1e30)
        return (row, begin, query_block, keys_row, values_row, scores)

    def attend(index):
        row, begin, query_block, keys_row, values_row, scores = block_scores(index)
        totals = jax.nn.logsumexp(scores, axis=-1)
        attention = jnp.exp(scores - totals[:, :, None]).astype(low_type)
        mixed = jnp.einsum(
            "hqk,khd->qhd", attention, values_row, preferred_element_type=jnp.float32
        )
        return (mixed, totals)

    mixed_all, log_totals = lax.map(attend, jnp.arange(total_blocks, dtype=jnp.int32))
    attended = mixed_all.reshape(count, heads * HD).astype(low_type)
    attn_part = matmul(attended, full_out)
    attn_branch = lax.psum(attn_part, "mp")
    hidden = flat + attn_branch
    normed_ffn, ffn_norm_back = jax.vjp(rms_scale, hidden, gain_ffn.astype(jnp.float32))
    ffn_low = normed_ffn.astype(low_type)
    gate = matmul(ffn_low, full_gate)
    upward = matmul(ffn_low, full_up)
    inner = gated_unit(gate, upward).astype(low_type)
    ffn_part = matmul(inner, full_down)
    ffn_branch = lax.psum(ffn_part.astype(jnp.bfloat16), "mp").astype(jnp.float32)
    output = (hidden + ffn_branch).astype(low_type).reshape(rows, seq, width)
    upstream = cotangent.reshape(count, width)
    grad_down = matmul_left_t(inner, upstream)
    grad_inner = matmul_right_t(upstream, full_down)
    _, unit_back = jax.vjp(gated_unit, gate, upward)
    grad_gate_act, grad_up_act = unit_back(grad_inner)
    grad_gate_low = grad_gate_act.astype(low_type)
    grad_up_low = grad_up_act.astype(low_type)
    grad_gate = matmul_left_t(ffn_low, grad_gate_low)
    grad_up = matmul_left_t(ffn_low, grad_up_low)
    ffn_input_part = matmul_right_t(grad_gate_low, full_gate) + matmul_right_t(grad_up_low, full_up)
    ffn_input = lax.psum(ffn_input_part, "mp")
    grad_hidden_norm, grad_ffn_gain = ffn_norm_back(ffn_input)
    grad_hidden = upstream.astype(jnp.float32) + grad_hidden_norm
    branch_low = grad_hidden.astype(low_type)
    grad_out = matmul_left_t(attended, branch_low)
    grad_attended = matmul_right_t(branch_low, full_out).astype(low_type)
    grad_mixed4 = grad_attended.reshape(rows, seq, heads, HD)

    def attend_back(carry, index):
        key_total, value_total = carry
        row, begin, query_block, keys_row, values_row, scores = block_scores(index)
        totals_block = lax.dynamic_index_in_dim(log_totals, index, 0, keepdims=False)
        attention = jnp.exp(scores - totals_block[:, :, None])
        grad_block = lax.dynamic_slice(grad_mixed4, (row, begin, 0, 0), (1, block, heads, HD))[0]
        grad_attention = jnp.einsum(
            "qhd,khd->hqk", grad_block, values_row, preferred_element_type=jnp.float32
        )
        delta = jnp.sum(grad_attention * attention, axis=-1, keepdims=True)
        grad_scores = (attention * (grad_attention - delta)).astype(low_type)
        grad_query_block = (
            jnp.einsum("hqk,khd->qhd", grad_scores, keys_row, preferred_element_type=jnp.float32)
            * scale
        )
        key_part = (
            jnp.einsum("hqk,qhd->khd", grad_scores, query_block, preferred_element_type=jnp.float32)
            * scale
        )
        value_part = jnp.einsum(
            "hqk,qhd->khd",
            attention.astype(low_type),
            grad_block,
            preferred_element_type=jnp.float32,
        )
        key_row = lax.dynamic_index_in_dim(key_total, row, 0, keepdims=False) + key_part
        value_row = lax.dynamic_index_in_dim(value_total, row, 0, keepdims=False) + value_part
        key_total = lax.dynamic_update_index_in_dim(key_total, key_row, row, 0)
        value_total = lax.dynamic_update_index_in_dim(value_total, value_row, row, 0)
        return ((key_total, value_total), grad_query_block)

    zeros = jnp.zeros((rows, seq, heads, HD), jnp.float32)
    (key_total, value_total), query_blocks = lax.scan(
        attend_back, (zeros, zeros), jnp.arange(total_blocks, dtype=jnp.int32)
    )
    grad_query_low = query_blocks.reshape(count, heads * HD).astype(low_type)
    grad_key_low = key_total.reshape(count, heads * HD).astype(low_type)
    grad_value_low = value_total.reshape(count, heads * HD).astype(low_type)
    grad_query = matmul_left_t(normed_low, grad_query_low)
    grad_key = matmul_left_t(normed_low, grad_key_low)
    grad_value = matmul_left_t(normed_low, grad_value_low)
    attn_input_part = (
        matmul_right_t(grad_query_low, full_query)
        + matmul_right_t(grad_key_low, full_key)
        + matmul_right_t(grad_value_low, full_value)
    )
    attn_input = lax.psum(attn_input_part, "mp")
    grad_flat_norm, grad_attn_gain = attn_norm_back(attn_input)
    grad_tokens = (grad_hidden + grad_flat_norm).reshape(rows, seq, width)
    results = tuple(
        (
            lax.psum_scatter(grad_query, "dp", scatter_dimension=0, tiled=True),
            lax.psum_scatter(grad_key, "dp", scatter_dimension=0, tiled=True),
            lax.psum_scatter(grad_value, "dp", scatter_dimension=0, tiled=True),
            lax.psum_scatter(grad_out, "dp", scatter_dimension=1, tiled=True),
            lax.psum_scatter(grad_attn_gain, "dp", scatter_dimension=0, tiled=True),
            lax.psum_scatter(grad_gate, "dp", scatter_dimension=0, tiled=True),
            lax.psum_scatter(grad_up, "dp", scatter_dimension=0, tiled=True),
            lax.psum_scatter(grad_down, "dp", scatter_dimension=1, tiled=True),
            lax.psum_scatter(grad_ffn_gain, "dp", scatter_dimension=0, tiled=True),
        )
    )
    return (output, grad_tokens) + results


def solution(mesh):
    return jax.shard_map(
        per_device,
        mesh=mesh,
        in_specs=(
            P("dp", None, None),
            P("dp", None),
            P("dp", "mp"),
            P("dp", "mp"),
            P("dp", "mp"),
            P("mp", "dp"),
            P("dp"),
            P("dp", "mp"),
            P("dp", "mp"),
            P("mp", "dp"),
            P("dp"),
            P("dp", None, None),
        ),
        out_specs=(
            P("dp", None, None),
            P("dp", None, None),
            P("dp", "mp"),
            P("dp", "mp"),
            P("dp", "mp"),
            P("mp", "dp"),
            P("dp"),
            P("dp", "mp"),
            P("dp", "mp"),
            P("mp", "dp"),
            P("dp"),
        ),
        check_vma=False,
    )
```

profile of v0, /device:TPU:0, one launch (start us, length us, event | category | flops | bytes accessed | tf_op | source)
XLA Modules:
  0.0 1129.6 jit_solution(17822091823279691268)
XLA Ops:
  12.0 15.7 %all-reduce.5 = (bf16[768]{0:T(1024)(128)(2,1)S(1)}, bf16[768]{0:T(1024)(128)(2,1)}) all-reduce(bf16[768]{0:T(1024)(128)(2,1)S(1)} %dynamic-update-slice, bf16[768]{0:T(1024)(128)(2,1)S(1)} %dynamic-update-slice.1), channel_id=1, replica_groups=mesh['dp'=8,'mp'=4] {'dp'}, use_global_device_ids=true, to_apply=%add | all-reduce | flops 1536 | bytes 6144
  33.7 9.6 all_gather.31
  43.3 9.5 all_gather.30
  52.8 8.7 all_gather.29
  61.5 9.7 all_gather.28
  76.9 37.3 %while.30 = (s32[]{:T(128)}, bf16[3,512,3,64]{1,3,2,0:T(8,128)(2,1)}, f32[3,3,512]{2,1,0:T(4,128)}, s32[3]{0:T(128)S(1)}, s32[1,1536]{1,0:T(1,128)S(1)}, /*index...) while((s32[]{:T(128)}, ...), condition=%wide.region_6.7_spmd, body=%wide.region_3.6_spmd.sunk | while | flops 630730752 | bytes 38048228 | solution.py:129
  79.9 2.9 fusion.150
  116.8 4.0 fusion.91
  124.3 10.9 all_gather.35
  135.2 10.9 all_gather.34
  146.1 11.1 all_gather.33
  157.1 136.1 %all-reduce.11.cloned.1.call-done = f32[1536,768]{1,0:T(8,128)} async-done(((f32[1536,768]{1,0:T(8,128)}), f32[1536,768]{1,0:T(8,128)}) %all-reduce.11.cloned.1.call-update) | async-done | bytes 4718608 | tf_op jit(solution)/shard_map/psum | solution.py:132
  293.2 3.0 multiply_reduce_fusion.3
  301.5 5.1 multiply_convert_fusion.2
  308.3 3.7 convolution_add_fusion
  313.2 4.3 convolution_convert_fusion
  317.5 165.7 %all-reduce.15.cloned.1.call-done = f32[1536,768]{1,0:T(8,128)} async-done(((f32[1536,768]{1,0:T(8,128)}), f32[1536,768]{1,0:T(8,128)}) %all-reduce.15.cloned.1.call-update) | async-done | bytes 4718608 | tf_op jit(solution)/shard_map/psum | solution.py:152
  483.2 5.1 multiply_reduce_fusion.1
  488.3 92.5 %all-reduce.13.cloned.1.call-done = bf16[1536,768]{1,0:T(8,128)(2,1)} async-done(((bf16[1536,768]{1,0:T(8,128)(2,1)}), bf16[1536,768]{1,0:T(8,128)(2,1)}) %all-reduce.13.cloned.1.call-update) | async-done | bytes 2359312 | tf_op jit(solution)/shard_map/psum | solution.py:140
  580.8 7.3 fusion.61
  592.2 4.1 convolution_convert_fusion.1
  598.0 104.8 %while.31 = (s32[]{:T(128)}, f32[1,1536,3,64]{1,3,2,0:T(8,128)S(1)}, f32[1,1536,3,64]{1,3,2,0:T(8,128)S(1)}, bf16[3,512,3,64]{1,3,2,0:T(8,128)(2,1)}, s32[3]{0:T...) while((s32[]{:T(128)}, ...), condition=%wide.region_14.15_spmd, body=%wide.region_12.14_spmd.sunk | while | flops 1532951040 | bytes 139059760 | solution.py:192
  604.3 3.6 subtract_exponential_fusion.2
  611.6 5.2 multiply_reduce_fusion.5
  616.8 9.5 multiply_convert_fusion.5
  626.3 4.7 fusion.164
  639.3 3.6 subtract_exponential_fusion.2
  646.6 5.2 multiply_reduce_fusion.5
  651.7 9.5 multiply_convert_fusion.5
  661.2 4.7 fusion.164
  674.2 3.6 subtract_exponential_fusion.2
  681.5 5.2 multiply_reduce_fusion.5
  686.7 9.5 multiply_convert_fusion.5
  696.1 4.7 fusion.164
  706.6 3.0 add_add_fusion.2
  711.1 4.2 fusion.97
  715.4 4.7 fusion.98
  720.4 4.9 fusion.72
  734.0 146.9 %all-reduce.17.cloned.1.call-done = f32[1536,768]{1,0:T(8,128)} async-done(((f32[1536,768]{1,0:T(8,128)}), f32[1536,768]{1,0:T(8,128)}) %all-reduce.17.cloned.1.call-update) | async-done | bytes 4718608 | tf_op jit(solution)/shard_map/psum | solution.py:206
  880.9 3.7 fusion.56
  884.6 13.9 %all-reduce.4 = (f32[768]{0:T(1024)S(1)}, f32[768]{0:T(1024)S(1)}) all-reduce(f32[768]{0:T(1024)S(1)} %get-tuple-element.261, f32[768]{0:T(1024)S(1)} %copy-done.39), channel_id=6, replica_groups=mesh['dp'=8,'mp'=4] {'dp'}, use_global_device_ids=true, to_apply=%region_22.23.clone | all-reduce | flops 1536 | bytes 12288
  899.7 5.8 fusion.63
  905.5 16.6 %reduce-scatter.16.cloned.1.call-done = f32[96,512]{1,0:T(8,128)} async-done(((f32[768,512]{1,0:T(8,128)}), f32[96,512]{1,0:T(8,128)}) %reduce-scatter.16.cloned.1.call-update) | async-done | bytes 196624 | tf_op jit(solution)/shard_map/reduce_scatter | solution.py:216
  922.2 42.3 %reduce-scatter.18.cloned.1.call-done = f32[96,512]{1,0:T(8,128)} async-done(((f32[768,512]{1,0:T(8,128)}), f32[96,512]{1,0:T(8,128)}) %reduce-scatter.18.cloned.1.call-update) | async-done | bytes 196624 | tf_op jit(solution)/shard_map/reduce_scatter | solution.py:217
  964.5 42.3 %reduce-scatter.20.cloned.1.call-done = f32[512,96]{0,1:T(8,128)} async-done(((f32[512,768]{0,1:T(8,128)}), f32[512,96]{0,1:T(8,128)}) %reduce-scatter.20.cloned.1.call-update) | async-done | bytes 196624 | tf_op jit(solution)/shard_map/reduce_scatter | solution.py:218
  1006.8 38.7 %reduce-scatter.14.cloned.1.call-done = f32[96,192]{1,0:T(8,128)} async-done(((f32[768,192]{1,0:T(8,128)}), f32[96,192]{1,0:T(8,128)}) %reduce-scatter.14.cloned.1.call-update) | async-done | bytes 73744 | tf_op jit(solution)/shard_map/reduce_scatter | solution.py:213
  1045.5 38.6 %reduce-scatter.12.cloned.1.call-done = f32[96,192]{1,0:T(8,128)} async-done(((f32[768,192]{1,0:T(8,128)}), f32[96,192]{1,0:T(8,128)}) %reduce-scatter.12.cloned.1.call-update) | async-done | bytes 73744 | tf_op jit(solution)/shard_map/reduce_scatter | solution.py:212
  1084.1 38.8 %reduce-scatter.10.cloned.1.call-done = f32[96,192]{1,0:T(8,128)} async-done(((f32[768,192]{1,0:T(8,128)}), f32[96,192]{1,0:T(8,128)}) %reduce-scatter.10.cloned.1.call-update) | async-done | bytes 73744 | tf_op jit(solution)/shard_map/reduce_scatter | solution.py:211
  (252 shorter events, 110.2 us)
Async XLA Ops:
  7.2 64.0 %copy-start.4 = (bf16[1,1536,768]{2,1,0:T(8,128)(2,1)S(1)}, bf16[1,1536,768]{2,1,0:T(8,128)(2,1)}, u32[]{:S(2)}) copy-start(bf16[1,1536,768]{2,1,0:T(8,128)(2,1)} %param.16) | copy-start | bytes 7077892
  7.2 286.0 %all-reduce.11.cloned.1.call-start = ((), (), s32[]{:S(2)}) async-start(), calls=%async_computation.7 | async-start | bytes 9437184 | tf_op jit(solution)/shard_map/psum | solution.py:132
  27.7 45.4 %copy-start.37 = (f32[768]{0:T(1024)}, f32[768]{0:T(1024)S(1)}, u32[]{:S(2)}) copy-start(f32[768]{0:T(1024)S(1)} %convert_element_type.153) | copy-start | bytes 9220
  30.0 43.1 %copy-start.29 = (f32[1536]{0:T(1024)}, f32[1536]{0:T(1024)S(1)}, u32[]{:S(2)}) copy-start(f32[1536]{0:T(1024)S(1)} %fusion.57) | copy-start | bytes 18436
  30.0 44.2 %copy-start.33 = (f32[1536]{0:T(1024)}, f32[1536]{0:T(1024)S(1)}, u32[]{:S(2)}) copy-start(f32[1536]{0:T(1024)S(1)} %fusion.78) | copy-start | bytes 18436
  52.8 21.4 %copy-start.25 = (bf16[768,192]{1,0:T(8,128)(2,1)}, bf16[768,192]{1,0:T(8,128)(2,1)S(1)}, u32[]{:S(2)}) copy-start(bf16[768,192]{1,0:T(8,128)(2,1)S(1)} %all_gather.30) | copy-start | bytes 884740
  61.5 12.7 %copy-start.20 = (bf16[768,192]{1,0:T(8,128)(2,1)}, bf16[768,192]{1,0:T(8,128)(2,1)S(1)}, u32[]{:S(2)}) copy-start(bf16[768,192]{1,0:T(8,128)(2,1)S(1)} %all_gather.29) | copy-start | bytes 884740
  71.2 3.1 copy-start.22
  82.9 2.9 copy-start.15
  85.8 3.5 copy-start.44
  95.3 2.9 copy-start.15
  98.2 3.5 copy-start.44
  110.7 3.5 copy-start.44
  116.8 4.1 copy-start.40
  120.8 362.4 %all-reduce.15.cloned.1.call-start = ((), (), s32[]{:S(2)}) async-start(), calls=%async_computation.9 | async-start | bytes 9437184 | tf_op jit(solution)/shard_map/psum | solution.py:152
  293.2 3.1 copy-start.35
  296.2 3.1 copy-start.3
  296.3 3.1 copy-start.31
  312.1 268.7 %all-reduce.13.cloned.1.call-start = ((), (), s32[]{:S(2)}) async-start(), calls=%async_computation.8 | async-start | bytes 4718592 | tf_op jit(solution)/shard_map/psum | solution.py:140
  313.2 170.0 %copy-start.36 = (f32[768]{0:T(1024)S(1)}, f32[768]{0:T(1024)}, u32[]{:S(2)}) copy-start(f32[768]{0:T(1024)} %convert_element_type.165) | copy-start | bytes 9220
  317.5 414.9 %reduce-scatter.22.cloned.1.call-start = ((), (), s32[]{:S(2)}) async-start(), calls=%async_computation.17 | async-start | bytes 884736
  317.5 170.8 %copy-start.32 = (f32[1536]{0:T(1024)S(1)}, f32[1536]{0:T(1024)}, u32[]{:S(2)}) copy-start(f32[1536]{0:T(1024)} %copy-done.31) | copy-start | bytes 18436
  488.3 102.0 %copy-start.8 = (bf16[24,8,3,512]{3,1,2,0:T(8,128)(2,1)S(1)}, bf16[24,8,3,512]{3,1,2,0:T(8,128)(2,1)}, u32[]{:S(2)}) copy-start(bf16[24,8,3,512]{3,1,2,0:T(8,128)(2,1)} %copy-done.7) | copy-start | bytes 1769476
  588.1 4.1 copy-start.11
  596.4 284.6 %all-reduce.17.cloned.1.call-start = ((), (), s32[]{:S(2)}) async-start(), calls=%async_computation.10 | async-start | bytes 9437184 | tf_op jit(solution)/shard_map/psum | solution.py:206
  598.0 3.8 copy-start.41
  604.3 3.7 copy-start.6
  608.0 3.7 copy-start
  626.3 4.7 copy-start.1
  632.9 3.8 copy-start.41
  639.2 3.7 copy-start.6
  642.9 3.7 copy-start
  661.2 4.7 copy-start.1
  667.9 3.8 copy-start.41
  674.2 3.7 copy-start.6
  677.8 3.7 copy-start
  696.1 4.7 copy-start.1
  709.7 212.5 %reduce-scatter.16.cloned.1.call-start = ((), (), s32[]{:S(2)}) async-start(), calls=%async_computation.14 | async-start | bytes 1769472 | tf_op jit(solution)/shard_map/reduce_scatter | solution.py:216
  715.3 249.2 %reduce-scatter.18.cloned.1.call-start = ((), (), s32[]{:S(2)}) async-start(), calls=%async_computation.15 | async-start | bytes 1769472 | tf_op jit(solution)/shard_map/reduce_scatter | solution.py:217
  720.1 5.2 copy-start.5
  720.1 5.2 copy-start.34
  720.1 5.2 copy-start.38
  720.1 286.7 %reduce-scatter.20.cloned.1.call-start = ((), (), s32[]{:S(2)}) async-start(), calls=%async_computation.16 | async-start | bytes 1769472 | tf_op jit(solution)/shard_map/reduce_scatter | solution.py:218
  725.3 320.3 %reduce-scatter.14.cloned.1.call-start = ((), (), s32[]{:S(2)}) async-start(), calls=%async_computation.13 | async-start | bytes 884736 | tf_op jit(solution)/shard_map/reduce_scatter | solution.py:213
  727.4 356.7 %reduce-scatter.12.cloned.1.call-start = ((), (), s32[]{:S(2)}) async-start(), calls=%async_computation.12 | async-start | bytes 884736 | tf_op jit(solution)/shard_map/reduce_scatter | solution.py:212
  729.5 393.3 %reduce-scatter.10.cloned.1.call-start = ((), (), s32[]{:S(2)}) async-start(), calls=%async_computation.11 | async-start | bytes 884736 | tf_op jit(solution)/shard_map/reduce_scatter | solution.py:211
  732.3 152.3 %copy-start.30 = (f32[1536]{0:T(1024)S(1)}, f32[1536]{0:T(1024)}, u32[]{:S(2)}) copy-start(f32[1536]{0:T(1024)} %copy-done.29) | copy-start | bytes 18436
  732.3 152.3 %copy-start.39 = (f32[768]{0:T(1024)S(1)}, f32[768]{0:T(1024)}, u32[]{:S(2)}) copy-start(f32[768]{0:T(1024)} %get-tuple-element.259) | copy-start | bytes 9220
  (26 other events, 43.6 us)
Sparse Core Ops, SparseCore 0:
  120.9 172.2 all-reduce.10
  312.2 170.9 all-reduce.14
  486.1 94.6 all-reduce.12
  596.5 33.9 reduce-scatter.21
  709.8 171.0 all-reduce.16
  884.7 37.4 reduce-scatter.15
  926.0 38.4 reduce-scatter.17
  968.4 38.4 reduce-scatter.19
  1010.5 34.9 reduce-scatter.13
  1049.1 34.9 reduce-scatter.11
  1087.8 34.9 reduce-scatter.9
where the time goes:
time: 1130 us
  waiting for transfers between devices  759 us (67%)
  matrix products  123 us (11%)
  blocking collectives  99.9 us (9%)
  other arithmetic  82.6 us (7%)
  local copies, waits for them, and re-layouts  38.1 us (3%)
  between operations  15.9 us (1%)
    psum x1, waiting for transfers between devices, per_device(): ffn_input = lax.psum(ffn_input_part, 'mp')  166 us
    psum x1, waiting for transfers between devices, per_device(): attn_input = lax.psum(attn_input_part, 'mp')  147 us
    psum x1, waiting for transfers between devices, per_device(): attn_branch = lax.psum(attn_part, 'mp')  136 us
    psum x1, waiting for transfers between devices, per_device(): lax.psum(ffn_part.astype(jnp.bfloat16), 'mp').astype(jnp.float32)  92.5 us
    reduce_scatter x1, waiting for transfers between devices, per_device(): lax.psum_scatter(grad_down, 'dp', scatter_dimension=1, tiled=True)  42.3 us
    reduce_scatter x1, waiting for transfers between devices, per_device(): lax.psum_scatter(grad_up, 'dp', scatter_dimension=0, tiled=True)  42.3 us
    reduce_scatter x1, waiting for transfers between devices, per_device(): lax.psum_scatter(grad_query, 'dp', scatter_dimension=0, tiled=True)  38.8 us
    reduce_scatter x1, waiting for transfers between devices, per_device(): lax.psum_scatter(grad_value, 'dp', scatter_dimension=0, tiled=True)  38.7 us
  transfers between devices with their start and end apart: 11, of which 10 were waited for; matrix products, arithmetic and copies ran while one was open for 13% of the time, Pallas kernels for 0%

commit v1 on v0

v1 whole, which is shorter than its diff:
```python
import functools
import jax
import jax.numpy as jnp
from jax import lax
from jax.experimental import pallas as pl
from jax.experimental.pallas import tpu as pltpu
from jax.sharding import PartitionSpec as P

EPSILON = 1e-06
GELU_COEF = 0.7978845608028654
GELU_CUBE = 0.044715
CAP = 512
NEG = -1e30
F32 = jnp.float32
BF16 = jnp.bfloat16


def nn(a, b):
    return lax.dot_general(a, b, (((1,), (0,)), ((), ())), preferred_element_type=F32)


def nt(a, b):
    return lax.dot_general(a, b, (((1,), (1,)), ((), ())), preferred_element_type=F32)


def tn(a, b):
    return lax.dot_general(a, b, (((0,), (0,)), ((), ())), preferred_element_type=F32)


def placement(len_ref, bins):
    count = len_ref.shape[1]
    sizes = [len_ref[0, i] for i in range(count)]
    starts = [jnp.int32(0)]
    for i in range(count - 1):
        starts.append(starts[-1] + sizes[i])
    ranks = []
    for i in range(count):
        rank = jnp.int32(0)
        for j in range(count):
            if j < i:
                rank = rank + jnp.where(sizes[j] >= sizes[i], 1, 0)
            elif j > i:
                rank = rank + jnp.where(sizes[j] > sizes[i], 1, 0)
        ranks.append(rank)
    fills = [jnp.int32(0)] * (bins - 1)
    spots = [jnp.int32(0)] * count
    for k in range(count):
        size = jnp.int32(0)
        for i in range(count):
            size = size + jnp.where(ranks[i] == k, sizes[i], 0)
        if k == 0:
            spot = jnp.int32((bins - 1) * CAP)
        else:
            free = jnp.int32(1)
            spot = jnp.int32(0)
            for b in range(bins - 1):
                fits = jnp.where(fills[b] + size <= CAP, free, 0) if b < bins - 2 else free
                spot = spot + fits * (b * CAP + fills[b])
                fills[b] = fills[b] + fits * size
                free = free - fits
        for i in range(count):
            spots[i] = spots[i] + jnp.where(ranks[i] == k, spot, 0)
    return starts, sizes, spots


def packed_source(place, first, shape, axis):
    spot = lax.broadcasted_iota(jnp.int32, shape, axis) + first
    source = jnp.full(shape, -1, jnp.int32)
    segment = jnp.full(shape, -1, jnp.int32)
    for i, (start, size, at) in enumerate(zip(*place)):
        here = (spot >= at) & (spot < at + size)
        source = jnp.where(here, spot + (start - at), source)
        segment = jnp.where(here, i, segment)
    return source, segment


def low_lanes():
    return lax.broadcasted_iota(jnp.int32, (1, 128), 1) < 64


def half(tile, low):
    lanes = low_lanes()
    return jnp.where(lanes if low else jnp.logical_not(lanes), tile, jnp.zeros_like(tile))


HEADS = ((0, 2, 4, True), (0, 2, 4, False), (1, 3, 5, True))


def tile_of(ref, m, t, rows=slice(None)):
    return ref[m, rows, 128 * t : 128 * (t + 1)]


def attend_group(qkv, m, bias, o_ref, at, lse_ref=None, qb=256):
    def rows_body(i, carry):
        rows = pl.ds(pl.multiple_of(i * qb, qb), qb)
        sums = [None, None]
        for head, (tq, tk, tv, low) in enumerate(HEADS):
            q = half(qkv[m, rows, 128 * tq : 128 * (tq + 1)], low) * jnp.asarray(0.125, BF16)
            s = nt(q, tile_of(qkv, m, tk)) + bias[rows, :]
            top = jnp.max(s, axis=1, keepdims=True)
            e = jnp.exp(s - top)
            total = jnp.sum(e, axis=1, keepdims=True)
            p = (e * (1.0 / total)).astype(BF16)
            o = nn(p, half(tile_of(qkv, m, tv), low))
            j = 0 if head < 2 else 1
            sums[j] = o if sums[j] is None else sums[j] + o
            if lse_ref is not None:
                lane = lax.broadcasted_iota(jnp.int32, (1, 128), 1)
                lse_ref[rows, :] = jnp.where(lane == 3 * m + head, top + jnp.log(total), lse_ref[rows, :])
        o_ref[at, rows, 0:128] = sums[0].astype(BF16)
        o_ref[at, rows, 128:256] = sums[1].astype(BF16)
        return carry

    lax.fori_loop(0, CAP // qb, rows_body, 0)


def attend_group_back(qkv, m, bias, lse_t, do_ref, dqkv, qb=256):
    dk = [None, None]
    dv = [None, None]
    dq = [[None] * (CAP // qb), [None] * (CAP // qb)]
    for head, (tq, tk, tv, low) in enumerate(HEADS):
        j = 0 if head < 2 else 1
        k = half(tile_of(qkv, m, tk), low) * jnp.asarray(0.125, BF16)
        v = half(tile_of(qkv, m, tv), low)
        lse = lse_t[pl.ds(3 * m + head, 1), :]
        for i in range(CAP // qb):
            rows = slice(i * qb, (i + 1) * qb)
            q = tile_of(qkv, m, tq, rows)
            do = do_ref[m, rows, 128 * j : 128 * (j + 1)]
            p = jnp.exp(nt(k, q) + bias[:, rows] - lse[:, rows])
            dp = nt(v, do)
            delta = jnp.sum(p * dp, axis=0, keepdims=True)
            ds = (p * (dp - delta)).astype(BF16)
            dv_part = nn(p.astype(BF16), half(do, low))
            dk_part = nn(ds, half(q, low) * jnp.asarray(0.125, BF16))
            dq_part = tn(ds, k)
            dv[j] = dv_part if dv[j] is None else dv[j] + dv_part
            dk[j] = dk_part if dk[j] is None else dk[j] + dk_part
            dq[j][i] = dq_part if dq[j][i] is None else dq[j][i] + dq_part
    for j in range(2):
        for i in range(CAP // qb):
            dqkv[m, i * qb : (i + 1) * qb, 128 * j : 128 * (j + 1)] = dq[j][i].astype(BF16)
        dqkv[m, :, 128 * (2 + j) : 128 * (3 + j)] = dk[j].astype(BF16)
        dqkv[m, :, 128 * (4 + j) : 128 * (5 + j)] = dv[j].astype(BF16)


def out_weight_tiles(w, m):
    lanes = low_lanes()
    t1 = tile_of(w, m, 1).astype(F32)
    t3 = tile_of(w, m, 3).astype(F32)
    t5 = tile_of(w, m, 5).astype(F32)
    first = jnp.where(lanes, pltpu.roll(t1, 64, 1), t3)
    second = jnp.where(lanes, pltpu.roll(t5, 64, 1), 0.0)
    return first.astype(BF16), second.astype(BF16)


def gelu_parts(a):
    inner = GELU_COEF * (a + GELU_CUBE * a * a * a)
    t = jnp.tanh(inner)
    return t


def rms_rows(values):
    return lax.rsqrt(jnp.mean(values * values, axis=1, keepdims=True) + EPSILON)


def layer_kernel(
    len_ref, x_ref, dy_ref, w_ref, gain_ref, which_ref,
    out_ref, gt_ref, g_ref, gg_ref,
    bias, xp, dyp, n1, n1t, n2, n2t, dypt, dhbt, qkv, o_all, wo, lse, lse_t, do, dqkv, h, acc,
):
    bins = w_ref.shape[0]
    seq = x_ref.shape[0]
    place = placement(len_ref, bins)
    me = which_ref[0]
    g1 = gain_ref[0:1, :]
    g2 = gain_ref[1:2, :]

    def wo_body(m, c):
        first, second = out_weight_tiles(w_ref, m)
        wo[m, :, 0:128] = first
        wo[m, :, 128:256] = second
        return c

    lax.fori_loop(0, bins, wo_body, 0)
    lse[...] = jnp.zeros_like(lse)

    def forward(b):
        source, segment = packed_source(place, b * CAP, (CAP, 1), 0)
        _, segment_row = packed_source(place, b * CAP, (1, CAP), 1)
        bias[...] = jnp.where(segment == segment_row, 0.0, NEG)
        pick = (source == lax.broadcasted_iota(jnp.int32, (CAP, seq), 1)).astype(BF16)
        xb = nn(pick, x_ref[...])
        xp[...] = xb.astype(BF16)
        dyp[...] = nn(pick, dy_ref[...]).astype(BF16)
        n1[...] = (xb * rms_rows(xb) * g1).astype(BF16)
        h[...] = xb

        def m_body(m, c):
            qkv[m] = nn(n1[...], w_ref[m, :, 0:768]).astype(BF16)
            attend_group(qkv, m, bias, o_all, m, lse)
            h[...] += nt(o_all[m], wo[m])
            return c

        lax.fori_loop(0, bins, m_body, 0)
        hb = h[...]
        n2[...] = (hb * rms_rows(hb) * g2).astype(BF16)

    def ffn_out(b):
        acc[...] = h[...]

        def m_body(m, c):
            a = nn(n2[...], w_ref[m, :, 768:1280])
            up = nn(n2[...], w_ref[m, :, 1280:1792])
            u = (0.5 * a * (1.0 + gelu_parts(a)) * up).astype(BF16)
            acc[...] += nt(u, w_ref[m, :, 1792:2304])
            return c

        lax.fori_loop(0, bins, m_body, 0)
        source, _ = packed_source(place, b * CAP, (1, CAP), 1)
        drop = (lax.broadcasted_iota(jnp.int32, (seq, CAP), 0) == source).astype(BF16)
        out_ref[...] = (out_ref[...].astype(F32) + nn(drop, acc[...].astype(BF16))).astype(BF16)

    out_ref[...] = jnp.zeros_like(out_ref)

    def others(i, c):
        b = lax.rem(me + 1 + i, bins)
        forward(b)
        ffn_out(b)
        return c

    lax.fori_loop(0, bins, others, 0)

    n1t[...] = n1[...].T
    n2t[...] = n2[...].T
    dypt[...] = dyp[...].T
    lse_t[...] = lse[...].T
    acc[...] = jnp.zeros_like(acc)

    def ffn_back(m, c):
        a = nn(n2[...], w_ref[m, :, 768:1280])
        up = nn(n2[...], w_ref[m, :, 1280:1792])
        t = gelu_parts(a)
        gel = 0.5 * a * (1.0 + t)
        u = (gel * up).astype(BF16)
        du = nn(dyp[...], w_ref[m, :, 1792:2304])
        slope = 0.5 * (1.0 + t) + 0.5 * a * (1.0 - t * t) * (GELU_COEF * (1.0 + 3.0 * GELU_CUBE * a * a))
        da = (du * up * slope).astype(BF16)
        db = (du * gel).astype(BF16)
        g_ref[m, :, 1792:2304] = nn(dypt[...], u).astype(BF16)
        g_ref[m, :, 768:1280] = nn(n2t[...], da).astype(BF16)
        g_ref[m, :, 1280:1792] = nn(n2t[...], db).astype(BF16)
        acc[...] += nt(da, w_ref[m, :, 768:1280]) + nt(db, w_ref[m, :, 1280:1792])
        return c

    lax.fori_loop(0, bins, ffn_back, 0)
    hb = h[...]
    r2 = rms_rows(hb)
    dn2 = acc[...]
    gg_ffn = jnp.sum(dn2 * hb * r2, axis=0, keepdims=True)
    wg = dn2 * g2
    dh = dyp[...].astype(F32) + r2 * wg - hb * (r2 * r2 * r2) * jnp.mean(wg * hb, axis=1, keepdims=True)
    h[...] = dh
    dhb = dh.astype(BF16)
    dhbt[...] = dhb.T
    n2[...] = dhb
    acc[...] = jnp.zeros_like(acc)

    def attn_back(m, c):
        do[m] = nn(n2[...], wo[m]).astype(BF16)
        attend_group_back(qkv, m, bias, lse_t, do, dqkv)
        acc[...] += nt(dqkv[m], w_ref[m, :, 0:768])
        grad = nn(n1t[...], dqkv[m])
        go = nn(dhbt[...], o_all[m])
        lanes = low_lanes()
        for t in range(6):
            g = grad[:, 128 * t : 128 * (t + 1)]
            if t == 1:
                g = jnp.where(lanes, g, pltpu.roll(go[:, 0:128], 64, 1))
            elif t == 3:
                g = jnp.where(lanes, g, go[:, 0:128])
            elif t == 5:
                g = jnp.where(lanes, g, pltpu.roll(go[:, 128:256], 64, 1))
            g_ref[m, :, 128 * t : 128 * (t + 1)] = g.astype(BF16)
        return c

    lax.fori_loop(0, bins, attn_back, 0)
    xb = xp[...].astype(F32)
    r1 = rms_rows(xb)
    dn1 = acc[...]
    gg_attn = jnp.sum(dn1 * xb * r1, axis=0, keepdims=True)
    wa = dn1 * g1
    gt = h[...] + r1 * wa - xb * (r1 * r1 * r1) * jnp.mean(wa * xb, axis=1, keepdims=True)
    gt_ref[...] = gt.astype(BF16)
    gg_ref[0:1, :] = gg_attn
    gg_ref[1:2, :] = gg_ffn


def unpack_kernel(len_ref, gt_ref, out_ref):
    bins = gt_ref.shape[0]
    seq = out_ref.shape[0]
    place = placement(len_ref, bins)
    total = jnp.zeros(out_ref.shape, F32)
    for b in range(bins):
        source, _ = packed_source(place, b * CAP, (1, CAP), 1)
        drop = (lax.broadcasted_iota(jnp.int32, (seq, CAP), 0) == source).astype(BF16)
        total = total + nn(drop, gt_ref[b])
    out_ref[...] = total


def per_device(
    tokens, lengths, query_weight, key_weight, value_weight, out_weight, attn_gain, gate_weight, up_weight, down_weight,
    ffn_gain, cotangent,
):
    rows, seq, width = tokens.shape
    bins = lax.axis_size("mp")
    q, k, v, o = (w.astype(BF16) for w in (query_weight, key_weight, value_weight, out_weight.T))
    package = jnp.concatenate(
        [q, o[:, 0:64], k, o[:, 64:128], v, o[:, 128:192], gate_weight.astype(BF16), up_weight.astype(BF16),
         down_weight.T.astype(BF16)], axis=1)
    w = lax.all_gather(lax.all_gather(package, "dp", axis=0, tiled=True), "mp", axis=0)
    gains = jnp.stack([attn_gain, ffn_gain]).astype(BF16)
    gains = lax.all_gather(gains, "dp", axis=1, tiled=True).astype(F32)
    gains = jnp.concatenate([gains, jnp.zeros((6, width), F32)], axis=0)
    which = lax.axis_index("mp").astype(jnp.int32).reshape(1)
    vmem = pl.BlockSpec(memory_space=pltpu.VMEM)
    smem = pl.BlockSpec(memory_space=pltpu.SMEM)
    group = w.shape[2]
    x = tokens.reshape(seq, width)
    dy = cotangent.reshape(seq, width)
    out, gt, g, gg = pl.pallas_call(
        layer_kernel,
        out_shape=(
            jax.ShapeDtypeStruct((seq, width), BF16),
            jax.ShapeDtypeStruct((CAP, width), BF16),
            jax.ShapeDtypeStruct((bins, width, group), BF16),
            jax.ShapeDtypeStruct((8, width), F32),
        ),
        in_specs=[smem, vmem, vmem, vmem, vmem, smem],
        out_specs=[vmem] * 4,
        scratch_shapes=[
            pltpu.VMEM((CAP, CAP), F32),
            pltpu.VMEM((CAP, width), BF16),
            pltpu.VMEM((CAP, width), BF16),
            pltpu.VMEM((CAP, width), BF16),
            pltpu.VMEM((width, CAP), BF16),
            pltpu.VMEM((CAP, width), BF16),
            pltpu.VMEM((width, CAP), BF16),
            pltpu.VMEM((width, CAP), BF16),
            pltpu.VMEM((width, CAP), BF16),
            pltpu.VMEM((bins, CAP, width), BF16),
            pltpu.VMEM((bins, CAP, 256), BF16),
            pltpu.VMEM((bins, width, 256), BF16),
            pltpu.VMEM((CAP, 128), F32),
            pltpu.VMEM((128, CAP), F32),
            pltpu.VMEM((bins, CAP, 256), BF16),
            pltpu.VMEM((bins, CAP, width), BF16),
            pltpu.VMEM((CAP, width), F32),
            pltpu.VMEM((CAP, width), F32),
        ],
        compiler_params=pltpu.CompilerParams(vmem_limit_bytes=63 * 2**20+900000),
        name="layer",
    )(lengths, x, dy, w, gains, which)
    gt_all = lax.all_gather(gt, "mp", axis=0)
    grad_tokens = pl.pallas_call(
        unpack_kernel,
        out_shape=jax.ShapeDtypeStruct((seq, width), F32),
        in_specs=[smem, vmem],
        out_specs=vmem,
        compiler_params=pltpu.CompilerParams(vmem_limit_bytes=60 * 2**20),
        name="unpack",
    )(lengths, gt_all)
    g = lax.psum_scatter(g, "mp", scatter_dimension=0, tiled=False)
    g = lax.psum_scatter(g, "dp", scatter_dimension=0, tiled=True).astype(F32)
    gg = lax.psum_scatter(lax.psum(gg[0:2], "mp"), "dp", scatter_dimension=1, tiled=True)
    go = jnp.concatenate([g[:, 192:256], g[:, 448:512], g[:, 704:768]], axis=1).T
    return (
        out.reshape(rows, seq, width),
        grad_tokens.reshape(rows, seq, width),
        g[:, 0:192],
        g[:, 256:448],
        g[:, 512:704],
        go,
        gg[0],
        g[:, 768:1280],
        g[:, 1280:1792],
        g[:, 1792:2304].T,
        gg[1],
    )


def solution(mesh):
    return jax.shard_map(
        per_device,
        mesh=mesh,
        in_specs=(
            P("dp", None, None), P("dp", None), P("dp", "mp"), P("dp", "mp"), P("dp", "mp"), P("mp", "dp"), P("dp"),
            P("dp", "mp"), P("dp", "mp"), P("mp", "dp"), P("dp"), P("dp", None, None),
        ),
        out_specs=(
            P("dp", None, None), P("dp", None, None), P("dp", "mp"), P("dp", "mp"), P("dp", "mp"), P("mp", "dp"),
            P("dp"), P("dp", "mp"), P("dp", "mp"), P("mp", "dp"), P("dp"),
        ),
        check_vma=False,
    )
```

time: 1130 us -> 852 us (0.75)
  Pallas kernels: 0 us -> 161 us
  matrix products: 123 us -> 0 us
  waiting for transfers between devices: 759 us -> 637 us
  blocking collectives: 99.9 us -> 20.4 us
  other arithmetic: 82.6 us -> 7.32 us
  local copies, waits for them, and re-layouts: 38.1 us -> 10.7 us
    psum x4 -> x0, waiting for transfers between devices: 541 us -> none  [the longest x1 166 us: per_device(): ffn_input = lax.psum(ffn_input_part, 'mp')]
    all_gather x0 -> x3, waiting for transfers between devices: none -> 325 us  [the longest x1 236 us: per_device(): lax.all_gather(lax.all_gather(package, 'dp', axis=0, tiled=True), 'mp', a...]
    pallas_call x0 -> x2, Pallas kernels: none -> 161 us  [the longest x1 152 us: per_device(): pl.pallas_call(layer_kernel, out_shape=(jax.ShapeDtypeStruct((seq, width)...]
    dot_general x41 -> x0, matrix products: 121 us -> none  [the longest x6 19.9 us: matmul_left_t(): lax.dot_general(left, right, (((0,), (0,)), ((), ())), preferred_element_...]
    all_gather x7 -> x1, blocking collectives: 70.3 us -> 8.7 us  [per_device(): gains = lax.all_gather(gains, 'dp', axis=1, tiled=True).astype(F32)]
    reduce_scatter x6 -> x2, waiting for transfers between devices: 217 us -> 274 us  [the longest x1 233 us: per_device(): g = lax.psum_scatter(g, 'mp', scatter_dimension=0, tiled=False)]
    unnamed x12 -> x7, waiting for transfers between devices: 0.2 us -> 38.4 us
    convert_element_type x16 -> x7, other arithmetic: 36.5 us -> 6.6 us  [the longest x3 2.7 us: per_device(): w.astype(BF16)]
  transfers between devices with their start and end apart: 11 -> 6, of which waited for: 10 -> 6; matrix products, arithmetic and copies ran while one was open for 13% -> 0% of each run, Pallas kernels for 0% -> 1%
where the time goes in v1:
time: 852 us; the launch traced here: 851 us
  waiting for transfers between devices  637 us (75%)
  Pallas kernels  161 us (19%)
  blocking collectives  20.4 us (2%)
  between operations  14.2 us (2%)
  local copies, waits for them, and re-layouts  10.7 us (1%)
    all_gather x1, waiting for transfers between devices, per_device(): lax.all_gather(lax.all_gather(package, 'dp', axis=0, tiled=True), 'mp', a...  236 us
    reduce_scatter x1, waiting for transfers between devices, per_device(): g = lax.psum_scatter(g, 'mp', scatter_dimension=0, tiled=False)  233 us
    pallas_call x1, Pallas kernels, per_device(): pl.pallas_call(layer_kernel, out_shape=(jax.ShapeDtypeStruct((seq, width)...  152 us
    all_gather x1, waiting for transfers between devices, per_device(): gt_all = lax.all_gather(gt, 'mp', axis=0)  52.5 us
    reduce_scatter x1, waiting for transfers between devices, per_device(): g = lax.psum_scatter(g, 'dp', scatter_dimension=0, tiled=True).astype(F32)  40.6 us
    unnamed x7, waiting for transfers between devices  38.4 us
    all_gather x1, waiting for transfers between devices, per_device(): lax.all_gather(package, 'dp', axis=0, tiled=True)  36.8 us
  transfers between devices with their start and end apart: 6, of which 6 were waited for; matrix products, arithmetic and copies ran while one was open for 0% of the time, Pallas kernels for 1%

profile of v1, /device:TPU:0, one launch (start us, length us, event | category | flops | bytes accessed | tf_op | source)
XLA Modules:
  0.0 851.5 jit_solution(10152375401715214653)
XLA Ops:
  7.2 0.0 copy-start
  7.2 0.0 copy-start.1
  7.2 0.0 all-gather.7.cloned.1.call-start
  7.2 0.9 convert_element_type.32
  8.1 0.9 convert_element_type.35
  9.0 0.9 convert_element_type.36
  9.9 1.0 copy.26
  10.9 0.1 fusion.3
  11.0 0.9 convert_element_type.37
  12.0 0.9 convert_element_type.38
  12.9 0.9 convert_bitcast_fusion
  13.8 0.9 concatenate.11
  14.7 0.0 all-gather.7.cloned.1.call-update
  14.8 0.0 all-gather.9.cloned.1.call-start
  14.8 36.8 %all-gather.7.cloned.1.call-done = bf16[768,2304]{1,0:T(8,128)(2,1)} async-done(((bf16[96,2304]{1,0:T(8,128)(2,1)}), bf16[768,2304]{1,0:T(8,128)(2,1)}) %all-gather.7.cloned.1.call-update) | async-done | bytes 3538960 | tf_op jit(solution)/shard_map/all_gather | solution.py:321
  51.6 0.0 all-gather.9.cloned.1.call-update
  51.6 0.0 reduce-scatter.6.cloned.1.call-start
  51.6 0.0 copy-done
  51.7 0.0 copy-done.1
  51.7 8.7 %all-gather.2 = bf16[8,96,2]{1,2,0:T(2,128)(2,1)S(1)} all-gather(bf16[1,96,2]{1,2,0:T(2,128)(2,1)S(1)} %maximum_bitcast_fusion.1), channel_id=1, replica_groups=mesh['dp'=8,'mp'=4] {'dp'}, dimensions={0}, use_global_device_ids=true | all-gather | bytes 3456 | tf_op jit(solution)/shard_map/all_gather | solution.py:323
  60.4 0.1 reshape.45
  60.5 0.6 pad_convert_fusion.gain_ref
  61.1 236.0 %all-gather.9.cloned.1.call-done = bf16[3072,2304]{1,0:T(8,128)(2,1)} async-done(((bf16[768,2304]{1,0:T(8,128)(2,1)}), bf16[3072,2304]{1,0:T(8,128)(2,1)}) %all-gather.9.cloned.1.call-update) | async-done | bytes 14155792 | tf_op jit(solution)/shard_map/all_gather | solution.py:321
  297.1 151.8 %layer.1 = (bf16[1536,768]{1,0:T(8,128)(2,1)}, bf16[512,768]{1,0:T(8,128)(2,1)}, bf16[4,768,2304]{2,1,0:T(8,128)(2,1)}, f32[8,768]{1,0:T(8,128)}) custom-call(s32[1,8]{1,0:T(1,128)} %len_ref.3, bf16[1536,768]{1,0:T(8,128)(2,1)} %bitcast.38, bf16[1536,768]{1,0:T(8,128)(2,1)} %bitcast.39, bf16[4,768,2304]{2,1,0:T(8,128)(2,1)} %bitcast.34, ...), custom_call_target="tpu_custom_call" | custom-call | tf_op jit(solution)/shard_map/layer/pallas_call | solution.py:331
  448.9 0.0 reduce-scatter.6.cloned.1.call-update
  448.9 0.0 reduce-scatter.10.cloned.1.call-start
  448.9 0.7 slice.54
  449.7 0.9 copy.29
  450.6 0.0 reduce-scatter.10.cloned.1.call-update
  450.6 0.0 all-gather.11.cloned.1.call-start
  450.7 0.5 all-gather.11.cloned.1.call-update
  451.2 0.0 reduce-scatter.8.cloned.1.call-start
  451.3 233.2 %reduce-scatter.6.cloned.1.call-done = bf16[1,768,2304]{2,1,0:T(8,128)(2,1)} async-done(((bf16[4,768,2304]{2,1,0:T(8,128)(2,1)}), bf16[1,768,2304]{2,1,0:T(8,128)(2,1)}) %reduce-scatter.6.cloned.1.call-update) | async-done | bytes 3538960 | tf_op jit(solution)/shard_map/reduce_scatter | solution.py:373
  684.5 0.0 reduce-scatter.8.cloned.1.call-update
  684.5 37.8 %reduce-scatter.10.cloned.1.call-done = f32[96,2]{1,0:T(8,128)} async-done(((f32[768,2]{1,0:T(8,128)}), f32[96,2]{1,0:T(8,128)}) %reduce-scatter.10.cloned.1.call-update) | async-done | bytes 784
  722.3 0.9 copy.30
  723.1 11.7 %psum.8 = f32[2,96]{1,0:T(2,128)S(1)} all-reduce(f32[2,96]{1,0:T(2,128)S(1)} %copy.30), channel_id=1, replica_groups=mesh['dp'=8,'mp'=4] {'mp'}, use_global_device_ids=true, to_apply=%region_2.0 | all-reduce | flops 192 | bytes 1536 | tf_op jit(solution)/shard_map/psum | solution.py:375
  734.8 0.5 slice_bitcast_fusion.1
  735.3 52.5 %all-gather.11.cloned.1.call-done = bf16[2048,768]{1,0:T(8,128)(2,1)} async-done(((bf16[512,768]{1,0:T(8,128)(2,1)}), bf16[2048,768]{1,0:T(8,128)(2,1)}) %all-gather.11.cloned.1.call-update) | async-done | bytes 3145744 | tf_op jit(solution)/shard_map/all_gather | solution.py:364
  787.8 9.5 %unpack.1 = f32[1536,768]{1,0:T(8,128)} custom-call(s32[1,8]{1,0:T(1,128)} %len_ref.3, bf16[4,512,768]{2,1,0:T(8,128)(2,1)} %bitcast.37), custom_call_target="tpu_custom_call" | custom-call | tf_op jit(solution)/shard_map/unpack/pallas_call | solution.py:365
  797.3 40.6 %reduce-scatter.8.cloned.1.call-done = bf16[96,2304]{1,0:T(8,128)(2,1)} async-done(((bf16[768,2304]{1,0:T(8,128)(2,1)}), bf16[96,2304]{1,0:T(8,128)(2,1)}) %reduce-scatter.8.cloned.1.call-update) | async-done | bytes 442384 | tf_op jit(solution)/shard_map/reduce_scatter | solution.py:374
  837.9 0.9 fusion.1
  838.8 0.1 maximum_bitcast_fusion
  838.9 0.7 copy.28
  839.6 1.1 convert_element_type.41
  840.7 0.7 slice_bitcast_fusion
  841.4 1.6 fusion.2
  842.9 1.7 fusion
  (3 shorter events, 0.0 us)
Async XLA Ops:
  7.2 44.5 %copy-start = (f32[96]{0:T(128)S(1)}, f32[96]{0:T(128)}, u32[]{:S(2)}) copy-start(f32[96]{0:T(128)} %param.22) | copy-start | bytes 1156
  7.2 44.5 %copy-start.1 = (f32[96]{0:T(128)S(1)}, f32[96]{0:T(128)}, u32[]{:S(2)}) copy-start(f32[96]{0:T(128)} %param.18) | copy-start | bytes 1156
  7.2 44.4 %all-gather.7.cloned.1.call-start = ((), (), s32[]{:S(2)}) async-start(), calls=%async_computation.3 | async-start | bytes 3981312 | tf_op jit(solution)/shard_map/all_gather | solution.py:321
  14.8 282.3 %all-gather.9.cloned.1.call-start = ((), (), s32[]{:S(2)}) async-start(), calls=%async_computation.6 | async-start | bytes 17694720 | tf_op jit(solution)/shard_map/all_gather | solution.py:321
  51.6 632.9 %reduce-scatter.6.cloned.1.call-start = ((), (), s32[]{:S(2)}) async-start(), calls=%async_computation.4 | async-start | bytes 17694720 | tf_op jit(solution)/shard_map/reduce_scatter | solution.py:373
  448.9 273.4 %reduce-scatter.10.cloned.1.call-start = ((), (), s32[]{:S(2)}) async-start(), calls=%async_computation.8 | async-start | bytes 442368
  450.6 337.1 %all-gather.11.cloned.1.call-start = ((), (), s32[]{:S(2)}) async-start(), calls=%async_computation.7 | async-start | bytes 3932160 | tf_op jit(solution)/shard_map/all_gather | solution.py:364
  451.2 386.7 %reduce-scatter.8.cloned.1.call-start = ((), (), s32[]{:S(2)}) async-start(), calls=%async_computation.5 | async-start | bytes 3981312 | tf_op jit(solution)/shard_map/reduce_scatter | solution.py:374
Sparse Core Ops, SparseCore 0:
  14.9 36.6 all-gather.6
  53.1 243.9 all-gather.8
  449.0 235.4 reduce-scatter.5
  687.4 34.8 reduce-scatter.9
  724.3 63.4 all-gather.10
  791.1 46.7 reduce-scatter.7

commit v2 on v1

--- a/solution.py
+++ b/solution.py
@@ -114,7 +114,7 @@
     lax.fori_loop(0, CAP // qb, rows_body, 0)
 
 
-def attend_group_back(qkv, m, bias, lse_t, do_ref, dqkv, qb=256):
+def attend_group_back(qkv, m, bias, lse_t, do_ref, at, dqkv, qb=256):
     dk = [None, None]
     dv = [None, None]
     dq = [[None] * (CAP // qb), [None] * (CAP // qb)]
@@ -126,7 +126,7 @@
         for i in range(CAP // qb):
             rows = slice(i * qb, (i + 1) * qb)
             q = tile_of(qkv, m, tq, rows)
-            do = do_ref[m, rows, 128 * j : 128 * (j + 1)]
+            do = do_ref[at, rows, 128 * j : 128 * (j + 1)]
             p = jnp.exp(nt(k, q) + bias[:, rows] - lse[:, rows])
             dp = nt(v, do)
             delta = jnp.sum(p * dp, axis=0, keepdims=True)
@@ -268,7 +268,7 @@
 
     def attn_back(m, c):
         do[m] = nn(n2[...], wo[m]).astype(BF16)
-        attend_group_back(qkv, m, bias, lse_t, do, dqkv)
+        attend_group_back(qkv, m, bias, lse_t, do, m, dqkv)
         acc[...] += nt(dqkv[m], w_ref[m, :, 0:768])
         grad = nn(n1t[...], dqkv[m])
         go = nn(dhbt[...], o_all[m])
@@ -389,9 +389,473 @@
     )
 
 
+MESH = pl.DeviceIdType.MESH
+PARTS = ((0, 768), (768, 2304))
+
+
+class Net:
+    def __init__(self):
+        self.dp = lax.axis_index("dp")
+        self.z = lax.axis_index("mp")
+        self.core = lax.rem(self.dp, 2)
+        self.chip = lax.div(self.dp, 2)
+        self.chip_x = self.chip + 1 - 2 * lax.rem(self.chip, 2)
+        self.chip_y = lax.rem(self.chip + 2, 4)
+        self.chip_d = 3 - self.chip
+        self.sibling = (2 * self.chip + 1 - self.core, self.z)
+        self.x = (2 * self.chip_x + self.core, self.z)
+        self.y = (2 * self.chip_y + self.core, self.z)
+
+    def up(self, k):
+        return (self.dp, lax.rem(self.z + k, 4))
+
+    def group(self, i):
+        z = self.z
+        one = jnp.where(z == 0, 1, jnp.where(z == 1, 0, jnp.where(z == 2, 3, 2)))
+        two = jnp.where(z < 2, 2, 1)
+        return jnp.where(i == 0, z, jnp.where(i == 1, one, jnp.where(i == 2, two, 6 - z - one - two)))
+
+
+class Gather:
+    def __init__(self, net, w, send, send_z, recv):
+        self.net, self.w, self.send, self.send_z, self.recv = net, w, send, send_z, recv
+
+    def unit(self, part, m, chip, core):
+        lo, hi = PARTS[part]
+        return self.w.at[m, chip, core, :, lo:hi]
+
+    def copy(self, part, m, chip, core, sem, to):
+        ref = self.unit(part, m, chip, core)
+        return pltpu.make_async_remote_copy(
+            src_ref=ref, dst_ref=ref, send_sem=sem, recv_sem=self.recv.at[part, m, chip, core],
+            device_id=to, device_id_type=MESH)
+
+    def wait(self, part, m, chip, core):
+        self.copy(part, m, chip, core, self.send.at[part, m, chip, 0], self.net.sibling).wait_recv()
+
+    def along_z(self, part):
+        net = self.net
+        for k in range(1, 4):
+            self.copy(part, net.z, net.chip, net.core, self.send_z.at[part, k - 1], net.up(k)).start()
+
+    def spread(self, part, i):
+        net = self.net
+        m = net.group(i)
+        if isinstance(i, int):
+            if i > 0:
+                self.wait(part, m, net.chip, net.core)
+        else:
+            @pl.when(i > 0)
+            def _():
+                self.wait(part, m, net.chip, net.core)
+        for k, to in enumerate((net.x, net.y, net.sibling)):
+            self.copy(part, m, net.chip, net.core, self.send.at[part, m, net.chip, k], to).start()
+
+    def relay(self, part, i):
+        net = self.net
+        m = net.group(i)
+        first = m < 2
+        self.wait(part, m, net.chip_x, net.core)
+        self.copy(part, m, net.chip_x, net.core, self.send.at[part, m, net.chip_x, 2], net.sibling).start()
+        self.wait(part, m, net.chip_y, net.core)
+        source = jnp.where(first, net.chip_x, net.chip_y)
+        target = jnp.where(first, net.chip_y, net.chip_x)
+        self.copy(part, m, source, net.core, self.send.at[part, m, source, 0], (2 * target + net.core, net.z)).start()
+        self.copy(part, m, net.chip_y, net.core, self.send.at[part, m, net.chip_y, 2], net.sibling).start()
+
+    def across(self, part, i):
+        net = self.net
+        m = net.group(i)
+        self.wait(part, m, net.chip_d, net.core)
+        self.copy(part, m, net.chip_d, net.core, self.send.at[part, m, net.chip_d, 2], net.sibling).start()
+
+    def complete(self, part, i):
+        net = self.net
+        m = net.group(i)
+        for chip in range(4):
+            self.wait(part, m, chip, 1 - net.core)
+
+    def drain(self):
+        net = self.net
+
+        def sent(part, m, chip, sem):
+            self.copy(part, m, chip, net.core, sem, net.sibling).wait_send()
+
+        for part in range(2):
+            for k in range(3):
+                sent(part, net.z, net.chip, self.send_z.at[part, k])
+
+            def body(m, c, part=part):
+                for k in range(3):
+                    sent(part, m, net.chip, self.send.at[part, m, net.chip, k])
+                for chip in (net.chip_x, net.chip_y, net.chip_d):
+                    sent(part, m, chip, self.send.at[part, m, chip, 2])
+                source = jnp.where(m < 2, net.chip_x, net.chip_y)
+                sent(part, m, source, self.send.at[part, m, source, 0])
+                return c
+
+            lax.fori_loop(0, 4, body, 0)
+
+
+def greet(net):
+    barrier = pltpu.get_barrier_semaphore()
+    for other in range(1, 8):
+        pl.semaphore_signal(barrier, inc=1, device_id=(lax.rem(net.dp + other, 8), net.z), device_id_type=MESH)
+    for k in range(1, 4):
+        pl.semaphore_signal(barrier, inc=1, device_id=net.up(k), device_id_type=MESH)
+    pl.semaphore_wait(barrier, 10)
+
+
+def share_gains(net, parts, send, recv):
+    copies = []
+    for k in range(1, 8):
+        copies.append(pltpu.make_async_remote_copy(
+            src_ref=parts.at[net.dp], dst_ref=parts.at[net.dp], send_sem=send.at[k - 1], recv_sem=recv.at[net.dp],
+            device_id=(lax.rem(net.dp + k, 8), net.z), device_id_type=MESH))
+        copies[-1].start()
+    return copies
+
+
+def join_gains(net, parts, send, recv, gain):
+    for k in range(1, 8):
+        other = lax.rem(net.dp + k, 8)
+        pltpu.make_async_remote_copy(
+            src_ref=parts.at[other], dst_ref=parts.at[other], send_sem=send.at[k - 1], recv_sem=recv.at[other],
+            device_id=net.sibling, device_id_type=MESH).wait_recv()
+    total = jnp.zeros(gain.shape, F32)
+    for d in range(8):
+        piece = jnp.concatenate([parts[d], jnp.zeros((8, gain.shape[1] - 128), F32)], axis=1)
+        total = total + pltpu.roll(piece, 96 * d, 1)
+    gain[...] = total
+
+
+def build_package(w, net, q_ref, k_ref, v_ref, o_ref, g_ref, u_ref, d_ref):
+    lanes = low_lanes()
+    ot = o_ref[...].T
+    pad = jnp.zeros((96, 64), F32)
+    at = (net.z, net.chip, net.core)
+
+    def put(tile, value):
+        w[at[0], at[1], at[2], :, 128 * tile : 128 * (tile + 1)] = value.astype(BF16)
+
+    for j, ref in enumerate((q_ref, k_ref, v_ref)):
+        put(2 * j, ref[:, 0:128])
+        last = jnp.concatenate([ref[:, 128:192], pad], axis=1)
+        extra = jnp.concatenate([ot[:, 64 * j : 64 * (j + 1)], pad], axis=1)
+        put(2 * j + 1, jnp.where(lanes, last, pltpu.roll(extra, 64, 1)))
+    w[at[0], at[1], at[2], :, 768:1280] = g_ref[...].astype(BF16)
+    w[at[0], at[1], at[2], :, 1280:1792] = u_ref[...].astype(BF16)
+    w[at[0], at[1], at[2], :, 1792:2304] = d_ref[...].T.astype(BF16)
+
+
+def rows768(ref, m, lo, hi):
+    return ref[m, :, :, :, lo:hi].reshape(768, hi - lo)
+
+
+def put768(ref, m, lo, hi, value):
+    ref[m, :, :, :, lo:hi] = value.reshape(4, 2, 96, hi - lo)
+
+
+def mega_kernel(
+    len_ref, x_ref, dy_ref, q_ref, k_ref, v_ref, o_ref, gate_ref, up_ref, down_ref, ga_ref, gf_ref,
+    out_ref, gt_ref, g_ref, gg_ref,
+    w, gain, gain_parts, bias, xp, dyp, n1, n1t, n2, n2t, dypt, dhbt, qkv, qkv_b, o_own, o_b, do, wo, lse, lse_t, h, acc, res,
+    ag_send, ag_send_z, ag_recv, gn_send, gn_recv, in_sem,
+):
+    net = Net()
+    bins = 4
+    halves = [pltpu.make_async_copy(dy_ref.at[j], g_ref.at[0, :, :, :, 768 * j : 768 * (j + 1)], in_sem.at[j]) for j in (0, 1)]
+    for copy in halves:
+        copy.start()
+    seq = x_ref.shape[0]
+    me = net.z
+    ag = Gather(net, w, ag_send, ag_send_z, ag_recv)
+    build_package(w, net, q_ref, k_ref, v_ref, o_ref, gate_ref, up_ref, down_ref)
+    pad = jnp.zeros((1, 32), F32)
+    mine = jnp.concatenate([
+        jnp.concatenate([ga_ref[...], pad], axis=1), jnp.concatenate([gf_ref[...], pad], axis=1),
+        jnp.zeros((6, 128), F32)], axis=0)
+    gain_parts[net.dp] = mine.astype(BF16).astype(F32)
+    greet(net)
+    gain_copies = share_gains(net, gain_parts, gn_send, gn_recv)
+    ag.along_z(0)
+    ag.spread(0, 0)
+
+    place = placement(len_ref, bins)
+    lse[...] = jnp.zeros_like(lse)
+
+    def pack(b):
+        source, segment = packed_source(place, b * CAP, (CAP, 1), 0)
+        _, segment_row = packed_source(place, b * CAP, (1, CAP), 1)
+        bias[...] = jnp.where(segment == segment_row, 0.0, NEG)
+        return (source == lax.broadcasted_iota(jnp.int32, (CAP, seq), 1)).astype(BF16)
+
+    def unpack(b, value):
+        source, _ = packed_source(place, b * CAP, (1, CAP), 1)
+        drop = (lax.broadcasted_iota(jnp.int32, (seq, CAP), 0) == source).astype(BF16)
+        out_ref[...] = (out_ref[...].astype(F32) + nn(drop, value)).astype(BF16)
+
+    pick = pack(me)
+    xb = nn(pick, x_ref[...])
+    xp[...] = xb.astype(BF16)
+    for copy in halves:
+        copy.wait()
+    dyp[...] = (nn(pick[:, 0:768], rows768(g_ref, 0, 0, 768)) + nn(pick[:, 768:1536], rows768(g_ref, 0, 768, 1536))).astype(BF16)
+    h[...] = xb
+    dypt[...] = dyp[...].T
+    ag.spread(0, 1)
+    ag.relay(0, 0)
+    join_gains(net, gain_parts, gn_send, gn_recv, gain)
+    g1 = gain[0:1, :]
+    g2 = gain[1:2, :]
+    n1[...] = (xb * rms_rows(xb) * g1).astype(BF16)
+    n1t[...] = n1[...].T
+    ag.spread(0, 2)
+    ag.across(0, 0)
+    ag.relay(0, 1)
+    ag.spread(0, 3)
+
+    def own_forward(i, c):
+        m = net.group(i)
+
+        @pl.when(i == 0)
+        def _():
+            ag.across(0, 1)
+            ag.relay(0, 2)
+
+        @pl.when(i == 1)
+        def _():
+            ag.across(0, 2)
+            ag.relay(0, 3)
+            ag.along_z(1)
+            ag.spread(1, 0)
+
+        @pl.when(i == 2)
+        def _():
+            ag.across(0, 3)
+            ag.spread(1, 1)
+
+        @pl.when(i == 3)
+        def _():
+            ag.relay(1, 0)
+
+        ag.complete(0, i)
+        first, second = out_weight_tiles_at(w, m)
+        wo[m, :, 0:128] = first
+        wo[m, :, 128:256] = second
+        qkv[m] = nn(n1[...], rows768(w, m, 0, 768)).astype(BF16)
+        attend_group(qkv, m, bias, o_own, m, lse)
+        h[...] += nt(o_own[m], wo[m])
+        return c
+
+    lax.fori_loop(0, 4, own_forward, 0)
+    hb = h[...]
+    n2[...] = (hb * rms_rows(hb) * g2).astype(BF16)
+    n2t[...] = n2[...].T
+    lse_t[...] = lse[...].T
+    acc[...] = jnp.zeros_like(acc)
+    res[...] = hb
+
+    def ffn_back(i, c):
+        m = net.group(i)
+        ag.across(1, i)
+
+        @pl.when(i < 3)
+        def _():
+            ag.relay(1, i + 1)
+
+        @pl.when(i < 2)
+        def _():
+            ag.spread(1, i + 2)
+
+        ag.complete(1, i)
+        for lo in (0, 256):
+            w_gate = rows768(w, m, 768 + lo, 1024 + lo)
+            w_up = rows768(w, m, 1280 + lo, 1536 + lo)
+            w_down = rows768(w, m, 1792 + lo, 2048 + lo)
+            a = nn(n2[...], w_gate)
+            up = nn(n2[...], w_up)
+            t = gelu_parts(a)
+            gel = 0.5 * a * (1.0 + t)
+            u = (gel * up).astype(BF16)
+            res[...] += nt(u, w_down)
+            put768(g_ref, m, 1792 + lo, 2048 + lo, nn(dypt[...], u).astype(BF16))
+            du = nn(dyp[...], w_down)
+            slope = 0.5 * (1.0 + t) + 0.5 * a * (1.0 - t * t) * (GELU_COEF * (1.0 + 3.0 * GELU_CUBE * a * a))
+            da = (du * up * slope).astype(BF16)
+            db = (du * gel).astype(BF16)
+            put768(g_ref, m, 768 + lo, 1024 + lo, nn(n2t[...], da).astype(BF16))
+            put768(g_ref, m, 1280 + lo, 1536 + lo, nn(n2t[...], db).astype(BF16))
+            acc[...] += nt(da, w_gate) + nt(db, w_up)
+        return c
+
+    lax.fori_loop(0, 4, ffn_back, 0)
+    out_ref[...] = jnp.zeros_like(out_ref)
+    unpack(me, res[...].astype(BF16))
+    hb = h[...]
+    r2 = rms_rows(hb)
+    dn2 = acc[...]
+    gg_ffn = jnp.sum(dn2 * hb * r2, axis=0, keepdims=True)
+    wg = dn2 * g2
+    dh = dyp[...].astype(F32) + r2 * wg - hb * (r2 * r2 * r2) * jnp.mean(wg * hb, axis=1, keepdims=True)
+    h[...] = dh
+    dhb = dh.astype(BF16)
+    dhbt[...] = dhb.T
+    n2[...] = dhb
+    acc[...] = jnp.zeros_like(acc)
+
+    def attn_back(m, c):
+        do[0] = nn(n2[...], wo[m]).astype(BF16)
+        attend_group_back(qkv, m, bias, lse_t, do, 0, qkv)
+        acc[...] += nt(qkv[m], rows768(w, m, 0, 768))
+        return c
+
+    lax.fori_loop(0, 4, attn_back, 0)
+    xb = xp[...].astype(F32)
+    r1 = rms_rows(xb)
+    dn1 = acc[...]
+    gg_attn = jnp.sum(dn1 * xb * r1, axis=0, keepdims=True)
+    wa = dn1 * g1
+    gt = h[...] + r1 * wa - xb * (r1 * r1 * r1) * jnp.mean(wa * xb, axis=1, keepdims=True)
+    gt_ref[...] = gt.astype(BF16)
+    gg_ref[0:1, :] = gg_attn
+    gg_ref[1:2, :] = gg_ffn
+
+    def attn_grads(m, c):
+        grad = nn(n1t[...], qkv[m])
+        go = nn(dhbt[...], o_own[m])
+        lanes = low_lanes()
+        for t in range(6):
+            g = grad[:, 128 * t : 128 * (t + 1)]
+            if t == 1:
+                g = jnp.where(lanes, g, pltpu.roll(go[:, 0:128], 64, 1))
+            elif t == 3:
+                g = jnp.where(lanes, g, go[:, 0:128])
+            elif t == 5:
+                g = jnp.where(lanes, g, pltpu.roll(go[:, 128:256], 64, 1))
+            put768(g_ref, m, 128 * t, 128 * (t + 1), g.astype(BF16))
+        return c
+
+    lax.fori_loop(0, 4, attn_grads, 0)
+
+    def others(k, c):
+        b = lax.rem(me + 1 + k, bins)
+        xo = nn(pack(b), x_ref[...])
+        n1[...] = (xo * rms_rows(xo) * g1).astype(BF16)
+        h[...] = xo
+
+        def attend(m, c):
+            qkv_b[0] = nn(n1[...], rows768(w, m, 0, 768)).astype(BF16)
+            attend_group(qkv_b, 0, bias, o_b, 0)
+            h[...] += nt(o_b[0], wo[m])
+            return c
+
+        lax.fori_loop(0, 4, attend, 0)
+        ho = h[...]
+        n2[...] = (ho * rms_rows(ho) * g2).astype(BF16)
+
+        def ffn(m, c):
+            a = nn(n2[...], rows768(w, m, 768, 1280))
+            up = nn(n2[...], rows768(w, m, 1280, 1792))
+            u = (0.5 * a * (1.0 + gelu_parts(a)) * up).astype(BF16)
+            h[...] += nt(u, rows768(w, m, 1792, 2304))
+            return c
+
+        lax.fori_loop(0, 4, ffn, 0)
+        unpack(b, h[...].astype(BF16))
+        return c
+
+    lax.fori_loop(0, 3, others, 0)
+    for copy in gain_copies:
+        copy.wait_send()
+    ag.drain()
+
+
+def out_weight_tiles_at(w, m):
+    lanes = low_lanes()
+    t1 = rows768(w, m, 128, 256).astype(F32)
+    t3 = rows768(w, m, 384, 512).astype(F32)
+    t5 = rows768(w, m, 640, 768).astype(F32)
+    first = jnp.where(lanes, pltpu.roll(t1, 64, 1), t3)
+    second = jnp.where(lanes, pltpu.roll(t5, 64, 1), 0.0)
+    return first.astype(BF16), second.astype(BF16)
+
+
+def on_this_slice(
+    tokens, lengths, query_weight, key_weight, value_weight, out_weight, attn_gain, gate_weight, up_weight, down_weight,
+    ffn_gain, cotangent,
+):
+    rows, seq, width = tokens.shape
+    vmem = pl.BlockSpec(memory_space=pltpu.VMEM)
+    smem = pl.BlockSpec(memory_space=pltpu.SMEM)
+    dma = pltpu.SemaphoreType.DMA
+    act = pltpu.VMEM((CAP, width), BF16)
+    act_t = pltpu.VMEM((width, CAP), BF16)
+    wide = pltpu.VMEM((CAP, width), F32)
+    out, gt, g, gg = pl.pallas_call(
+        mega_kernel,
+        out_shape=(
+            jax.ShapeDtypeStruct((seq, width), BF16),
+            jax.ShapeDtypeStruct((CAP, width), BF16),
+            jax.ShapeDtypeStruct((4, 4, 2, 96, 2304), BF16),
+            jax.ShapeDtypeStruct((8, width), F32),
+        ),
+        in_specs=[smem, vmem, pl.BlockSpec(memory_space=pl.ANY)] + [vmem] * 9,
+        out_specs=[vmem] * 4,
+        scratch_shapes=[
+            pltpu.VMEM((4, 4, 2, 96, 2304), BF16),
+            pltpu.VMEM((8, width), F32),
+            pltpu.VMEM((8, 8, 128), F32),
+            pltpu.VMEM((CAP, CAP), F32),
+            act, act, act, act_t, act, act_t, act_t, act_t,
+            pltpu.VMEM((4, CAP, width), BF16),
+            pltpu.VMEM((1, CAP, width), BF16),
+            pltpu.VMEM((4, CAP, 256), BF16),
+            pltpu.VMEM((1, CAP, 256), BF16),
+            pltpu.VMEM((1, CAP, 256), BF16),
+            pltpu.VMEM((4, width, 256), BF16),
+            pltpu.VMEM((CAP, 128), F32),
+            pltpu.VMEM((128, CAP), F32),
+            wide, wide, wide,
+            dma((2, 4, 4, 3)), dma((2, 3)), dma((2, 4, 4, 2)), dma((7,)), dma((8,)), dma((2,)),
+        ],
+        compiler_params=pltpu.CompilerParams(
+            vmem_limit_bytes=60 * 2**20, collective_id=0, has_side_effects=True),
+        name="layer",
+    )(lengths, tokens.reshape(seq, width), cotangent.reshape(2, 4, 2, 96, width), query_weight, key_weight, value_weight, out_weight,
+      gate_weight, up_weight, down_weight, attn_gain.reshape(1, 96), ffn_gain.reshape(1, 96))
+    bins = 4
+    gt_all = lax.all_gather(gt, "mp", axis=0)
+    grad_tokens = pl.pallas_call(
+        unpack_kernel,
+        out_shape=jax.ShapeDtypeStruct((seq, width), F32),
+        in_specs=[smem, vmem],
+        out_specs=vmem,
+        compiler_params=pltpu.CompilerParams(vmem_limit_bytes=60 * 2**20),
+        name="unpack",
+    )(lengths, gt_all)
+    g = g.reshape(4, width, 2304)
+    g = lax.psum_scatter(g, "mp", scatter_dimension=0, tiled=False)
+    g = lax.psum_scatter(g, "dp", scatter_dimension=0, tiled=True).astype(F32)
+    gg = lax.psum_scatter(lax.psum(gg[0:2], "mp"), "dp", scatter_dimension=1, tiled=True)
+    go = jnp.concatenate([g[:, 192:256], g[:, 448:512], g[:, 704:768]], axis=1).T
+    return (
+        out.reshape(rows, seq, width),
+        grad_tokens.reshape(rows, seq, width),
+        g[:, 0:192],
+        g[:, 256:448],
+        g[:, 512:704],
+        go,
+        gg[0],
+        g[:, 768:1280],
+        g[:, 1280:1792],
+        g[:, 1792:2304].T,
+        gg[1],
+    )
 def solution(mesh):
+    body = on_this_slice if dict(mesh.shape) == {"dp": 8, "mp": 4} else per_device
     return jax.shard_map(
-        per_device,
+        body,
         mesh=mesh,
         in_specs=(
             P("dp", None, None), P("dp", None), P("dp", "mp"), P("dp", "mp"), P("dp", "mp"), P("mp", "dp"), P("dp"),

time: 852 us -> 624 us (0.73)
  waiting for transfers between devices: 637 us -> 367 us
  Pallas kernels: 161 us -> 218 us
  blocking collectives: 20.4 us -> 11.8 us
    all_gather x3 -> x1, waiting for transfers between devices: 325 us -> 51.9 us  [on_this_slice(): gt_all = lax.all_gather(gt, 'mp', axis=0)]
    pallas_call x2, Pallas kernels: 161 us -> 218 us  [the longest x1 208 us: on_this_slice(): pl.pallas_call(mega_kernel, out_shape=(jax.ShapeDtypeStruct((seq, width),...]
    all_gather x1 -> x0, blocking collectives: 8.7 us -> none  [per_device(): gains = lax.all_gather(gains, 'dp', axis=1, tiled=True).astype(F32)]
    unnamed x7 -> x5, waiting for transfers between devices: 38.4 us -> 39.2 us
  transfers between devices with their start and end apart: 6 -> 4, of which waited for: 6 -> 4; matrix products, arithmetic and copies ran while one was open for 0% -> 0% of each run, Pallas kernels for 1% -> 2%
where the time goes in v2:
time: 624 us; the launch traced here: 623 us
  waiting for transfers between devices  367 us (59%)
  Pallas kernels  218 us (35%)
  between operations  13.8 us (2%)
  blocking collectives  11.8 us (2%)
  local copies, waits for them, and re-layouts  11.2 us (2%)
    reduce_scatter x1, waiting for transfers between devices, on_this_slice(): g = lax.psum_scatter(g, 'mp', scatter_dimension=0, tiled=False)  235 us
    pallas_call x1, Pallas kernels, on_this_slice(): pl.pallas_call(mega_kernel, out_shape=(jax.ShapeDtypeStruct((seq, width),...  208 us
    all_gather x1, waiting for transfers between devices, on_this_slice(): gt_all = lax.all_gather(gt, 'mp', axis=0)  51.9 us
    reduce_scatter x1, waiting for transfers between devices, on_this_slice(): g = lax.psum_scatter(g, 'dp', scatter_dimension=0, tiled=True).astype(F32)  40.6 us
    unnamed x5, waiting for transfers between devices  39.2 us
  transfers between devices with their start and end apart: 4, of which 4 were waited for; matrix products, arithmetic and copies ran while one was open for 0% of the time, Pallas kernels for 2%

profile of v2, /device:TPU:0, one launch (start us, length us, event | category | flops | bytes accessed | tf_op | source)
XLA Modules:
  0.0 623.0 jit_solution(3267841111078342113)
XLA Ops:
  7.2 0.0 reduce-scatter.6.cloned.1.call-start
  7.2 1.8 copy.25.down_ref
  9.0 208.2 %layer.1 = (bf16[1536,768]{1,0:T(8,128)(2,1)}, bf16[512,768]{1,0:T(8,128)(2,1)}, bf16[4,4,2,96,2304]{4,3,2,1,0:T(8,128)(2,1)}, f32[8,768]{1,0:T(8,128)}) custom-call(s32[1,8]{1,0:T(1,128)} %len_ref.3, bf16[1536,768]{1,0:T(8,128)(2,1)} %bitcast.23, bf16[2,4,2,96,768]{4,3,2,1,0:T(8,128)(2,1)} %bitcast.24, f32[96,192]{1,0:T(8,128)} %q_ref.1, f32[96,192]{1,0:T(8,128)} %k_ref.1, ...), custom_call_target="tpu_custom_call" | custom-call | tf_op jit(solution)/shard_map/layer/pallas_call | solution.py:795
  217.2 0.0 reduce-scatter.6.cloned.1.call-update
  217.2 0.0 reduce-scatter.10.cloned.1.call-start
  217.3 0.7 slice.42
  218.0 0.9 copy.27
  219.0 0.0 reduce-scatter.10.cloned.1.call-update
  219.0 0.0 all-gather.3.cloned.1.call-start
  219.0 0.7 all-gather.3.cloned.1.call-update
  219.7 0.0 reduce-scatter.8.cloned.1.call-start
  219.8 235.4 %reduce-scatter.6.cloned.1.call-done = bf16[1,768,2304]{2,1,0:T(8,128)(2,1)} async-done(((bf16[4,768,2304]{2,1,0:T(8,128)(2,1)}), bf16[1,768,2304]{2,1,0:T(8,128)(2,1)}) %reduce-scatter.6.cloned.1.call-update) | async-done | bytes 3538960 | tf_op jit(solution)/shard_map/reduce_scatter | solution.py:838
  455.2 0.0 reduce-scatter.8.cloned.1.call-update
  455.2 38.5 %reduce-scatter.10.cloned.1.call-done = f32[96,2]{1,0:T(8,128)} async-done(((f32[768,2]{1,0:T(8,128)}), f32[96,2]{1,0:T(8,128)}) %reduce-scatter.10.cloned.1.call-update) | async-done | bytes 784
  493.7 0.9 copy.28
  494.6 11.8 %psum.8 = f32[2,96]{1,0:T(2,128)S(1)} all-reduce(f32[2,96]{1,0:T(2,128)S(1)} %copy.28), channel_id=1, replica_groups=mesh['dp'=8,'mp'=4] {'mp'}, use_global_device_ids=true, to_apply=%region_2.0 | all-reduce | flops 192 | bytes 1536 | tf_op jit(solution)/shard_map/psum | solution.py:840
  506.4 0.5 slice_bitcast_fusion.1
  506.9 51.9 %all-gather.3.cloned.1.call-done = bf16[2048,768]{1,0:T(8,128)(2,1)} async-done(((bf16[512,768]{1,0:T(8,128)(2,1)}), bf16[2048,768]{1,0:T(8,128)(2,1)}) %all-gather.3.cloned.1.call-update) | async-done | bytes 3145744 | tf_op jit(solution)/shard_map/all_gather | solution.py:828
  558.8 9.5 %unpack.1 = f32[1536,768]{1,0:T(8,128)} custom-call(s32[1,8]{1,0:T(1,128)} %len_ref.3, bf16[4,512,768]{2,1,0:T(8,128)(2,1)} %bitcast.22), custom_call_target="tpu_custom_call" | custom-call | tf_op jit(solution)/shard_map/unpack/pallas_call | solution.py:829
  568.3 0.0 copy-start
  568.3 40.6 %reduce-scatter.8.cloned.1.call-done = bf16[96,2304]{1,0:T(8,128)(2,1)} async-done(((bf16[768,2304]{1,0:T(8,128)(2,1)}), bf16[96,2304]{1,0:T(8,128)(2,1)}) %reduce-scatter.8.cloned.1.call-update) | async-done | bytes 442384 | tf_op jit(solution)/shard_map/reduce_scatter | solution.py:839
  609.0 0.9 fusion.1
  609.8 0.1 maximum_bitcast_fusion
  609.9 0.7 copy.26
  610.7 1.1 convert_element_type.3
  611.7 1.6 fusion.2
  613.3 1.8 fusion
  615.1 0.0 copy-done
  615.1 1.4 copy.30
Async XLA Ops:
  7.2 448.0 %reduce-scatter.6.cloned.1.call-start = ((), (), s32[]{:S(2)}) async-start(), calls=%async_computation.3 | async-start | bytes 17694720 | tf_op jit(solution)/shard_map/reduce_scatter | solution.py:838
  217.2 276.5 %reduce-scatter.10.cloned.1.call-start = ((), (), s32[]{:S(2)}) async-start(), calls=%async_computation.6 | async-start | bytes 442368
  219.0 339.8 %all-gather.3.cloned.1.call-start = ((), (), s32[]{:S(2)}) async-start(), calls=%async_computation.5 | async-start | bytes 3932160 | tf_op jit(solution)/shard_map/all_gather | solution.py:828
  219.7 389.2 %reduce-scatter.8.cloned.1.call-start = ((), (), s32[]{:S(2)}) async-start(), calls=%async_computation.4 | async-start | bytes 3981312 | tf_op jit(solution)/shard_map/reduce_scatter | solution.py:839
  568.3 46.8 %copy-start = (bf16[1536,768]{1,0:T(8,128)(2,1)S(1)}, bf16[1536,768]{1,0:T(8,128)(2,1)}, u32[]{:S(2)}) copy-start(bf16[1536,768]{1,0:T(8,128)(2,1)} %get-tuple-element.15) | copy-start | bytes 7077892
Sparse Core Ops, SparseCore 0:
  217.4 237.7 reduce-scatter.5
  458.8 34.8 reduce-scatter.9
  495.3 63.4 all-gather.2
  562.2 46.7 reduce-scatter.7

commit v3 on v2

--- a/solution.py
+++ b/solution.py
@@ -497,6 +497,143 @@
             lax.fori_loop(0, 4, body, 0)
 
 
+class Reduce:
+    def __init__(self, net, g, slots, sems, ok):
+        self.net, self.g, self.slots, self.sems, self.ok = net, g, slots, sems, ok
+
+    def lanes(self, part):
+        return slice(*PARTS[part])
+
+    def unit(self, part, m, chip, core, rows=slice(0, 96)):
+        return self.g.at[m, chip, core, rows, self.lanes(part)]
+
+    def copy(self, kind, part, key, src, dst, to):
+        return pltpu.make_async_remote_copy(
+            src_ref=src, dst_ref=dst, send_sem=self.sems.at[0, kind, part, key], recv_sem=self.sems.at[1, kind, part, key],
+            device_id=to, device_id_type=MESH)
+
+    def core_copy(self, part, i):
+        m = self.net.group(i)
+        lo, hi = PARTS[part]
+        return self.copy(
+            0, part, m, self.g.at[m, :, 1 - self.net.core, :, lo:hi],
+            self.slots.at[lax.rem(i, 2), :, :, 0 : hi - lo], self.net.sibling)
+
+    def to_core(self, part, i, credit):
+        if credit:
+            pl.semaphore_wait(self.ok.at[3, part, self.net.group(i)], 1)
+        self.core_copy(part, i).start()
+
+    def from_core(self, part, i, credit):
+        net = self.net
+        m = net.group(i)
+        lo, hi = PARTS[part]
+        copy = self.core_copy(part, i)
+        copy.wait_recv()
+        slot = lax.rem(i, 2)
+        for chip in range(4):
+            mine = self.g[m, chip, net.core, :, lo:hi].astype(F32)
+            theirs = self.slots[slot, chip, :, 0 : hi - lo].astype(F32)
+            self.g[m, chip, net.core, :, lo:hi] = (mine + theirs).astype(BF16)
+        if credit is not None:
+            p, j = credit
+            pl.semaphore_signal(self.ok.at[3, p, net.group(j)], inc=1, device_id=net.sibling, device_id_type=MESH)
+        copy.wait_send()
+        pl.semaphore_signal(self.ok.at[0, part, m], inc=1, device_id=net.x, device_id_type=MESH)
+        pl.semaphore_signal(self.ok.at[1, part, m], inc=1, device_id=net.y, device_id_type=MESH)
+
+        @pl.when(m != net.z)
+        def _():
+            pl.semaphore_signal(self.ok.at[2, part, net.z], inc=1, device_id=(net.dp, m), device_id_type=MESH)
+
+    def across_copies(self, part, m):
+        net = self.net
+        out = []
+        for kind, rows, to in ((1, slice(0, 48), net.y), (2, slice(48, 96), net.x)):
+            out.append(self.copy(
+                kind, part, m, self.unit(part, m, net.chip_d, net.core, rows),
+                self.unit(part, m, 0, 1 - net.core, rows), to))
+        return out
+
+    def side_copies(self, part, m):
+        net = self.net
+        return [
+            self.copy(kind, part, m, self.unit(part, m, chip, net.core), self.unit(part, m, slot, 1 - net.core), to)
+            for kind, chip, slot, to in ((3, net.chip_x, 1, net.x), (4, net.chip_y, 2, net.y))]
+
+    def z_copy(self, part, m):
+        net = self.net
+        return pltpu.make_async_remote_copy(
+            src_ref=self.unit(part, m, net.chip, net.core), dst_ref=self.unit(part, net.z, 3, 1 - net.core),
+            send_sem=self.sems.at[0, 5, part, m], recv_sem=self.sems.at[1, 5, part, net.z],
+            device_id=(net.dp, m), device_id_type=MESH)
+
+    def add(self, part, m, chip, slot, rows=slice(0, 96)):
+        net = self.net
+        lanes = self.lanes(part)
+        mine = self.g[m, chip, net.core, rows, lanes].astype(F32)
+        theirs = self.g[m, slot, 1 - net.core, rows, lanes].astype(F32)
+        self.g[m, chip, net.core, rows, lanes] = (mine + theirs).astype(BF16)
+
+    def start_across(self, part, i):
+        m = self.net.group(i)
+        pl.semaphore_wait(self.ok.at[0, part, m], 1)
+        pl.semaphore_wait(self.ok.at[1, part, m], 1)
+        for copy in self.across_copies(part, m):
+            copy.start()
+
+    def start_sides(self, part, i):
+        net = self.net
+        m = net.group(i)
+        by_y, by_x = self.across_copies(part, m)
+        by_y.wait_recv()
+        self.add(part, m, net.chip_x, 0, slice(0, 48))
+        by_x.wait_recv()
+        self.add(part, m, net.chip_y, 0, slice(48, 96))
+        for copy in self.side_copies(part, m):
+            copy.start()
+
+    def start_z(self, part, i):
+        net = self.net
+        m = net.group(i)
+        for slot, copy in zip((1, 2), self.side_copies(part, m)):
+            copy.wait_recv()
+            self.add(part, m, net.chip, slot)
+
+        @pl.when(m != net.z)
+        def _():
+            pl.semaphore_wait(self.ok.at[2, part, m], 1)
+            self.z_copy(part, m).start()
+
+    def total(self, part):
+        net = self.net
+        value = self.g[net.z, net.chip, net.core, :, self.lanes(part)].astype(F32)
+        for k in range(1, 4):
+            other = lax.rem(net.z + k, 4)
+            ref = self.unit(part, other, 3, 1 - net.core)
+            pltpu.make_async_remote_copy(
+                src_ref=ref, dst_ref=ref, send_sem=self.sems.at[0, 5, part, other],
+                recv_sem=self.sems.at[1, 5, part, other], device_id=(net.dp, other), device_id_type=MESH).wait_recv()
+            value = value + self.g[other, 3, 1 - net.core, :, self.lanes(part)].astype(F32)
+        return value
+
+    def drain(self):
+        net = self.net
+        for part in range(2):
+
+            def body(m, c, part=part):
+                for copy in self.across_copies(part, m) + self.side_copies(part, m):
+                    copy.wait_send()
+
+                @pl.when(m != net.z)
+                def _():
+                    self.z_copy(part, m).wait_send()
+
+                return c
+
+            lax.fori_loop(0, 4, body, 0)
+
+
 def greet(net):
     barrier = pltpu.get_barrier_semaphore()
     for other in range(1, 8):
@@ -558,18 +695,26 @@
 
 def mega_kernel(
     len_ref, x_ref, dy_ref, q_ref, k_ref, v_ref, o_ref, gate_ref, up_ref, down_ref, ga_ref, gf_ref,
-    out_ref, gt_ref, g_ref, gg_ref,
-    w, gain, gain_parts, bias, xp, dyp, n1, n1t, n2, n2t, dypt, dhbt, qkv, qkv_b, o_own, o_b, do, wo, lse, lse_t, h, acc, res,
-    ag_send, ag_send_z, ag_recv, gn_send, gn_recv, in_sem,
+    out_ref, gt_ref, gq_ref, gk_ref, gv_ref, go_ref, gate_grad_ref, up_grad_ref, down_grad_ref, gga_ref, ggf_ref, bins_ref,
+    w, g, slots, pool, gain, gain_parts, gg_out, gg_in, gg_z, bias, n1t, n2t, dypt, n_b, qkv, qkv_b, o_own, o_b, do, wo, lse, lse_t,
+    h, acc, res,
+    ag_send, ag_send_z, ag_recv, gn_send, gn_recv, in_sem, rs_sems, ok, gt_send, gt_recv, gt_ok, bin_sem, out_sem, gs_send,
+    gs_recv, gz_send, gz_recv,
 ):
     net = Net()
     bins = 4
-    halves = [pltpu.make_async_copy(dy_ref.at[j], g_ref.at[0, :, :, :, 768 * j : 768 * (j + 1)], in_sem.at[j]) for j in (0, 1)]
+    seq = 1536
+    me = net.z
+    xp, dyp, n1, n2 = (pool.at[j] for j in range(4))
+    halves = []
+    for t, ref in enumerate((x_ref, dy_ref)):
+        for j in range(2):
+            halves.append(pltpu.make_async_copy(
+                ref.at[j], g.at[t, :, :, :, 768 * j : 768 * (j + 1)], in_sem.at[2 * t + j]))
     for copy in halves:
         copy.start()
-    seq = x_ref.shape[0]
-    me = net.z
     ag = Gather(net, w, ag_send, ag_send_z, ag_recv)
+    rs = Reduce(net, g, slots, rs_sems, ok)
     build_package(w, net, q_ref, k_ref, v_ref, o_ref, gate_ref, up_ref, down_ref)
     pad = jnp.zeros((1, 32), F32)
     mine = jnp.concatenate([
@@ -584,36 +729,65 @@
     place = placement(len_ref, bins)
     lse[...] = jnp.zeros_like(lse)
 
-    def pack(b):
-        source, segment = packed_source(place, b * CAP, (CAP, 1), 0)
+    def set_bias(b):
+        _, segment = packed_source(place, b * CAP, (CAP, 1), 0)
         _, segment_row = packed_source(place, b * CAP, (1, CAP), 1)
         bias[...] = jnp.where(segment == segment_row, 0.0, NEG)
+
+    def picks(b):
+        source, _ = packed_source(place, b * CAP, (CAP, 1), 0)
         return (source == lax.broadcasted_iota(jnp.int32, (CAP, seq), 1)).astype(BF16)
 
+    def packed(pick, t):
+        return nn(pick[:, 0:768], rows768(g, t, 0, 768)) + nn(pick[:, 768:1536], rows768(g, t, 768, 1536))
+
+    def drops(b, first, count):
+        source, _ = packed_source(place, b * CAP, (1, CAP), 1)
+        return (lax.broadcasted_iota(jnp.int32, (count, CAP), 0) + first == source).astype(BF16)
+
     def unpack(b, value):
-        source, _ = packed_source(place, b * CAP, (1, CAP), 1)
-        drop = (lax.broadcasted_iota(jnp.int32, (seq, CAP), 0) == source).astype(BF16)
-        out_ref[...] = (out_ref[...].astype(F32) + nn(drop, value)).astype(BF16)
-
-    pick = pack(me)
-    xb = nn(pick, x_ref[...])
-    xp[...] = xb.astype(BF16)
+        def body(j, c):
+            at = pl.ds(pl.multiple_of(j * 256, 256), 256)
+            out_ref[at, :] = (out_ref[at, :].astype(F32) + nn(drops(b, j * 256, 256), value)).astype(BF16)
+            return c
+
+        lax.fori_loop(0, seq // 256, body, 0)
+
     for copy in halves:
         copy.wait()
-    dyp[...] = (nn(pick[:, 0:768], rows768(g_ref, 0, 0, 768)) + nn(pick[:, 768:1536], rows768(g_ref, 0, 768, 1536))).astype(BF16)
+    pick = picks(me)
+    xb = packed(pick, 0)
+    xp[...] = xb.astype(BF16)
     h[...] = xb
+    dyp[...] = packed(pick, 1).astype(BF16)
+    set_bias(me)
     dypt[...] = dyp[...].T
     ag.spread(0, 1)
     ag.relay(0, 0)
     join_gains(net, gain_parts, gn_send, gn_recv, gain)
     g1 = gain[0:1, :]
     g2 = gain[1:2, :]
+    xb = h[...]
     n1[...] = (xb * rms_rows(xb) * g1).astype(BF16)
     n1t[...] = n1[...].T
     ag.spread(0, 2)
     ag.across(0, 0)
     ag.relay(0, 1)
     ag.spread(0, 3)
+
+    def bin_copy(k, up):
+        there = bins_ref.at[k]
+        return pltpu.make_async_copy(qkv_b.at[0], there, bin_sem) if up else pltpu.make_async_copy(there, qkv_b.at[0], bin_sem)
+
+    def pack_others(k, c):
+        b = lax.rem(me + 1 + k, bins)
+        qkv_b[0] = packed(picks(b), 0).astype(BF16)
+        copy = bin_copy(k, True)
+        copy.start()
+        copy.wait()
+        return c
+
+    lax.fori_loop(0, 3, pack_others, 0)
 
     def own_forward(i, c):
         m = net.group(i)
@@ -649,12 +823,20 @@
         return c
 
     lax.fori_loop(0, 4, own_forward, 0)
-    hb = h[...]
-    n2[...] = (hb * rms_rows(hb) * g2).astype(BF16)
+    def norm(dst, gain_row):
+        def body(j, c):
+            at = pl.ds(pl.multiple_of(j * 128, 128), 128)
+            rows = h[at, :]
+            dst[at, :] = (rows * rms_rows(rows) * gain_row).astype(BF16)
+            return c
+
+        lax.fori_loop(0, CAP // 128, body, 0)
+
+    norm(n2, g2)
     n2t[...] = n2[...].T
     lse_t[...] = lse[...].T
     acc[...] = jnp.zeros_like(acc)
-    res[...] = hb
+    res[...] = h[...]
 
     def ffn_back(i, c):
         m = net.group(i)
@@ -679,84 +861,203 @@
             gel = 0.5 * a * (1.0 + t)
             u = (gel * up).astype(BF16)
             res[...] += nt(u, w_down)
-            put768(g_ref, m, 1792 + lo, 2048 + lo, nn(dypt[...], u).astype(BF16))
+            put768(g, m, 1792 + lo, 2048 + lo, nn(dypt[...], u).astype(BF16))
             du = nn(dyp[...], w_down)
             slope = 0.5 * (1.0 + t) + 0.5 * a * (1.0 - t * t) * (GELU_COEF * (1.0 + 3.0 * GELU_CUBE * a * a))
             da = (du * up * slope).astype(BF16)
             db = (du * gel).astype(BF16)
-            put768(g_ref, m, 768 + lo, 1024 + lo, nn(n2t[...], da).astype(BF16))
-            put768(g_ref, m, 1280 + lo, 1536 + lo, nn(n2t[...], db).astype(BF16))
+            put768(g, m, 768 + lo, 1024 + lo, nn(n2t[...], da).astype(BF16))
+            put768(g, m, 1280 + lo, 1536 + lo, nn(n2t[...], db).astype(BF16))
             acc[...] += nt(da, w_gate) + nt(db, w_up)
+
+        @pl.when(i < 2)
+        def _():
+            rs.to_core(1, i, False)
+
+        @pl.when(i >= 2)
+        def _():
+            rs.to_core(1, i, True)
+
+        @pl.when(jnp.logical_and(i >= 1, i < 3))
+        def _():
+            rs.from_core(1, i - 1, (1, i + 1))
+
+        @pl.when(i == 3)
+        def _():
+            rs.from_core(1, 2, (0, 0))
+
         return c
 
     lax.fori_loop(0, 4, ffn_back, 0)
     out_ref[...] = jnp.zeros_like(out_ref)
     unpack(me, res[...].astype(BF16))
-    hb = h[...]
-    r2 = rms_rows(hb)
-    dn2 = acc[...]
-    gg_ffn = jnp.sum(dn2 * hb * r2, axis=0, keepdims=True)
-    wg = dn2 * g2
-    dh = dyp[...].astype(F32) + r2 * wg - hb * (r2 * r2 * r2) * jnp.mean(wg * hb, axis=1, keepdims=True)
-    h[...] = dh
-    dhb = dh.astype(BF16)
-    dhbt[...] = dhb.T
-    n2[...] = dhb
-    acc[...] = jnp.zeros_like(acc)
-
-    def attn_back(m, c):
+    def hidden_back(j, total):
+        at = pl.ds(pl.multiple_of(j * 128, 128), 128)
+        hb = h[at, :]
+        r2 = rms_rows(hb)
+        dn2 = acc[at, :]
+        wg = dn2 * g2
+        dh = dyp[at, :].astype(F32) + r2 * wg - hb * (r2 * r2 * r2) * jnp.mean(wg * hb, axis=1, keepdims=True)
+        h[at, :] = dh
+        n2[at, :] = dh.astype(BF16)
+        acc[at, :] = jnp.zeros_like(dh)
+        return total + jnp.sum(dn2 * hb * r2, axis=0, keepdims=True)
+
+    gg_ffn = lax.fori_loop(0, CAP // 128, hidden_back, jnp.zeros((1, 768), F32))
+    n2t[...] = n2[...].T
+    rs.from_core(1, 3, (0, 1))
+    rs.start_across(1, 0)
+
+    def attn_back(i, c):
+        m = net.group(i)
         do[0] = nn(n2[...], wo[m]).astype(BF16)
         attend_group_back(qkv, m, bias, lse_t, do, 0, qkv)
         acc[...] += nt(qkv[m], rows768(w, m, 0, 768))
+
+        rs.start_sides(1, i)
+
+        @pl.when(i < 3)
+        def _():
+            rs.start_across(1, i + 1)
+
         return c
 
     lax.fori_loop(0, 4, attn_back, 0)
-    xb = xp[...].astype(F32)
-    r1 = rms_rows(xb)
-    dn1 = acc[...]
-    gg_attn = jnp.sum(dn1 * xb * r1, axis=0, keepdims=True)
-    wa = dn1 * g1
-    gt = h[...] + r1 * wa - xb * (r1 * r1 * r1) * jnp.mean(wa * xb, axis=1, keepdims=True)
-    gt_ref[...] = gt.astype(BF16)
-    gg_ref[0:1, :] = gg_attn
-    gg_ref[1:2, :] = gg_ffn
-
-    def attn_grads(m, c):
-        grad = nn(n1t[...], qkv[m])
-        go = nn(dhbt[...], o_own[m])
+    def input_back(j, total):
+        at = pl.ds(pl.multiple_of(j * 128, 128), 128)
+        xb = xp[at, :].astype(F32)
+        r1 = rms_rows(xb)
+        dn1 = acc[at, :]
+        wa = dn1 * g1
+        gt = h[at, :] + r1 * wa - xb * (r1 * r1 * r1) * jnp.mean(wa * xb, axis=1, keepdims=True)
+        n_b[at, :] = gt.astype(BF16)
+        return total + jnp.sum(dn1 * xb * r1, axis=0, keepdims=True)
+
+    gg_attn = lax.fori_loop(0, CAP // 128, input_back, jnp.zeros((1, 768), F32))
+    pool[me] = n_b[...]
+    for k in range(1, 4):
+        pl.semaphore_signal(gt_ok.at[me], inc=1, device_id=net.up(k), device_id_type=MESH)
+    gt_copies = []
+    for k in range(1, 4):
+        pl.semaphore_wait(gt_ok.at[lax.rem(me + k, 4)], 1)
+        gt_copies.append(pltpu.make_async_remote_copy(
+            src_ref=pool.at[me], dst_ref=pool.at[me], send_sem=gt_send.at[k - 1], recv_sem=gt_recv.at[me],
+            device_id=net.up(k), device_id_type=MESH))
+        gt_copies[-1].start()
+    gg = jnp.concatenate([gg_attn, gg_ffn, jnp.zeros((6, 768), F32)], axis=0)
+    for d in range(8):
+        gg_out[d] = pltpu.roll(gg, (768 - 96 * d) % 768, 1)[:, 0:128] if d else gg[:, 0:128]
+
+    def gg_copy(k):
+        to = lax.rem(net.dp + k, 8)
+        return pltpu.make_async_remote_copy(
+            src_ref=gg_out.at[to], dst_ref=gg_in.at[net.dp], send_sem=gs_send.at[k - 1], recv_sem=gs_recv.at[net.dp],
+            device_id=(to, net.z), device_id_type=MESH)
+
+    for k in range(1, 8):
+        gg_copy(k).start()
+
+    def attn_grads(i, c):
+        m = net.group(i)
+        go = nn(n2t[...], o_own[m])
         lanes = low_lanes()
-        for t in range(6):
-            g = grad[:, 128 * t : 128 * (t + 1)]
-            if t == 1:
-                g = jnp.where(lanes, g, pltpu.roll(go[:, 0:128], 64, 1))
-            elif t == 3:
-                g = jnp.where(lanes, g, go[:, 0:128])
-            elif t == 5:
-                g = jnp.where(lanes, g, pltpu.roll(go[:, 128:256], 64, 1))
-            put768(g_ref, m, 128 * t, 128 * (t + 1), g.astype(BF16))
+        for j in range(3):
+            grad = nn(n1t[...], qkv[m, :, 256 * j : 256 * (j + 1)])
+            put768(g, m, 256 * j, 256 * j + 128, grad[:, 0:128].astype(BF16))
+            if j == 1:
+                extra = go[:, 0:128]
+            else:
+                extra = pltpu.roll(go[:, 64 * j : 64 * j + 128], 64, 1)
+            put768(g, m, 256 * j + 128, 256 * (j + 1), jnp.where(lanes, grad[:, 128:256], extra).astype(BF16))
+
+        rs.to_core(0, i, True)
+
+        @pl.when(jnp.logical_and(i >= 1, i < 3))
+        def _():
+            rs.from_core(0, i - 1, (0, i + 1))
+
+        @pl.when(i == 3)
+        def _():
+            rs.from_core(0, 2, None)
+
         return c
 
     lax.fori_loop(0, 4, attn_grads, 0)
+    rs.from_core(0, 3, None)
+
+    part = gg_out[net.dp]
+    for k in range(1, 8):
+        other = lax.rem(net.dp + k, 8)
+        pltpu.make_async_remote_copy(
+            src_ref=gg_out.at[other], dst_ref=gg_in.at[other], send_sem=gs_send.at[k - 1], recv_sem=gs_recv.at[other],
+            device_id=net.sibling, device_id_type=MESH).wait_recv()
+        part = part + gg_in[other]
+    gg_z[me] = part
+    gz_copies = [pltpu.make_async_remote_copy(
+        src_ref=gg_z.at[me], dst_ref=gg_z.at[me], send_sem=gz_send.at[k - 1], recv_sem=gz_recv.at[me],
+        device_id=net.up(k), device_id_type=MESH) for k in range(1, 4)]
+    for copy in gz_copies:
+        copy.start()
 
     def others(k, c):
         b = lax.rem(me + 1 + k, bins)
-        xo = nn(pack(b), x_ref[...])
-        n1[...] = (xo * rms_rows(xo) * g1).astype(BF16)
-        h[...] = xo
+        copy = bin_copy(k, False)
+        copy.start()
+        set_bias(b)
+        copy.wait()
+        h[...] = qkv_b[0].astype(F32)
+        norm(n_b, g1)
 
         def attend(m, c):
-            qkv_b[0] = nn(n1[...], rows768(w, m, 0, 768)).astype(BF16)
+            qkv_b[0] = nn(n_b[...], rows768(w, m, 0, 768)).astype(BF16)
             attend_group(qkv_b, 0, bias, o_b, 0)
             h[...] += nt(o_b[0], wo[m])
+
+            @pl.when(jnp.logical_and(k == 0, m == 0))
+            def _():
+                rs.start_z(1, 0)
+
+            @pl.when(jnp.logical_and(k == 0, m == 1))
+            def _():
+                rs.start_z(1, 1)
+
+            @pl.when(jnp.logical_and(k == 0, m == 2))
+            def _():
+                rs.start_across(0, 0)
+                rs.start_across(0, 1)
+                rs.start_z(1, 2)
+
+            @pl.when(jnp.logical_and(k == 0, m == 3))
+            def _():
+                rs.start_sides(0, 0)
+                rs.start_sides(0, 1)
+                rs.start_z(1, 3)
+
+            @pl.when(jnp.logical_and(k == 1, m == 0))
+            def _():
+                rs.start_across(0, 2)
+                rs.start_across(0, 3)
+                rs.start_z(0, 0)
+
+            @pl.when(jnp.logical_and(k == 1, m == 1))
+            def _():
+                rs.start_sides(0, 2)
+                rs.start_sides(0, 3)
+                rs.start_z(0, 1)
+
+            @pl.when(jnp.logical_and(k == 1, m == 3))
+            def _():
+                rs.start_z(0, 2)
+                rs.start_z(0, 3)
+
             return c
 
         lax.fori_loop(0, 4, attend, 0)
-        ho = h[...]
-        n2[...] = (ho * rms_rows(ho) * g2).astype(BF16)
+        norm(n_b, g2)
 
         def ffn(m, c):
-            a = nn(n2[...], rows768(w, m, 768, 1280))
-            up = nn(n2[...], rows768(w, m, 1280, 1792))
+            a = nn(n_b[...], rows768(w, m, 768, 1280))
+            up = nn(n_b[...], rows768(w, m, 1280, 1792))
             u = (0.5 * a * (1.0 + gelu_parts(a)) * up).astype(BF16)
             h[...] += nt(u, rows768(w, m, 1792, 2304))
             return c
@@ -766,8 +1067,45 @@
         return c
 
     lax.fori_loop(0, 3, others, 0)
-    for copy in gain_copies:
+
+    rows = (h, acc, res)
+    for j in range(3):
+        rows[j][...] = nn(drops(me, CAP * j, CAP), pool[me])
+    for k in (1, 3, 2):
+        other = lax.rem(me + k, 4)
+        pltpu.make_async_remote_copy(
+            src_ref=pool.at[other], dst_ref=pool.at[other], send_sem=gt_send.at[k - 1], recv_sem=gt_recv.at[other],
+            device_id=net.up(k), device_id_type=MESH).wait_recv()
+        for j in range(3):
+            rows[j][...] += nn(drops(other, CAP * j, CAP), pool[other])
+    outs = [pltpu.make_async_copy(rows[j], gt_ref.at[j], out_sem.at[j]) for j in range(3)]
+    for copy in outs:
+        copy.start()
+
+    for k in range(1, 4):
+        other = lax.rem(me + k, 4)
+        pltpu.make_async_remote_copy(
+            src_ref=gg_z.at[other], dst_ref=gg_z.at[other], send_sem=gz_send.at[k - 1], recv_sem=gz_recv.at[other],
+            device_id=net.up(k), device_id_type=MESH).wait_recv()
+        part = part + gg_z[other]
+    gga_ref[...] = part[0:1, 0:96]
+    ggf_ref[...] = part[1:2, 0:96]
+    ffn_sum = rs.total(1)
+    gate_grad_ref[...] = ffn_sum[:, 0:512]
+    up_grad_ref[...] = ffn_sum[:, 512:1024]
+    down_grad_ref[...] = ffn_sum[:, 1024:1536].T
+    attn_sum = rs.total(0)
+    gq_ref[...] = attn_sum[:, 0:192]
+    gk_ref[...] = attn_sum[:, 256:448]
+    gv_ref[...] = attn_sum[:, 512:704]
+    go_ref[...] = jnp.concatenate([attn_sum[:, 192:256], attn_sum[:, 448:512], attn_sum[:, 704:768]], axis=1).T
+    for copy in outs:
+        copy.wait()
+    for copy in gain_copies + gt_copies + gz_copies:
         copy.wait_send()
+    for k in range(1, 8):
+        gg_copy(k).wait_send()
+    rs.drain()
     ag.drain()
 
 
@@ -792,22 +1130,29 @@
     act = pltpu.VMEM((CAP, width), BF16)
     act_t = pltpu.VMEM((width, CAP), BF16)
     wide = pltpu.VMEM((CAP, width), F32)
-    out, gt, g, gg = pl.pallas_call(
+    hbm = pl.BlockSpec(memory_space=pl.ANY)
+
+    def f32(*shape):
+        return jax.ShapeDtypeStruct(shape, F32)
+
+    out, gt, gq, gk, gv, go, gate, up, down, gain_a, gain_f, _ = pl.pallas_call(
         mega_kernel,
         out_shape=(
-            jax.ShapeDtypeStruct((seq, width), BF16),
-            jax.ShapeDtypeStruct((CAP, width), BF16),
-            jax.ShapeDtypeStruct((4, 4, 2, 96, 2304), BF16),
-            jax.ShapeDtypeStruct((8, width), F32),
+            jax.ShapeDtypeStruct((seq, width), BF16), f32(3, CAP, width), f32(96, 192), f32(96, 192), f32(96, 192), f32(192, 96),
+            f32(96, 512), f32(96, 512), f32(512, 96), f32(1, 96), f32(1, 96), jax.ShapeDtypeStruct((3, CAP, width), BF16),
         ),
-        in_specs=[smem, vmem, pl.BlockSpec(memory_space=pl.ANY)] + [vmem] * 9,
-        out_specs=[vmem] * 4,
+        in_specs=[smem, hbm, hbm] + [vmem] * 9,
+        out_specs=[vmem, hbm] + [vmem] * 9 + [hbm],
         scratch_shapes=[
             pltpu.VMEM((4, 4, 2, 96, 2304), BF16),
+            pltpu.VMEM((4, 4, 2, 96, 2304), BF16),
+            pltpu.VMEM((2, 4, 96, 1536), BF16),
+            pltpu.VMEM((4, CAP, width), BF16),
             pltpu.VMEM((8, width), F32),
-            pltpu.VMEM((8, 8, 128), F32),
+            pltpu.VMEM((8, 8, 128), F32), pltpu.VMEM((8, 8, 128), F32), pltpu.VMEM((8, 8, 128), F32),
+            pltpu.VMEM((4, 8, 128), F32),
             pltpu.VMEM((CAP, CAP), F32),
-            act, act, act, act_t, act, act_t, act_t, act_t,
+            act_t, act_t, act_t, act,
             pltpu.VMEM((4, CAP, width), BF16),
             pltpu.VMEM((1, CAP, width), BF16),
             pltpu.VMEM((4, CAP, 256), BF16),
@@ -817,40 +1162,18 @@
             pltpu.VMEM((CAP, 128), F32),
             pltpu.VMEM((128, CAP), F32),
             wide, wide, wide,
-            dma((2, 4, 4, 3)), dma((2, 3)), dma((2, 4, 4, 2)), dma((7,)), dma((8,)), dma((2,)),
+            dma((2, 4, 4, 3)), dma((2, 3)), dma((2, 4, 4, 2)), dma((7,)), dma((8,)), dma((4,)),
+            dma((2, 6, 2, 4)), pltpu.SemaphoreType.REGULAR((4, 2, 4)),
+            dma((3,)), dma((4,)), pltpu.SemaphoreType.REGULAR((4,)), dma, dma((3,)), dma((7,)), dma((8,)), dma((3,)), dma((4,)),
         ],
         compiler_params=pltpu.CompilerParams(
             vmem_limit_bytes=60 * 2**20, collective_id=0, has_side_effects=True),
         name="layer",
-    )(lengths, tokens.reshape(seq, width), cotangent.reshape(2, 4, 2, 96, width), query_weight, key_weight, value_weight, out_weight,
-      gate_weight, up_weight, down_weight, attn_gain.reshape(1, 96), ffn_gain.reshape(1, 96))
-    bins = 4
-    gt_all = lax.all_gather(gt, "mp", axis=0)
-    grad_tokens = pl.pallas_call(
-        unpack_kernel,
-        out_shape=jax.ShapeDtypeStruct((seq, width), F32),
-        in_specs=[smem, vmem],
-        out_specs=vmem,
-        compiler_params=pltpu.CompilerParams(vmem_limit_bytes=60 * 2**20),
-        name="unpack",
-    )(lengths, gt_all)
-    g = g.reshape(4, width, 2304)
-    g = lax.psum_scatter(g, "mp", scatter_dimension=0, tiled=False)
-    g = lax.psum_scatter(g, "dp", scatter_dimension=0, tiled=True).astype(F32)
-    gg = lax.psum_scatter(lax.psum(gg[0:2], "mp"), "dp", scatter_dimension=1, tiled=True)
-    go = jnp.concatenate([g[:, 192:256], g[:, 448:512], g[:, 704:768]], axis=1).T
+    )(lengths, tokens.reshape(2, 4, 2, 96, width), cotangent.reshape(2, 4, 2, 96, width), query_weight, key_weight,
+      value_weight, out_weight, gate_weight, up_weight, down_weight, attn_gain.reshape(1, 96), ffn_gain.reshape(1, 96))
     return (
-        out.reshape(rows, seq, width),
-        grad_tokens.reshape(rows, seq, width),
-        g[:, 0:192],
-        g[:, 256:448],
-        g[:, 512:704],
-        go,
-        gg[0],
-        g[:, 768:1280],
-        g[:, 1280:1792],
-        g[:, 1792:2304].T,
-        gg[1],
+        out.reshape(rows, seq, width), gt.reshape(rows, seq, width), gq, gk, gv, go, gain_a.reshape(96), gate, up, down,
+        gain_f.reshape(96),
     )
 def solution(mesh):
     body = on_this_slice if dict(mesh.shape) == {"dp": 8, "mp": 4} else per_device

time: 624 us -> 277 us (0.44)
  waiting for transfers between devices: 367 us -> 0 us
  Pallas kernels: 218 us -> 262 us
  between operations: 13.8 us -> 0.7 us
  blocking collectives: 11.8 us -> 0 us
    reduce_scatter x2 -> x0, waiting for transfers between devices: 276 us -> none  [the longest x1 235 us: on_this_slice(): g = lax.psum_scatter(g, 'mp', scatter_dimension=0, tiled=False)]
    pallas_call x1, Pallas kernels: 208 us -> 262 us  [on_this_slice(): pl.pallas_call(mega_kernel, out_shape=(jax.ShapeDtypeStruct((seq, width),...]
    all_gather x1 -> x0, waiting for transfers between devices: 51.9 us -> none  [on_this_slice(): gt_all = lax.all_gather(gt, 'mp', axis=0)]
    unnamed x5 -> x0, waiting for transfers between devices: 39.2 us -> none
    psum x1 -> x0, blocking collectives: 11.8 us -> none  [on_this_slice(): lax.psum(gg[0:2], 'mp')]
    pallas_call x1 -> x0, Pallas kernels: 9.48 us -> none  [on_this_slice(): pl.pallas_call(unpack_kernel, out_shape=jax.ShapeDtypeStruct((seq, width)...]
    unnamed x7 -> x30, local copies, waits for them, and re-layouts: 5.72 us -> 14.1 us
  transfers between devices with their start and end apart: 4 -> 0, of which waited for: 4 -> 0; matrix products, arithmetic and copies ran while one was open for 0% -> 0% of each run, Pallas kernels for 2% -> 0%
where the time goes in v3:
time: 277 us
  Pallas kernels  262 us (95%)
  local copies, waits for them, and re-layouts  14.1 us (5%)
    pallas_call x1, Pallas kernels, on_this_slice(): pl.pallas_call(mega_kernel, out_shape=(jax.ShapeDtypeStruct((seq, width),...  262 us
    unnamed x30, local copies, waits for them, and re-layouts  14.1 us

profile of v3, /device:TPU:0, one launch (start us, length us, event | category | flops | bytes accessed | tf_op | source)
XLA Modules:
  0.0 277.1 jit_solution(13739347165137072410)
XLA Ops:
  0.6 1.8 copy.23.down_ref
  2.4 262.4 %layer.1 = (bf16[1536,768]{1,0:T(8,128)(2,1)}, f32[3,512,768]{2,1,0:T(8,128)}, f32[96,192]{1,0:T(8,128)}, f32[96,192]{1,0:T(8,128)}, f32[96,192]{1,0:T(8,128)}, ...) custom-call(s32[1,8]{1,0:T(1,128)} %len_ref.1, ...), custom_call_target="tpu_custom_call" | custom-call | tf_op jit(solution)/shard_map/layer/pallas_call | solution.py:1138
  264.8 1.8 copy.24
  266.5 0.0 copy-start
  266.5 3.4 %copy.35 = bf16[1,1536,768]{2,1,0:T(8,128)(2,1)} copy(bf16[1,1536,768]{2,1,0:T(8,128)(2,1)} %bitcast.11) | data formatting | bytes 4718592
  269.9 0.0 copy-done
  269.9 0.0 copy-start.6
  269.9 0.0 copy-start.5
  269.9 0.0 copy-start.4
  269.9 0.0 copy-start.3
  270.0 0.0 copy-start.8
  270.0 0.0 copy-start.2
  270.0 0.0 copy-start.1
  270.0 0.0 copy-start.7
  270.0 2.2 copy.36
  272.2 0.0 copy-done.6
  272.2 0.6 copy.37
  272.8 0.0 copy-done.5
  272.8 0.6 copy.38
  273.5 0.0 copy-done.4
  273.5 0.6 copy.39
  274.1 0.0 copy-done.3
  274.1 0.6 copy.40
  274.8 0.0 copy-done.8
  274.8 0.5 copy.41
  275.3 0.0 copy-done.2
  275.3 0.7 copy.42
  275.9 0.0 copy-done.1
  276.0 0.7 copy.43
  276.6 0.0 copy-done.7
  276.6 0.5 copy.44
Async XLA Ops:
  266.5 3.4 %copy-start = (f32[3,512,768]{2,1,0:T(8,128)S(1)}, f32[3,512,768]{2,1,0:T(8,128)}, u32[]{:S(2)}) copy-start(f32[3,512,768]{2,1,0:T(8,128)} %get-tuple-element.23) | copy-start | bytes 14155780
  269.9 2.2 copy-start.6
  269.9 2.9 %copy-start.5 = (f32[96,192]{1,0:T(8,128)S(1)}, f32[96,192]{1,0:T(8,128)}, u32[]{:S(2)}) copy-start(f32[96,192]{1,0:T(8,128)} %get-tuple-element.58) | copy-start | bytes 221188
  269.9 3.5 %copy-start.4 = (f32[96,192]{1,0:T(8,128)S(1)}, f32[96,192]{1,0:T(8,128)}, u32[]{:S(2)}) copy-start(f32[96,192]{1,0:T(8,128)} %get-tuple-element.59) | copy-start | bytes 221188
  269.9 4.2 %copy-start.3 = (f32[192,96]{1,0:T(8,128)S(1)}, f32[192,96]{1,0:T(8,128)}, u32[]{:S(2)}) copy-start(f32[192,96]{1,0:T(8,128)} %get-tuple-element.60) | copy-start | bytes 221188
  270.0 4.8 %copy-start.8 = (f32[1,96]{1,0:T(1,128)S(1)}, f32[1,96]{1,0:T(1,128)}, u32[]{:S(2)}) copy-start(f32[1,96]{1,0:T(1,128)} %get-tuple-element.28) | copy-start | bytes 1156
  270.0 5.3 %copy-start.2 = (f32[96,512]{1,0:T(8,128)S(1)}, f32[96,512]{1,0:T(8,128)}, u32[]{:S(2)}) copy-start(f32[96,512]{1,0:T(8,128)} %get-tuple-element.62) | copy-start | bytes 589828
  270.0 6.0 %copy-start.1 = (f32[96,512]{1,0:T(8,128)S(1)}, f32[96,512]{1,0:T(8,128)}, u32[]{:S(2)}) copy-start(f32[96,512]{1,0:T(8,128)} %get-tuple-element.63) | copy-start | bytes 589828
  270.0 6.7 %copy-start.7 = (f32[1,96]{1,0:T(1,128)S(1)}, f32[1,96]{1,0:T(1,128)}, u32[]{:S(2)}) copy-start(f32[1,96]{1,0:T(1,128)} %get-tuple-element.32) | copy-start | bytes 1156

commit v4 on v3

--- a/solution.py
+++ b/solution.py
@@ -91,57 +91,51 @@
 
 
 def attend_group(qkv, m, bias, o_ref, at, lse_ref=None, qb=256):
-    def rows_body(i, carry):
-        rows = pl.ds(pl.multiple_of(i * qb, qb), qb)
-        sums = [None, None]
-        for head, (tq, tk, tv, low) in enumerate(HEADS):
-            q = half(qkv[m, rows, 128 * tq : 128 * (tq + 1)], low) * jnp.asarray(0.125, BF16)
-            s = nt(q, tile_of(qkv, m, tk)) + bias[rows, :]
+    for i in range(CAP // qb):
+        rows = slice(i * qb, (i + 1) * qb)
+        scores = []
+        for tq, tk, tv, low in HEADS:
+            q = half(tile_of(qkv, m, tq, rows), low) * jnp.asarray(0.125, BF16)
+            scores.append(nt(q, tile_of(qkv, m, tk)))
+        shares, totals = [], []
+        for head, s in enumerate(scores):
+            s = s + bias[rows, :]
             top = jnp.max(s, axis=1, keepdims=True)
             e = jnp.exp(s - top)
             total = jnp.sum(e, axis=1, keepdims=True)
-            p = (e * (1.0 / total)).astype(BF16)
-            o = nn(p, half(tile_of(qkv, m, tv), low))
-            j = 0 if head < 2 else 1
-            sums[j] = o if sums[j] is None else sums[j] + o
+            shares.append(e.astype(BF16))
+            totals.append(total)
             if lse_ref is not None:
                 lane = lax.broadcasted_iota(jnp.int32, (1, 128), 1)
                 lse_ref[rows, :] = jnp.where(lane == 3 * m + head, top + jnp.log(total), lse_ref[rows, :])
-        o_ref[at, rows, 0:128] = sums[0].astype(BF16)
-        o_ref[at, rows, 128:256] = sums[1].astype(BF16)
-        return carry
-
-    lax.fori_loop(0, CAP // qb, rows_body, 0)
-
-
-def attend_group_back(qkv, m, bias, lse_t, do_ref, at, dqkv, qb=256):
+        parts = []
+        for (tq, tk, tv, low), e, total in zip(HEADS, shares, totals):
+            parts.append(nn(e, half(tile_of(qkv, m, tv), low)) * (1.0 / total))
+        o_ref[at, rows, 0:128] = (parts[0] + parts[1]).astype(BF16)
+        o_ref[at, rows, 128:256] = parts[2].astype(BF16)
+
+
+def attend_group_back(qkv, m, bias, lse_t, do_ref, at, dqkv):
     dk = [None, None]
     dv = [None, None]
-    dq = [[None] * (CAP // qb), [None] * (CAP // qb)]
+    dq = [None, None]
+    scale = jnp.asarray(0.125, BF16)
     for head, (tq, tk, tv, low) in enumerate(HEADS):
         j = 0 if head < 2 else 1
-        k = half(tile_of(qkv, m, tk), low) * jnp.asarray(0.125, BF16)
-        v = half(tile_of(qkv, m, tv), low)
-        lse = lse_t[pl.ds(3 * m + head, 1), :]
-        for i in range(CAP // qb):
-            rows = slice(i * qb, (i + 1) * qb)
-            q = tile_of(qkv, m, tq, rows)
-            do = do_ref[at, rows, 128 * j : 128 * (j + 1)]
-            p = jnp.exp(nt(k, q) + bias[:, rows] - lse[:, rows])
-            dp = nt(v, do)
-            delta = jnp.sum(p * dp, axis=0, keepdims=True)
-            ds = (p * (dp - delta)).astype(BF16)
-            dv_part = nn(p.astype(BF16), half(do, low))
-            dk_part = nn(ds, half(q, low) * jnp.asarray(0.125, BF16))
-            dq_part = tn(ds, k)
-            dv[j] = dv_part if dv[j] is None else dv[j] + dv_part
-            dk[j] = dk_part if dk[j] is None else dk[j] + dk_part
-            dq[j][i] = dq_part if dq[j][i] is None else dq[j][i] + dq_part
+        k = half(tile_of(qkv, m, tk), low) * scale
+        s = nt(k, tile_of(qkv, m, tq))
+        do = do_ref[at, :, 128 * j : 128 * (j + 1)]
+        dp = nt(half(tile_of(qkv, m, tv), low), do)
+        p = jnp.exp(s + bias[...] - lse_t[pl.ds(3 * m + head, 1), :])
+        delta = jnp.sum(p * dp, axis=0, keepdims=True)
+        ds = (p * (dp - delta)).astype(BF16)
+        parts = (
+            nn(p.astype(BF16), half(do, low)), nn(ds, half(tile_of(qkv, m, tq), low) * scale), tn(ds, k))
+        for total, part in zip((dv, dk, dq), parts):
+            total[j] = part if total[j] is None else total[j] + part
     for j in range(2):
-        for i in range(CAP // qb):
-            dqkv[m, i * qb : (i + 1) * qb, 128 * j : 128 * (j + 1)] = dq[j][i].astype(BF16)
-        dqkv[m, :, 128 * (2 + j) : 128 * (3 + j)] = dk[j].astype(BF16)
-        dqkv[m, :, 128 * (4 + j) : 128 * (5 + j)] = dv[j].astype(BF16)
+        for t, total in ((0, dq), (2, dk), (4, dv)):
+            dqkv[m, :, 128 * (t + j) : 128 * (t + j + 1)] = total[j].astype(BF16)
 
 
 def out_weight_tiles(w, m):
@@ -409,6 +403,9 @@
     def up(self, k):
         return (self.dp, lax.rem(self.z + k, 4))
 
+    def along(self, step):
+        return (self.dp, lax.rem(self.z + 4 + step, 4))
+
     def group(self, i):
         z = self.z
         one = jnp.where(z == 0, 1, jnp.where(z == 1, 0, jnp.where(z == 2, 3, 2)))
@@ -417,57 +414,65 @@
 
 
 class Gather:
-    def __init__(self, net, w, send, send_z, recv):
-        self.net, self.w, self.send, self.send_z, self.recv = net, w, send, send_z, recv
-
-    def unit(self, part, m, chip, core):
+    def __init__(self, net, w, send, recv):
+        self.net, self.w, self.send, self.recv = net, w, send, recv
+
+    def copy(self, part, m, chip, core, kind, to, rows=None):
         lo, hi = PARTS[part]
-        return self.w.at[m, chip, core, :, lo:hi]
-
-    def copy(self, part, m, chip, core, sem, to):
-        ref = self.unit(part, m, chip, core)
+        first, last, mark = (0, 96, 0) if rows is None else (48 * rows, 48 * (rows + 1), 1 + rows)
+        ref = self.w.at[m, chip, core, first:last, lo:hi]
         return pltpu.make_async_remote_copy(
-            src_ref=ref, dst_ref=ref, send_sem=sem, recv_sem=self.recv.at[part, m, chip, core],
-            device_id=to, device_id_type=MESH)
-
-    def wait(self, part, m, chip, core):
-        self.copy(part, m, chip, core, self.send.at[part, m, chip, 0], self.net.sibling).wait_recv()
-
-    def along_z(self, part):
-        net = self.net
-        for k in range(1, 4):
-            self.copy(part, net.z, net.chip, net.core, self.send_z.at[part, k - 1], net.up(k)).start()
+            src_ref=ref, dst_ref=ref, send_sem=self.send.at[part, m, chip, kind],
+            recv_sem=self.recv.at[part, m, chip, core, mark], device_id=to, device_id_type=MESH)
+
+    def wait(self, part, m, chip, core, rows=None):
+        self.copy(part, m, chip, core, 0, self.net.sibling, rows).wait_recv()
+
+    def each_along_z(self, part, m, act):
+        net = self.net
+
+        @pl.when(jnp.logical_and(m <= net.z, net.z < 3))
+        def _():
+            act(self.copy(part, m, net.chip, net.core, 3, net.along(1)))
+
+        @pl.when(jnp.logical_and(m >= net.z, net.z > 0))
+        def _():
+            act(self.copy(part, m, net.chip, net.core, 4, net.along(-1)))
+
+    def own_copies(self, part, m):
+        net = self.net
+        return [self.copy(part, m, net.chip, net.core, k, to) for k, to in enumerate((net.x, net.y, net.sibling))]
+
+    def relay_copies(self, part, m):
+        net = self.net
+        return [
+            self.copy(part, m, net.chip_x, net.core, 0, net.y, 0), self.copy(part, m, net.chip_x, net.core, 2, net.sibling),
+            self.copy(part, m, net.chip_y, net.core, 1, net.x, 1), self.copy(part, m, net.chip_y, net.core, 2, net.sibling)]
 
     def spread(self, part, i):
         net = self.net
         m = net.group(i)
-        if isinstance(i, int):
-            if i > 0:
-                self.wait(part, m, net.chip, net.core)
-        else:
-            @pl.when(i > 0)
-            def _():
-                self.wait(part, m, net.chip, net.core)
-        for k, to in enumerate((net.x, net.y, net.sibling)):
-            self.copy(part, m, net.chip, net.core, self.send.at[part, m, net.chip, k], to).start()
+        if not isinstance(i, int) or i > 0:
+            self.wait(part, m, net.chip, net.core)
+        self.each_along_z(part, m, lambda copy: copy.start())
+        for copy in self.own_copies(part, m):
+            copy.start()
 
     def relay(self, part, i):
         net = self.net
         m = net.group(i)
-        first = m < 2
-        self.wait(part, m, net.chip_x, net.core)
-        self.copy(part, m, net.chip_x, net.core, self.send.at[part, m, net.chip_x, 2], net.sibling).start()
-        self.wait(part, m, net.chip_y, net.core)
-        source = jnp.where(first, net.chip_x, net.chip_y)
-        target = jnp.where(first, net.chip_y, net.chip_x)
-        self.copy(part, m, source, net.core, self.send.at[part, m, source, 0], (2 * target + net.core, net.z)).start()
-        self.copy(part, m, net.chip_y, net.core, self.send.at[part, m, net.chip_y, 2], net.sibling).start()
+        copies = self.relay_copies(part, m)
+        for j, chip in enumerate((net.chip_x, net.chip_y)):
+            self.wait(part, m, chip, net.core)
+            copies[2 * j].start()
+            copies[2 * j + 1].start()
 
     def across(self, part, i):
         net = self.net
         m = net.group(i)
-        self.wait(part, m, net.chip_d, net.core)
-        self.copy(part, m, net.chip_d, net.core, self.send.at[part, m, net.chip_d, 2], net.sibling).start()
+        self.wait(part, m, net.chip_d, net.core, 0)
+        self.wait(part, m, net.chip_d, net.core, 1)
+        self.copy(part, m, net.chip_d, net.core, 2, net.sibling).start()
 
     def complete(self, part, i):
         net = self.net
@@ -477,29 +482,21 @@
 
     def drain(self):
         net = self.net
-
-        def sent(part, m, chip, sem):
-            self.copy(part, m, chip, net.core, sem, net.sibling).wait_send()
-
         for part in range(2):
-            for k in range(3):
-                sent(part, net.z, net.chip, self.send_z.at[part, k])
 
             def body(m, c, part=part):
-                for k in range(3):
-                    sent(part, m, net.chip, self.send.at[part, m, net.chip, k])
-                for chip in (net.chip_x, net.chip_y, net.chip_d):
-                    sent(part, m, chip, self.send.at[part, m, chip, 2])
-                source = jnp.where(m < 2, net.chip_x, net.chip_y)
-                sent(part, m, source, self.send.at[part, m, source, 0])
+                self.each_along_z(part, m, lambda copy: copy.wait_send())
+                for copy in self.own_copies(part, m) + self.relay_copies(part, m):
+                    copy.wait_send()
+                self.copy(part, m, net.chip_d, net.core, 2, net.sibling).wait_send()
                 return c
 
             lax.fori_loop(0, 4, body, 0)
 
 
 class Reduce:
-    def __init__(self, net, g, slots, sems, ok):
-        self.net, self.g, self.slots, self.sems, self.ok = net, g, slots, sems, ok
+    def __init__(self, net, g, slots, zbuf, sems, ok):
+        self.net, self.g, self.slots, self.zbuf, self.sems, self.ok = net, g, slots, zbuf, sems, ok
 
     def lanes(self, part):
         return slice(*PARTS[part])
@@ -532,9 +529,7 @@
         copy.wait_recv()
         slot = lax.rem(i, 2)
         for chip in range(4):
-            mine = self.g[m, chip, net.core, :, lo:hi].astype(F32)
-            theirs = self.slots[slot, chip, :, 0 : hi - lo].astype(F32)
-            self.g[m, chip, net.core, :, lo:hi] = (mine + theirs).astype(BF16)
+            self.g[m, chip, net.core, :, lo:hi] = self.g[m, chip, net.core, :, lo:hi] + self.slots[slot, chip, :, 0 : hi - lo]
         if credit is not None:
             p, j = credit
             pl.semaphore_signal(self.ok.at[3, p, net.group(j)], inc=1, device_id=net.sibling, device_id_type=MESH)
@@ -542,9 +537,13 @@
         pl.semaphore_signal(self.ok.at[0, part, m], inc=1, device_id=net.x, device_id_type=MESH)
         pl.semaphore_signal(self.ok.at[1, part, m], inc=1, device_id=net.y, device_id_type=MESH)
 
-        @pl.when(m != net.z)
-        def _():
-            pl.semaphore_signal(self.ok.at[2, part, net.z], inc=1, device_id=(net.dp, m), device_id_type=MESH)
+        @pl.when(jnp.logical_and(m >= net.z, net.z > 0))
+        def _():
+            pl.semaphore_signal(self.ok.at[2, part, m], inc=1, device_id=net.along(-1), device_id_type=MESH)
+
+        @pl.when(jnp.logical_and(m <= net.z, net.z < 3))
+        def _():
+            pl.semaphore_signal(self.ok.at[2, part, m], inc=1, device_id=net.along(1), device_id_type=MESH)
 
     def across_copies(self, part, m):
         net = self.net
@@ -561,19 +560,42 @@
             self.copy(kind, part, m, self.unit(part, m, chip, net.core), self.unit(part, m, slot, 1 - net.core), to)
             for kind, chip, slot, to in ((3, net.chip_x, 1, net.x), (4, net.chip_y, 2, net.y))]
 
-    def z_copy(self, part, m):
-        net = self.net
-        return pltpu.make_async_remote_copy(
-            src_ref=self.unit(part, m, net.chip, net.core), dst_ref=self.unit(part, net.z, 3, 1 - net.core),
-            send_sem=self.sems.at[0, 5, part, m], recv_sem=self.sems.at[1, 5, part, net.z],
-            device_id=(net.dp, m), device_id_type=MESH)
+    def each_z(self, part, m, act):
+        net = self.net
+        z = net.z
+        src = self.unit(part, m, net.chip, net.core)
+        far = self.unit(part, m, 3, 1 - net.core)
+        lo, hi = PARTS[part]
+        near = self.zbuf.at[:, lo:hi]
+
+        def copy(dst, kind, step):
+            return pltpu.make_async_remote_copy(
+                src_ref=src, dst_ref=dst, send_sem=self.sems.at[0, 5, part, m], recv_sem=self.sems.at[1, kind, part, m],
+                device_id=net.along(step), device_id_type=MESH)
+
+        for test, dst, kind, step in ((m > z, far, 5, 1), (m < z - 1, far, 5, -1), (m == z - 1, near, 6, -1)):
+
+            @pl.when(test)
+            def _(dst=dst, kind=kind, step=step):
+                act(copy(dst, kind, step))
+
+    def z_arrived(self, part, m, near):
+        net = self.net
+        lo, hi = PARTS[part]
+        ref = self.zbuf.at[:, lo:hi] if near else self.unit(part, m, 3, 1 - net.core)
+        pltpu.make_async_remote_copy(
+            src_ref=ref, dst_ref=ref, send_sem=self.sems.at[0, 5, part, m],
+            recv_sem=self.sems.at[1, 6 if near else 5, part, m], device_id=net.sibling, device_id_type=MESH).wait_recv()
+        if near:
+            mine = self.g[m, net.chip, net.core, :, lo:hi]
+            self.g[m, net.chip, net.core, :, lo:hi] = mine + self.zbuf[:, lo:hi]
+        else:
+            self.add(part, m, net.chip, 3)
 
     def add(self, part, m, chip, slot, rows=slice(0, 96)):
         net = self.net
         lanes = self.lanes(part)
-        mine = self.g[m, chip, net.core, rows, lanes].astype(F32)
-        theirs = self.g[m, slot, 1 - net.core, rows, lanes].astype(F32)
-        self.g[m, chip, net.core, rows, lanes] = (mine + theirs).astype(BF16)
+        self.g[m, chip, net.core, rows, lanes] = self.g[m, chip, net.core, rows, lanes] + self.g[m, slot, 1 - net.core, rows, lanes]
 
     def start_across(self, part, i):
         m = self.net.group(i)
@@ -593,29 +615,39 @@
         for copy in self.side_copies(part, m):
             copy.start()
 
-    def start_z(self, part, i):
+    def gather_sides(self, part, i):
         net = self.net
         m = net.group(i)
         for slot, copy in zip((1, 2), self.side_copies(part, m)):
             copy.wait_recv()
             self.add(part, m, net.chip, slot)
 
-        @pl.when(m != net.z)
+    def start_z(self, part, m):
+        net = self.net
+        z = net.z
+
+        @pl.when(jnp.logical_or(jnp.logical_and(m > z, z > 0), jnp.logical_and(m < z, z < 3)))
+        def _():
+            self.z_arrived(part, m, False)
+
+        @pl.when(m != z)
         def _():
             pl.semaphore_wait(self.ok.at[2, part, m], 1)
-            self.z_copy(part, m).start()
+
+        self.each_z(part, m, lambda copy: copy.start())
 
     def total(self, part):
         net = self.net
-        value = self.g[net.z, net.chip, net.core, :, self.lanes(part)].astype(F32)
-        for k in range(1, 4):
-            other = lax.rem(net.z + k, 4)
-            ref = self.unit(part, other, 3, 1 - net.core)
-            pltpu.make_async_remote_copy(
-                src_ref=ref, dst_ref=ref, send_sem=self.sems.at[0, 5, part, other],
-                recv_sem=self.sems.at[1, 5, part, other], device_id=(net.dp, other), device_id_type=MESH).wait_recv()
-            value = value + self.g[other, 3, 1 - net.core, :, self.lanes(part)].astype(F32)
-        return value
+
+        @pl.when(net.z > 0)
+        def _():
+            self.z_arrived(part, net.z, False)
+
+        @pl.when(net.z < 3)
+        def _():
+            self.z_arrived(part, net.z, True)
+
+        return self.g[net.z, net.chip, net.core, :, self.lanes(part)].astype(F32)
 
     def drain(self):
         net = self.net
@@ -624,11 +656,7 @@
             def body(m, c, part=part):
                 for copy in self.across_copies(part, m) + self.side_copies(part, m):
                     copy.wait_send()
-
-                @pl.when(m != net.z)
-                def _():
-                    self.z_copy(part, m).wait_send()
-
+                self.each_z(part, m, lambda copy: copy.wait_send())
                 return c
 
             lax.fori_loop(0, 4, body, 0)
@@ -640,7 +668,7 @@
         pl.semaphore_signal(barrier, inc=1, device_id=(lax.rem(net.dp + other, 8), net.z), device_id_type=MESH)
     for k in range(1, 4):
         pl.semaphore_signal(barrier, inc=1, device_id=net.up(k), device_id_type=MESH)
-    pl.semaphore_wait(barrier, 10)
+    return barrier
 
 
 def share_gains(net, parts, send, recv):
@@ -682,7 +710,7 @@
         put(2 * j + 1, jnp.where(lanes, last, pltpu.roll(extra, 64, 1)))
     w[at[0], at[1], at[2], :, 768:1280] = g_ref[...].astype(BF16)
     w[at[0], at[1], at[2], :, 1280:1792] = u_ref[...].astype(BF16)
-    w[at[0], at[1], at[2], :, 1792:2304] = d_ref[...].T.astype(BF16)
+    w[at[0], at[1], at[2], :, 1792:2304] = d_ref[...].astype(BF16)
 
 
 def rows768(ref, m, lo, hi):
@@ -693,12 +721,77 @@
     ref[m, :, :, :, lo:hi] = value.reshape(4, 2, 96, hi - lo)
 
 
+class RowGather:
+    def __init__(self, net, pool, send, recv, ok):
+        self.net, self.pool, self.send, self.recv, self.ok = net, pool, send, recv, ok
+
+    def copy(self, m, way):
+        net = self.net
+        return pltpu.make_async_remote_copy(
+            src_ref=self.pool.at[m], dst_ref=self.pool.at[m], send_sem=self.send.at[way, m], recv_sem=self.recv.at[m],
+            device_id=net.along(1 - 2 * way), device_id_type=MESH)
+
+    def each(self, m, act):
+        net = self.net
+
+        @pl.when(jnp.logical_and(m <= net.z, net.z < 3))
+        def _():
+            act(self.copy(m, 0))
+
+        @pl.when(jnp.logical_and(m >= net.z, net.z > 0))
+        def _():
+            act(self.copy(m, 1))
+
+    def start(self):
+        net = self.net
+        if self.ok is not None:
+            for test, way in ((net.z < 3, 0), (net.z > 0, 1)):
+
+                @pl.when(test)
+                def _(way=way):
+                    pl.semaphore_signal(self.ok.at[1 - way], inc=1, device_id=net.along(1 - 2 * way), device_id_type=MESH)
+
+        for test, way in ((net.z < 3, 0), (net.z > 0, 1)):
+
+            @pl.when(test)
+            def _(way=way):
+                if self.ok is not None:
+                    pl.semaphore_wait(self.ok.at[way], 1)
+                self.copy(net.z, way).start()
+
+    def relay(self, i):
+        z = self.net.z
+        m = self.net.group(i)
+
+        @pl.when(jnp.logical_and(z > 0, z < 3))
+        def _():
+            self.copy(m, 0).wait_recv()
+            self.each(m, lambda copy: copy.start())
+
+    def arrived(self, i):
+        z = self.net.z
+        m = self.net.group(i)
+
+        @pl.when(jnp.logical_or(z == 0, z == 3))
+        def _():
+            self.copy(m, 0).wait_recv()
+
+        return m
+
+    def drain(self):
+        def body(m, c):
+            self.each(m, lambda copy: copy.wait_send())
+            return c
+
+        lax.fori_loop(0, 4, body, 0)
+
+
 def mega_kernel(
     len_ref, x_ref, dy_ref, q_ref, k_ref, v_ref, o_ref, gate_ref, up_ref, down_ref, ga_ref, gf_ref,
-    out_ref, gt_ref, gq_ref, gk_ref, gv_ref, go_ref, gate_grad_ref, up_grad_ref, down_grad_ref, gga_ref, ggf_ref, bins_ref,
-    w, g, slots, pool, gain, gain_parts, gg_out, gg_in, gg_z, bias, n1t, n2t, dypt, n_b, qkv, qkv_b, o_own, o_b, do, wo, lse, lse_t,
-    h, acc, res,
-    ag_send, ag_send_z, ag_recv, gn_send, gn_recv, in_sem, rs_sems, ok, gt_send, gt_recv, gt_ok, bin_sem, out_sem, gs_send,
+    out_ref, gt_ref, gq_ref, gk_ref, gv_ref, go_ref, gate_grad_ref, up_grad_ref, down_grad_ref, gga_ref, ggf_ref,
+    w, g, slots, pool, gain, gain_parts, gg_out, gg_in, gg_z, bias, n1t, n2t, dypt, n_b, qkv, hx, o_own, do, wo, lse, lse_t,
+    h, acc, res, zbuf,
+    ag_send, ag_recv, gn_send, gn_recv, in_sem, rs_sems, ok, gt_send, gt_recv, gt_ok, hx_send, hx_recv, out_sem, gs_send,
     gs_recv, gz_send, gz_recv,
 ):
     net = Net()
@@ -706,6 +799,7 @@
     seq = 1536
     me = net.z
     xp, dyp, n1, n2 = (pool.at[j] for j in range(4))
+    barrier = greet(net)
     halves = []
     for t, ref in enumerate((x_ref, dy_ref)):
         for j in range(2):
@@ -713,17 +807,18 @@
                 ref.at[j], g.at[t, :, :, :, 768 * j : 768 * (j + 1)], in_sem.at[2 * t + j]))
     for copy in halves:
         copy.start()
-    ag = Gather(net, w, ag_send, ag_send_z, ag_recv)
-    rs = Reduce(net, g, slots, rs_sems, ok)
+    ag = Gather(net, w, ag_send, ag_recv)
+    rs = Reduce(net, g, slots, zbuf, rs_sems, ok)
+    rows = RowGather(net, pool, gt_send, gt_recv, gt_ok)
+    mids = RowGather(net, hx, hx_send, hx_recv, None)
     build_package(w, net, q_ref, k_ref, v_ref, o_ref, gate_ref, up_ref, down_ref)
     pad = jnp.zeros((1, 32), F32)
     mine = jnp.concatenate([
         jnp.concatenate([ga_ref[...], pad], axis=1), jnp.concatenate([gf_ref[...], pad], axis=1),
         jnp.zeros((6, 128), F32)], axis=0)
     gain_parts[net.dp] = mine.astype(BF16).astype(F32)
-    greet(net)
+    pl.semaphore_wait(barrier, 10)
     gain_copies = share_gains(net, gain_parts, gn_send, gn_recv)
-    ag.along_z(0)
     ag.spread(0, 0)
 
     place = placement(len_ref, bins)
@@ -734,85 +829,63 @@
         _, segment_row = packed_source(place, b * CAP, (1, CAP), 1)
         bias[...] = jnp.where(segment == segment_row, 0.0, NEG)
 
-    def picks(b):
-        source, _ = packed_source(place, b * CAP, (CAP, 1), 0)
-        return (source == lax.broadcasted_iota(jnp.int32, (CAP, seq), 1)).astype(BF16)
-
-    def packed(pick, t):
-        return nn(pick[:, 0:768], rows768(g, t, 0, 768)) + nn(pick[:, 768:1536], rows768(g, t, 768, 1536))
-
-    def drops(b, first, count):
-        source, _ = packed_source(place, b * CAP, (1, CAP), 1)
-        return (lax.broadcasted_iota(jnp.int32, (count, CAP), 0) + first == source).astype(BF16)
-
-    def unpack(b, value):
+    def pack(b, t, store):
         def body(j, c):
-            at = pl.ds(pl.multiple_of(j * 256, 256), 256)
-            out_ref[at, :] = (out_ref[at, :].astype(F32) + nn(drops(b, j * 256, 256), value)).astype(BF16)
+            source, _ = packed_source(place, b * CAP + j * 128, (128, 1), 0)
+            pick = (source == lax.broadcasted_iota(jnp.int32, (128, seq), 1)).astype(BF16)
+            value = nn(pick[:, 0:768], rows768(g, t, 0, 768)) + nn(pick[:, 768:1536], rows768(g, t, 768, 1536))
+            store(pl.ds(pl.multiple_of(j * 128, 128), 128), value)
             return c
 
-        lax.fori_loop(0, seq // 256, body, 0)
+        lax.fori_loop(0, CAP // 128, body, 0)
+
+    def drops(b, first, rows, count=1):
+        source, _ = packed_source(place, b * CAP, (1, count * CAP), 1)
+        return (lax.broadcasted_iota(jnp.int32, (rows, count * CAP), 0) + first == source).astype(BF16)
+
+    def norm(src, dst, gain_row):
+        def body(j, c):
+            at = pl.ds(pl.multiple_of(j * 128, 128), 128)
+            values = src[at, :]
+            dst[at, :] = (values * rms_rows(values) * gain_row).astype(BF16)
+            return c
+
+        lax.fori_loop(0, CAP // 128, body, 0)
 
     for copy in halves:
         copy.wait()
-    pick = picks(me)
-    xb = packed(pick, 0)
-    xp[...] = xb.astype(BF16)
-    h[...] = xb
-    dyp[...] = packed(pick, 1).astype(BF16)
-    set_bias(me)
-    dypt[...] = dyp[...].T
+    def store_x(at, value):
+        xp[at, :] = value.astype(BF16)
+        h[at, :] = value
+
+    def store_dy(at, value):
+        dyp[at, :] = value.astype(BF16)
+
+    pack(me, 0, store_x)
     ag.spread(0, 1)
     ag.relay(0, 0)
+    pack(me, 1, store_dy)
     join_gains(net, gain_parts, gn_send, gn_recv, gain)
     g1 = gain[0:1, :]
     g2 = gain[1:2, :]
-    xb = h[...]
-    n1[...] = (xb * rms_rows(xb) * g1).astype(BF16)
+    ag.spread(0, 2)
+    ag.relay(0, 1)
+    ag.across(0, 0)
+    norm(h, n1, g1)
     n1t[...] = n1[...].T
-    ag.spread(0, 2)
-    ag.across(0, 0)
-    ag.relay(0, 1)
+    dypt[...] = dyp[...].T
+
+    set_bias(me)
     ag.spread(0, 3)
-
-    def bin_copy(k, up):
-        there = bins_ref.at[k]
-        return pltpu.make_async_copy(qkv_b.at[0], there, bin_sem) if up else pltpu.make_async_copy(there, qkv_b.at[0], bin_sem)
-
-    def pack_others(k, c):
-        b = lax.rem(me + 1 + k, bins)
-        qkv_b[0] = packed(picks(b), 0).astype(BF16)
-        copy = bin_copy(k, True)
-        copy.start()
-        copy.wait()
-        return c
-
-    lax.fori_loop(0, 3, pack_others, 0)
+    ag.relay(0, 2)
+    ag.across(0, 1)
+    ag.relay(0, 3)
+    ag.across(0, 2)
+    ag.spread(1, 0)
+    ag.across(0, 3)
 
     def own_forward(i, c):
         m = net.group(i)
-
-        @pl.when(i == 0)
-        def _():
-            ag.across(0, 1)
-            ag.relay(0, 2)
-
-        @pl.when(i == 1)
-        def _():
-            ag.across(0, 2)
-            ag.relay(0, 3)
-            ag.along_z(1)
-            ag.spread(1, 0)
-
-        @pl.when(i == 2)
-        def _():
-            ag.across(0, 3)
-            ag.spread(1, 1)
-
-        @pl.when(i == 3)
-        def _():
-            ag.relay(1, 0)
-
         ag.complete(0, i)
         first, second = out_weight_tiles_at(w, m)
         wo[m, :, 0:128] = first
@@ -820,36 +893,49 @@
         qkv[m] = nn(n1[...], rows768(w, m, 0, 768)).astype(BF16)
         attend_group(qkv, m, bias, o_own, m, lse)
         h[...] += nt(o_own[m], wo[m])
+
+        @pl.when(i == 1)
+        def _():
+            ag.spread(1, 1)
+            ag.relay(1, 0)
+
         return c
 
     lax.fori_loop(0, 4, own_forward, 0)
-    def norm(dst, gain_row):
-        def body(j, c):
-            at = pl.ds(pl.multiple_of(j * 128, 128), 128)
-            rows = h[at, :]
-            dst[at, :] = (rows * rms_rows(rows) * gain_row).astype(BF16)
-            return c
-
-        lax.fori_loop(0, CAP // 128, body, 0)
-
-    norm(n2, g2)
+    hx[me] = h[...].astype(BF16)
+    mids.start()
+    norm(h, n2, g2)
     n2t[...] = n2[...].T
     lse_t[...] = lse[...].T
     acc[...] = jnp.zeros_like(acc)
     res[...] = h[...]
 
     def ffn_back(i, c):
+        @pl.when(i == 0)
+        def _():
+            ag.spread(1, 2)
+            ag.relay(1, 1)
+            ag.across(1, 0)
+
+        @pl.when(i == 1)
+        def _():
+            ag.spread(1, 3)
+            ag.relay(1, 2)
+            ag.across(1, 1)
+
+        @pl.when(i == 2)
+        def _():
+            ag.relay(1, 3)
+            ag.across(1, 2)
+
+            mids.relay(1)
+
+        @pl.when(i == 3)
+        def _():
+            ag.across(1, 3)
+            mids.relay(2)
+
         m = net.group(i)
-        ag.across(1, i)
-
-        @pl.when(i < 3)
-        def _():
-            ag.relay(1, i + 1)
-
-        @pl.when(i < 2)
-        def _():
-            ag.spread(1, i + 2)
-
         ag.complete(1, i)
         for lo in (0, 256):
             w_gate = rows768(w, m, 768 + lo, 1024 + lo)
@@ -889,40 +975,38 @@
         return c
 
     lax.fori_loop(0, 4, ffn_back, 0)
-    out_ref[...] = jnp.zeros_like(out_ref)
-    unpack(me, res[...].astype(BF16))
+    rs.start_across(1, 0)
+    rs.start_across(1, 1)
+    rs.start_across(1, 2)
+
     def hidden_back(j, total):
         at = pl.ds(pl.multiple_of(j * 128, 128), 128)
-        hb = h[at, :]
-        r2 = rms_rows(hb)
+        ho = h[at, :]
+        r2 = rms_rows(ho)
         dn2 = acc[at, :]
         wg = dn2 * g2
-        dh = dyp[at, :].astype(F32) + r2 * wg - hb * (r2 * r2 * r2) * jnp.mean(wg * hb, axis=1, keepdims=True)
+        dh = dyp[at, :].astype(F32) + r2 * wg - ho * (r2 * r2 * r2) * jnp.mean(wg * ho, axis=1, keepdims=True)
         h[at, :] = dh
         n2[at, :] = dh.astype(BF16)
         acc[at, :] = jnp.zeros_like(dh)
-        return total + jnp.sum(dn2 * hb * r2, axis=0, keepdims=True)
+        return total + jnp.sum(dn2 * ho * r2, axis=0, keepdims=True)
 
     gg_ffn = lax.fori_loop(0, CAP // 128, hidden_back, jnp.zeros((1, 768), F32))
     n2t[...] = n2[...].T
     rs.from_core(1, 3, (0, 1))
-    rs.start_across(1, 0)
+    rs.start_across(1, 3)
+    mids.relay(3)
 
     def attn_back(i, c):
         m = net.group(i)
         do[0] = nn(n2[...], wo[m]).astype(BF16)
         attend_group_back(qkv, m, bias, lse_t, do, 0, qkv)
         acc[...] += nt(qkv[m], rows768(w, m, 0, 768))
-
         rs.start_sides(1, i)
-
-        @pl.when(i < 3)
-        def _():
-            rs.start_across(1, i + 1)
-
         return c
 
     lax.fori_loop(0, 4, attn_back, 0)
+
     def input_back(j, total):
         at = pl.ds(pl.multiple_of(j * 128, 128), 128)
         xb = xp[at, :].astype(F32)
@@ -935,15 +1019,7 @@
 
     gg_attn = lax.fori_loop(0, CAP // 128, input_back, jnp.zeros((1, 768), F32))
     pool[me] = n_b[...]
-    for k in range(1, 4):
-        pl.semaphore_signal(gt_ok.at[me], inc=1, device_id=net.up(k), device_id_type=MESH)
-    gt_copies = []
-    for k in range(1, 4):
-        pl.semaphore_wait(gt_ok.at[lax.rem(me + k, 4)], 1)
-        gt_copies.append(pltpu.make_async_remote_copy(
-            src_ref=pool.at[me], dst_ref=pool.at[me], send_sem=gt_send.at[k - 1], recv_sem=gt_recv.at[me],
-            device_id=net.up(k), device_id_type=MESH))
-        gt_copies[-1].start()
+    rows.start()
     gg = jnp.concatenate([gg_attn, gg_ffn, jnp.zeros((6, 768), F32)], axis=0)
     for d in range(8):
         gg_out[d] = pltpu.roll(gg, (768 - 96 * d) % 768, 1)[:, 0:128] if d else gg[:, 0:128]
@@ -984,6 +1060,8 @@
 
     lax.fori_loop(0, 4, attn_grads, 0)
     rs.from_core(0, 3, None)
+    for i in range(4):
+        rs.start_across(0, i)
 
     part = gg_out[net.dp]
     for k in range(1, 8):
@@ -999,88 +1077,80 @@
     for copy in gz_copies:
         copy.start()
 
-    def others(k, c):
-        b = lax.rem(me + 1 + k, bins)
-        copy = bin_copy(k, False)
-        copy.start()
-        set_bias(b)
-        copy.wait()
-        h[...] = qkv_b[0].astype(F32)
-        norm(n_b, g1)
-
-        def attend(m, c):
-            qkv_b[0] = nn(n_b[...], rows768(w, m, 0, 768)).astype(BF16)
-            attend_group(qkv_b, 0, bias, o_b, 0)
-            h[...] += nt(o_b[0], wo[m])
-
-            @pl.when(jnp.logical_and(k == 0, m == 0))
-            def _():
-                rs.start_z(1, 0)
-
-            @pl.when(jnp.logical_and(k == 0, m == 1))
-            def _():
-                rs.start_z(1, 1)
-
-            @pl.when(jnp.logical_and(k == 0, m == 2))
-            def _():
-                rs.start_across(0, 0)
-                rs.start_across(0, 1)
-                rs.start_z(1, 2)
-
-            @pl.when(jnp.logical_and(k == 0, m == 3))
-            def _():
-                rs.start_sides(0, 0)
-                rs.start_sides(0, 1)
-                rs.start_z(1, 3)
-
-            @pl.when(jnp.logical_and(k == 1, m == 0))
-            def _():
-                rs.start_across(0, 2)
-                rs.start_across(0, 3)
-                rs.start_z(0, 0)
-
-            @pl.when(jnp.logical_and(k == 1, m == 1))
-            def _():
-                rs.start_sides(0, 2)
-                rs.start_sides(0, 3)
-                rs.start_z(0, 1)
-
-            @pl.when(jnp.logical_and(k == 1, m == 3))
-            def _():
-                rs.start_z(0, 2)
-                rs.start_z(0, 3)
-
-            return c
-
-        lax.fori_loop(0, 4, attend, 0)
-        norm(n_b, g2)
+    rs.gather_sides(1, 0)
+    rs.gather_sides(1, 1)
+    mids.drain()
+    hx[me] = res[...].astype(BF16)
+
+    def ffn_out(j, c):
+        b = mids.arrived(j)
+        acc[...] = hx[b].astype(F32)
+        norm(acc, n_b, g2)
 
         def ffn(m, c):
             a = nn(n_b[...], rows768(w, m, 768, 1280))
             up = nn(n_b[...], rows768(w, m, 1280, 1792))
             u = (0.5 * a * (1.0 + gelu_parts(a)) * up).astype(BF16)
-            h[...] += nt(u, rows768(w, m, 1792, 2304))
+            acc[...] += nt(u, rows768(w, m, 1792, 2304))
             return c
 
         lax.fori_loop(0, 4, ffn, 0)
-        unpack(b, h[...].astype(BF16))
+        hx[b] = acc[...].astype(BF16)
+
+        @pl.when(j == 1)
+        def _():
+            rows.relay(1)
+            rows.relay(2)
+            rs.start_sides(0, 0)
+            rs.start_sides(0, 1)
+            rs.gather_sides(1, 2)
+            rs.gather_sides(1, 3)
+            rs.start_z(1, 0)
+            rs.start_z(1, 1)
+
+        @pl.when(j == 2)
+        def _():
+            rs.start_sides(0, 2)
+            rs.start_sides(0, 3)
+            rs.start_z(1, 2)
+            rs.start_z(1, 3)
+            rows.relay(3)
+
         return c
 
-    lax.fori_loop(0, 3, others, 0)
-
-    rows = (h, acc, res)
-    for j in range(3):
-        rows[j][...] = nn(drops(me, CAP * j, CAP), pool[me])
-    for k in (1, 3, 2):
-        other = lax.rem(me + k, 4)
-        pltpu.make_async_remote_copy(
-            src_ref=pool.at[other], dst_ref=pool.at[other], send_sem=gt_send.at[k - 1], recv_sem=gt_recv.at[other],
-            device_id=net.up(k), device_id_type=MESH).wait_recv()
-        for j in range(3):
-            rows[j][...] += nn(drops(other, CAP * j, CAP), pool[other])
-    outs = [pltpu.make_async_copy(rows[j], gt_ref.at[j], out_sem.at[j]) for j in range(3)]
-    for copy in outs:
-        copy.start()
+    lax.fori_loop(1, 4, ffn_out, 0)
+
+    def place_out(j, c):
+        at = pl.ds(pl.multiple_of(j * 256, 256), 256)
+        pick = drops(0, j * 256, 256, 4)
+        value = nn(pick[:, 0:CAP], hx[0])
+        for b in range(1, 4):
+            value = value + nn(pick[:, b * CAP : (b + 1) * CAP], hx[b])
+        out_ref[at, :] = value.astype(BF16)
+        return c
+
+    lax.fori_loop(0, seq // 256, place_out, 0)
+    for i in range(4):
+        rs.gather_sides(0, i)
+    for m in range(4):
+        rs.start_z(0, m)
+
+    def place_rows(bs, first):
+        def body(j, c):
+            value = nn(drops(bs[0], CAP * j, CAP), pool[bs[0]])
+            for b in bs[1:]:
+                value = value + nn(drops(b, CAP * j, CAP), pool[b])
+            if not first:
+                value = value + qkv[j].astype(F32)
+            qkv[j] = value.astype(BF16)
+            return c
+
+        lax.fori_loop(0, 3, body, 0)
+
+    place_rows([me, rows.arrived(1), rows.arrived(2)], True)
+    place_rows([rows.arrived(3)], False)
+    out = pltpu.make_async_copy(qkv.at[0:3], gt_ref, out_sem)
+    out.start()
 
     for k in range(1, 4):
         other = lax.rem(me + k, 4)
@@ -1093,20 +1163,31 @@
     ffn_sum = rs.total(1)
     gate_grad_ref[...] = ffn_sum[:, 0:512]
     up_grad_ref[...] = ffn_sum[:, 512:1024]
-    down_grad_ref[...] = ffn_sum[:, 1024:1536].T
+    down_grad_ref[...] = ffn_sum[:, 1024:1536]
     attn_sum = rs.total(0)
     gq_ref[...] = attn_sum[:, 0:192]
     gk_ref[...] = attn_sum[:, 256:448]
     gv_ref[...] = attn_sum[:, 512:704]
     go_ref[...] = jnp.concatenate([attn_sum[:, 192:256], attn_sum[:, 448:512], attn_sum[:, 704:768]], axis=1).T
-    for copy in outs:
-        copy.wait()
-    for copy in gain_copies + gt_copies + gz_copies:
+    out.wait()
+    for copy in gain_copies + gz_copies:
         copy.wait_send()
     for k in range(1, 8):
         gg_copy(k).wait_send()
+    rows.drain()
     rs.drain()
     ag.drain()
+
+
+def finish_kernel(*refs):
+    count = len(refs) // 2
+    refs[count][...] = refs[0][...].astype(F32)
+    refs[count + 1][...] = refs[1][...]
+
+    @pl.when(pl.program_id(0) == 0)
+    def _():
+        for j in range(2, count):
+            refs[count + j][...] = refs[j][...]
 
 
 def out_weight_tiles_at(w, m):
@@ -1135,14 +1216,14 @@
     def f32(*shape):
         return jax.ShapeDtypeStruct(shape, F32)
 
-    out, gt, gq, gk, gv, go, gate, up, down, gain_a, gain_f, _ = pl.pallas_call(
+    out, gt, gq, gk, gv, go, gate, up, down, gain_a, gain_f = pl.pallas_call(
         mega_kernel,
         out_shape=(
-            jax.ShapeDtypeStruct((seq, width), BF16), f32(3, CAP, width), f32(96, 192), f32(96, 192), f32(96, 192), f32(192, 96),
-            f32(96, 512), f32(96, 512), f32(512, 96), f32(1, 96), f32(1, 96), jax.ShapeDtypeStruct((3, CAP, width), BF16),
+            jax.ShapeDtypeStruct((seq, width), BF16), jax.ShapeDtypeStruct((3, CAP, width), BF16),
+            f32(96, 192), f32(96, 192), f32(96, 192), f32(192, 96), f32(96, 512), f32(96, 512), f32(96, 512), f32(1, 96), f32(1, 96),
         ),
         in_specs=[smem, hbm, hbm] + [vmem] * 9,
-        out_specs=[vmem, hbm] + [vmem] * 9 + [hbm],
+        out_specs=[vmem, hbm] + [vmem] * 9,
         scratch_shapes=[
             pltpu.VMEM((4, 4, 2, 96, 2304), BF16),
             pltpu.VMEM((4, 4, 2, 96, 2304), BF16),
@@ -1154,25 +1235,36 @@
             pltpu.VMEM((CAP, CAP), F32),
             act_t, act_t, act_t, act,
             pltpu.VMEM((4, CAP, width), BF16),
-            pltpu.VMEM((1, CAP, width), BF16),
+            pltpu.VMEM((4, CAP, width), BF16),
             pltpu.VMEM((4, CAP, 256), BF16),
-            pltpu.VMEM((1, CAP, 256), BF16),
             pltpu.VMEM((1, CAP, 256), BF16),
             pltpu.VMEM((4, width, 256), BF16),
             pltpu.VMEM((CAP, 128), F32),
             pltpu.VMEM((128, CAP), F32),
             wide, wide, wide,
-            dma((2, 4, 4, 3)), dma((2, 3)), dma((2, 4, 4, 2)), dma((7,)), dma((8,)), dma((4,)),
-            dma((2, 6, 2, 4)), pltpu.SemaphoreType.REGULAR((4, 2, 4)),
-            dma((3,)), dma((4,)), pltpu.SemaphoreType.REGULAR((4,)), dma, dma((3,)), dma((7,)), dma((8,)), dma((3,)), dma((4,)),
+            pltpu.VMEM((96, 2304), BF16),
+            dma((2, 4, 4, 5)), dma((2, 4, 4, 2, 3)), dma((7,)), dma((8,)), dma((4,)),
+            dma((2, 7, 2, 4)), pltpu.SemaphoreType.REGULAR((4, 2, 4)),
+            dma((2, 4)), dma((4,)), pltpu.SemaphoreType.REGULAR((2,)), dma((2, 4)), dma((4,)), dma, dma((7,)), dma((8,)), dma((3,)), dma((4,)),
         ],
         compiler_params=pltpu.CompilerParams(
             vmem_limit_bytes=60 * 2**20, collective_id=0, has_side_effects=True),
         name="layer",
     )(lengths, tokens.reshape(2, 4, 2, 96, width), cotangent.reshape(2, 4, 2, 96, width), query_weight, key_weight,
-      value_weight, out_weight, gate_weight, up_weight, down_weight, attn_gain.reshape(1, 96), ffn_gain.reshape(1, 96))
+      value_weight, out_weight, gate_weight, up_weight, down_weight.T, attn_gain.reshape(1, 96), ffn_gain.reshape(1, 96))
+    rest = (out, gq, gk, gv, go, gate, up, down, gain_a, gain_f)
+    block = pl.BlockSpec((256, width), lambda i: (i, 0))
+    whole = [pl.BlockSpec(a.shape, lambda i: (0, 0)) for a in rest[1:]]
+    gt, out, gq, gk, gv, go, gate, up, down, gain_a, gain_f = pl.pallas_call(
+        finish_kernel,
+        grid=(seq // 256,),
+        out_shape=(f32(seq, width),) + tuple(jax.ShapeDtypeStruct(a.shape, a.dtype) for a in rest),
+        in_specs=[block, block] + whole,
+        out_specs=(block, block) + tuple(whole),
+        name="finish",
+    )(gt.reshape(seq, width), *rest)
     return (
-        out.reshape(rows, seq, width), gt.reshape(rows, seq, width), gq, gk, gv, go, gain_a.reshape(96), gate, up, down,
+        out.reshape(rows, seq, width), gt.reshape(rows, seq, width), gq, gk, gv, go, gain_a.reshape(96), gate, up, down.T,
         gain_f.reshape(96),
     )
 def solution(mesh):

time: 277 us -> 229 us (0.83)
  the two profiles are of different devices: /device:TPU:0 before, /device:TPU:16 now
where the time goes in v4:
time: 229 us
  Pallas kernels  228 us (100%)
    pallas_call x1, Pallas kernels, on_this_slice(): pl.pallas_call(mega_kernel, out_shape=(jax.ShapeDtypeStruct((seq, width),...  221 us
    pallas_call x1, Pallas kernels, on_this_slice(): pl.pallas_call(finish_kernel, grid=(seq // 256,), out_shape=(f32(seq, wid...  7.13 us

profile of v4, /device:TPU:16, one launch (start us, length us, event | category | flops | bytes accessed | tf_op | source)
XLA Modules:
  0.0 228.7 jit_solution(12397052521494689561)
XLA Ops:
  0.6 220.7 %layer.1 = (bf16[1536,768]{1,0:T(8,128)(2,1)}, bf16[3,512,768]{2,1,0:T(8,128)(2,1)}, f32[96,192]{1,0:T(8,128)}, f32[96,192]{1,0:T(8,128)}, f32[96,192]{1,0:T(8,1...) custom-call(s32[1,8]{1,0:T(1,128)} %len_ref.1, ...), custom_call_target="tpu_custom_call" | custom-call | tf_op jit(solution)/shard_map/layer/pallas_call | solution.py:1219
  221.4 7.1 %finish.1 = (f32[1536,768]{1,0:T(8,128)}, bf16[1536,768]{1,0:T(8,128)(2,1)}, f32[96,192]{1,0:T(8,128)}, f32[96,192]{1,0:T(8,128)}, f32[96,192]{1,0:T(8,128)}, /*...) custom-call(bf16[1536,768]{1,0:T(8,128)(2,1)} %bitcast.13, ...), custom_call_target="tpu_custom_call" | custom-call | tf_op jit(solution)/shard_map/finish/pallas_call | solution.py:1258

commit v5 on v4

--- a/solution.py
+++ b/solution.py
@@ -449,14 +449,20 @@
             self.copy(part, m, net.chip_x, net.core, 0, net.y, 0), self.copy(part, m, net.chip_x, net.core, 2, net.sibling),
             self.copy(part, m, net.chip_y, net.core, 1, net.x, 1), self.copy(part, m, net.chip_y, net.core, 2, net.sibling)]
 
-    def spread(self, part, i):
+    def along_z(self, part, i):
         net = self.net
         m = net.group(i)
         if not isinstance(i, int) or i > 0:
             self.wait(part, m, net.chip, net.core)
         self.each_along_z(part, m, lambda copy: copy.start())
-        for copy in self.own_copies(part, m):
+
+    def sideways(self, part, i):
+        for copy in self.own_copies(part, self.net.group(i)):
             copy.start()
+
+    def spread(self, part, i):
+        self.along_z(part, i)
+        self.sideways(part, i)
 
     def relay(self, part, i):
         net = self.net
@@ -622,19 +628,32 @@
             copy.wait_recv()
             self.add(part, m, net.chip, slot)
 
-    def start_z(self, part, m):
-        net = self.net
-        z = net.z
-
-        @pl.when(jnp.logical_or(jnp.logical_and(m > z, z > 0), jnp.logical_and(m < z, z < 3)))
-        def _():
-            self.z_arrived(part, m, False)
-
-        @pl.when(m != z)
-        def _():
-            pl.semaphore_wait(self.ok.at[2, part, m], 1)
-
+    def send_z(self, part, m):
+        pl.semaphore_wait(self.ok.at[2, part, m], 1)
         self.each_z(part, m, lambda copy: copy.start())
+
+    def pass_z(self, part, m):
+        self.z_arrived(part, m, False)
+        self.send_z(part, m)
+
+    def wave(self, part, n):
+        z = self.net.z
+        for at, groups, act in (
+            ((0, (3, 2, 1), self.send_z), (3, (0, 1, 2), self.send_z)),
+            ((1, (3, 2), self.pass_z), (2, (0, 1), self.pass_z)),
+            ((1, (0,), self.pass_z), (2, (3,), self.pass_z)),
+        )[n]:
+
+            @pl.when(z == at)
+            def _(groups=groups, act=act):
+                for m in groups:
+                    act(part, m)
+
+    def step(self, n):
+        if n > 0:
+            self.start_sides(1 if n < 5 else 0, (n - 1) % 4)
+        if n < 8:
+            self.start_across(1 if n < 4 else 0, n % 4)
 
     def total(self, part):
         net = self.net
@@ -789,7 +808,7 @@
 def mega_kernel(
     len_ref, x_ref, dy_ref, q_ref, k_ref, v_ref, o_ref, gate_ref, up_ref, down_ref, ga_ref, gf_ref,
     out_ref, gt_ref, gq_ref, gk_ref, gv_ref, go_ref, gate_grad_ref, up_grad_ref, down_grad_ref, gga_ref, ggf_ref,
-    w, g, slots, pool, gain, gain_parts, gg_out, gg_in, gg_z, bias, n1t, n2t, dypt, n_b, qkv, hx, o_own, do, wo, lse, lse_t,
+    w, g, slots, pool, gain, gain_parts, gg_out, gg_in, gg_z, bias, n1t, n2t, dypt, spare, qkv, hx, o_own, wo, lse, lse_t,
     h, acc, res, zbuf,
     ag_send, ag_recv, gn_send, gn_recv, in_sem, rs_sems, ok, gt_send, gt_recv, gt_ok, hx_send, hx_recv, out_sem, gs_send,
     gs_recv, gz_send, gz_recv,
@@ -799,6 +818,7 @@
     seq = 1536
     me = net.z
     xp, dyp, n1, n2 = (pool.at[j] for j in range(4))
+    n_b = spare.at[0]
     barrier = greet(net)
     halves = []
     for t, ref in enumerate((x_ref, dy_ref)):
@@ -879,10 +899,13 @@
     ag.spread(0, 3)
     ag.relay(0, 2)
     ag.across(0, 1)
+    ag.along_z(1, 0)
     ag.relay(0, 3)
     ag.across(0, 2)
-    ag.spread(1, 0)
+    ag.sideways(1, 0)
     ag.across(0, 3)
+    ag.along_z(1, 1)
+    ag.sideways(1, 1)
 
     def own_forward(i, c):
         m = net.group(i)
@@ -894,10 +917,21 @@
         attend_group(qkv, m, bias, o_own, m, lse)
         h[...] += nt(o_own[m], wo[m])
 
+        @pl.when(i == 0)
+        def _():
+            ag.along_z(1, 2)
+
         @pl.when(i == 1)
         def _():
-            ag.spread(1, 1)
             ag.relay(1, 0)
+            ag.sideways(1, 2)
+
+        @pl.when(i == 3)
+        def _():
+            ag.along_z(1, 3)
+            ag.relay(1, 1)
+            ag.across(1, 0)
+            ag.sideways(1, 3)
 
         return c
 
@@ -906,20 +940,13 @@
     mids.start()
     norm(h, n2, g2)
     n2t[...] = n2[...].T
-    lse_t[...] = lse[...].T
+    lse_t[...] = lse[...].T[0:16, :]
     acc[...] = jnp.zeros_like(acc)
     res[...] = h[...]
 
     def ffn_back(i, c):
-        @pl.when(i == 0)
-        def _():
-            ag.spread(1, 2)
-            ag.relay(1, 1)
-            ag.across(1, 0)
-
         @pl.when(i == 1)
         def _():
-            ag.spread(1, 3)
             ag.relay(1, 2)
             ag.across(1, 1)
 
@@ -927,16 +954,20 @@
         def _():
             ag.relay(1, 3)
             ag.across(1, 2)
-
             mids.relay(1)
+            mids.relay(2)
 
         @pl.when(i == 3)
         def _():
             ag.across(1, 3)
-            mids.relay(2)
 
         m = net.group(i)
         ag.complete(1, i)
+
+        @pl.when(i == 3)
+        def _():
+            rs.step(0)
+
         for lo in (0, 256):
             w_gate = rows768(w, m, 768 + lo, 1024 + lo)
             w_up = rows768(w, m, 1280 + lo, 1536 + lo)
@@ -975,9 +1006,7 @@
         return c
 
     lax.fori_loop(0, 4, ffn_back, 0)
-    rs.start_across(1, 0)
-    rs.start_across(1, 1)
-    rs.start_across(1, 2)
+    rs.step(1)
 
     def hidden_back(j, total):
         at = pl.ds(pl.multiple_of(j * 128, 128), 128)
@@ -994,15 +1023,25 @@
     gg_ffn = lax.fori_loop(0, CAP // 128, hidden_back, jnp.zeros((1, 768), F32))
     n2t[...] = n2[...].T
     rs.from_core(1, 3, (0, 1))
-    rs.start_across(1, 3)
-    mids.relay(3)
 
     def attn_back(i, c):
         m = net.group(i)
-        do[0] = nn(n2[...], wo[m]).astype(BF16)
-        attend_group_back(qkv, m, bias, lse_t, do, 0, qkv)
+        spare[0, :, 0:256] = nn(n2[...], wo[m]).astype(BF16)
+        attend_group_back(qkv, m, bias, lse_t, spare, 0, qkv)
         acc[...] += nt(qkv[m], rows768(w, m, 0, 768))
-        rs.start_sides(1, i)
+
+        @pl.when(i == 0)
+        def _():
+            mids.relay(3)
+
+        @pl.when(i == 1)
+        def _():
+            rs.step(2)
+
+        @pl.when(i == 2)
+        def _():
+            rs.gather_sides(1, 0)
+
         return c
 
     lax.fori_loop(0, 4, attn_back, 0)
@@ -1020,6 +1059,7 @@
     gg_attn = lax.fori_loop(0, CAP // 128, input_back, jnp.zeros((1, 768), F32))
     pool[me] = n_b[...]
     rows.start()
+    rs.step(3)
     gg = jnp.concatenate([gg_attn, gg_ffn, jnp.zeros((6, 768), F32)], axis=0)
     for d in range(8):
         gg_out[d] = pltpu.roll(gg, (768 - 96 * d) % 768, 1)[:, 0:128] if d else gg[:, 0:128]
@@ -1055,13 +1095,13 @@
         @pl.when(i == 3)
         def _():
             rs.from_core(0, 2, None)
+            rs.gather_sides(1, 1)
 
         return c
 
     lax.fori_loop(0, 4, attn_grads, 0)
     rs.from_core(0, 3, None)
-    for i in range(4):
-        rs.start_across(0, i)
+    rs.step(4)
 
     part = gg_out[net.dp]
     for k in range(1, 8):
@@ -1077,8 +1117,6 @@
     for copy in gz_copies:
         copy.start()
 
-    rs.gather_sides(1, 0)
-    rs.gather_sides(1, 1)
     mids.drain()
     hx[me] = res[...].astype(BF16)
 
@@ -1092,29 +1130,31 @@
             up = nn(n_b[...], rows768(w, m, 1280, 1792))
             u = (0.5 * a * (1.0 + gelu_parts(a)) * up).astype(BF16)
             acc[...] += nt(u, rows768(w, m, 1792, 2304))
+
+            @pl.when(jnp.logical_and(j == 2, m == 1))
+            def _():
+                rs.step(5)
+                rs.gather_sides(1, 2)
+                rs.gather_sides(1, 3)
+
+            @pl.when(jnp.logical_and(j == 3, m == 1))
+            def _():
+                rs.step(6)
+
             return c
 
         lax.fori_loop(0, 4, ffn, 0)
         hx[b] = acc[...].astype(BF16)
 
-        @pl.when(j == 1)
+        @pl.when(j == 2)
         def _():
             rows.relay(1)
             rows.relay(2)
-            rs.start_sides(0, 0)
-            rs.start_sides(0, 1)
-            rs.gather_sides(1, 2)
-            rs.gather_sides(1, 3)
-            rs.start_z(1, 0)
-            rs.start_z(1, 1)
-
-        @pl.when(j == 2)
-        def _():
-            rs.start_sides(0, 2)
-            rs.start_sides(0, 3)
-            rs.start_z(1, 2)
-            rs.start_z(1, 3)
-            rows.relay(3)
+            rs.wave(1, 0)
+
+        @pl.when(j == 3)
+        def _():
+            rs.step(7)
 
         return c
 
@@ -1130,10 +1170,11 @@
         return c
 
     lax.fori_loop(0, seq // 256, place_out, 0)
-    for i in range(4):
+    rs.step(8)
+    rows.relay(3)
+    rs.wave(1, 1)
+    for i in range(3):
         rs.gather_sides(0, i)
-    for m in range(4):
-        rs.start_z(0, m)
 
     def place_rows(bs, first):
         def body(j, c):
@@ -1148,6 +1189,15 @@
         lax.fori_loop(0, 3, body, 0)
 
     place_rows([me, rows.arrived(1), rows.arrived(2)], True)
+    rs.gather_sides(0, 3)
+    rs.wave(0, 0)
+    rs.wave(1, 2)
+    rs.wave(0, 1)
+    ffn_sum = rs.total(1)
+    gate_grad_ref[...] = ffn_sum[:, 0:512]
+    up_grad_ref[...] = ffn_sum[:, 512:1024]
+    down_grad_ref[...] = ffn_sum[:, 1024:1536]
+    rs.wave(0, 2)
     place_rows([rows.arrived(3)], False)
     out = pltpu.make_async_copy(qkv.at[0:3], gt_ref, out_sem)
     out.start()
@@ -1160,10 +1210,6 @@
         part = part + gg_z[other]
     gga_ref[...] = part[0:1, 0:96]
     ggf_ref[...] = part[1:2, 0:96]
-    ffn_sum = rs.total(1)
-    gate_grad_ref[...] = ffn_sum[:, 0:512]
-    up_grad_ref[...] = ffn_sum[:, 512:1024]
-    down_grad_ref[...] = ffn_sum[:, 1024:1536]
     attn_sum = rs.total(0)
     gq_ref[...] = attn_sum[:, 0:192]
     gk_ref[...] = attn_sum[:, 256:448]
@@ -1233,14 +1279,13 @@
             pltpu.VMEM((8, 8, 128), F32), pltpu.VMEM((8, 8, 128), F32), pltpu.VMEM((8, 8, 128), F32),
             pltpu.VMEM((4, 8, 128), F32),
             pltpu.VMEM((CAP, CAP), F32),
-            act_t, act_t, act_t, act,
+            act_t, act_t, act_t, pltpu.VMEM((1, CAP, width), BF16),
             pltpu.VMEM((4, CAP, width), BF16),
             pltpu.VMEM((4, CAP, width), BF16),
             pltpu.VMEM((4, CAP, 256), BF16),
-            pltpu.VMEM((1, CAP, 256), BF16),
             pltpu.VMEM((4, width, 256), BF16),
             pltpu.VMEM((CAP, 128), F32),
-            pltpu.VMEM((128, CAP), F32),
+            pltpu.VMEM((16, CAP), F32),
             wide, wide, wide,
             pltpu.VMEM((96, 2304), BF16),
             dma((2, 4, 4, 5)), dma((2, 4, 4, 2, 3)), dma((7,)), dma((8,)), dma((4,)),

time: 229 us -> 193 us (0.84)
  the two profiles are of different devices: /device:TPU:16 before, /device:TPU:0 now
where the time goes in v5:
time: 193 us
  Pallas kernels  192 us (99%)
    pallas_call x1, Pallas kernels, on_this_slice(): pl.pallas_call(mega_kernel, out_shape=(jax.ShapeDtypeStruct((seq, width),...  185 us
    pallas_call x1, Pallas kernels, on_this_slice(): pl.pallas_call(finish_kernel, grid=(seq // 256,), out_shape=(f32(seq, wid...  7.13 us

profile of v5, /device:TPU:0, one launch (start us, length us, event | category | flops | bytes accessed | tf_op | source)
XLA Modules:
  0.0 193.0 jit_solution(16946649229608996613)
XLA Ops:
  0.6 185.1 %layer.1 = (bf16[1536,768]{1,0:T(8,128)(2,1)}, bf16[3,512,768]{2,1,0:T(8,128)(2,1)}, f32[96,192]{1,0:T(8,128)}, f32[96,192]{1,0:T(8,128)}, f32[96,192]{1,0:T(8,1...) custom-call(s32[1,8]{1,0:T(1,128)} %len_ref.1, ...), custom_call_target="tpu_custom_call" | custom-call | tf_op jit(solution)/shard_map/layer/pallas_call | solution.py:1265
  185.7 7.1 %finish.1 = (f32[1536,768]{1,0:T(8,128)}, bf16[1536,768]{1,0:T(8,128)(2,1)}, f32[96,192]{1,0:T(8,128)}, f32[96,192]{1,0:T(8,128)}, f32[96,192]{1,0:T(8,128)}, /*...) custom-call(bf16[1536,768]{1,0:T(8,128)(2,1)} %bitcast.13, ...), custom_call_target="tpu_custom_call" | custom-call | tf_op jit(solution)/shard_map/finish/pallas_call | solution.py:1303

commit v6 on v5

--- a/solution.py
+++ b/solution.py
@@ -960,13 +960,14 @@
         @pl.when(i == 3)
         def _():
             ag.across(1, 3)
+            rs.step(0)
 
         m = net.group(i)
         ag.complete(1, i)
 
         @pl.when(i == 3)
         def _():
-            rs.step(0)
+            rs.step(1)
 
         for lo in (0, 256):
             w_gate = rows768(w, m, 768 + lo, 1024 + lo)
@@ -1006,7 +1007,6 @@
         return c
 
     lax.fori_loop(0, 4, ffn_back, 0)
-    rs.step(1)
 
     def hidden_back(j, total):
         at = pl.ds(pl.multiple_of(j * 128, 128), 128)
@@ -1034,9 +1034,13 @@
         def _():
             mids.relay(3)
 
-        @pl.when(i == 1)
+        @pl.when(i == 0)
         def _():
             rs.step(2)
+
+        @pl.when(i == 3)
+        def _():
+            rs.step(3)
 
         @pl.when(i == 2)
         def _():
@@ -1059,7 +1063,6 @@
     gg_attn = lax.fori_loop(0, CAP // 128, input_back, jnp.zeros((1, 768), F32))
     pool[me] = n_b[...]
     rows.start()
-    rs.step(3)
     gg = jnp.concatenate([gg_attn, gg_ffn, jnp.zeros((6, 768), F32)], axis=0)
     for d in range(8):
         gg_out[d] = pltpu.roll(gg, (768 - 96 * d) % 768, 1)[:, 0:128] if d else gg[:, 0:128]
@@ -1131,15 +1134,24 @@
             u = (0.5 * a * (1.0 + gelu_parts(a)) * up).astype(BF16)
             acc[...] += nt(u, rows768(w, m, 1792, 2304))
 
-            @pl.when(jnp.logical_and(j == 2, m == 1))
+            @pl.when(jnp.logical_and(j == 2, m == 0))
+            def _():
+                rows.relay(1)
+                rows.relay(2)
+
+            @pl.when(jnp.logical_and(j == 1, m == 3))
             def _():
                 rs.step(5)
                 rs.gather_sides(1, 2)
+
+            @pl.when(jnp.logical_and(j == 2, m == 1))
+            def _():
+                rs.step(6)
                 rs.gather_sides(1, 3)
 
             @pl.when(jnp.logical_and(j == 3, m == 1))
             def _():
-                rs.step(6)
+                rs.step(8)
 
             return c
 
@@ -1148,33 +1160,28 @@
 
         @pl.when(j == 2)
         def _():
-            rows.relay(1)
-            rows.relay(2)
             rs.wave(1, 0)
+            rs.step(7)
 
         @pl.when(j == 3)
         def _():
-            rs.step(7)
+            rows.relay(3)
 
         return c
 
     lax.fori_loop(1, 4, ffn_out, 0)
+    for i in range(4):
+        rs.gather_sides(0, i)
+    rs.wave(0, 0)
 
     def place_out(j, c):
         at = pl.ds(pl.multiple_of(j * 256, 256), 256)
         pick = drops(0, j * 256, 256, 4)
-        value = nn(pick[:, 0:CAP], hx[0])
-        for b in range(1, 4):
-            value = value + nn(pick[:, b * CAP : (b + 1) * CAP], hx[b])
-        out_ref[at, :] = value.astype(BF16)
+        out_ref[at, :] = nn(pick, hx[...].reshape(4 * CAP, 768)).astype(BF16)
         return c
 
     lax.fori_loop(0, seq // 256, place_out, 0)
-    rs.step(8)
-    rows.relay(3)
     rs.wave(1, 1)
-    for i in range(3):
-        rs.gather_sides(0, i)
 
     def place_rows(bs, first):
         def body(j, c):
@@ -1189,8 +1196,6 @@
         lax.fori_loop(0, 3, body, 0)
 
     place_rows([me, rows.arrived(1), rows.arrived(2)], True)
-    rs.gather_sides(0, 3)
-    rs.wave(0, 0)
     rs.wave(1, 2)
     rs.wave(0, 1)
     ffn_sum = rs.total(1)
@@ -1298,11 +1303,11 @@
     )(lengths, tokens.reshape(2, 4, 2, 96, width), cotangent.reshape(2, 4, 2, 96, width), query_weight, key_weight,
       value_weight, out_weight, gate_weight, up_weight, down_weight.T, attn_gain.reshape(1, 96), ffn_gain.reshape(1, 96))
     rest = (out, gq, gk, gv, go, gate, up, down, gain_a, gain_f)
-    block = pl.BlockSpec((256, width), lambda i: (i, 0))
+    block = pl.BlockSpec((512, width), lambda i: (i, 0))
     whole = [pl.BlockSpec(a.shape, lambda i: (0, 0)) for a in rest[1:]]
     gt, out, gq, gk, gv, go, gate, up, down, gain_a, gain_f = pl.pallas_call(
         finish_kernel,
-        grid=(seq // 256,),
+        grid=(seq // 512,),
         out_shape=(f32(seq, width),) + tuple(jax.ShapeDtypeStruct(a.shape, a.dtype) for a in rest),
         in_specs=[block, block] + whole,
         out_specs=(block, block) + tuple(whole),

time: 193 us -> 187 us (0.969)
  Pallas kernels: 192 us -> 186 us
    pallas_call x1, Pallas kernels: 185 us -> 180 us  [on_this_slice(): pl.pallas_call(mega_kernel, out_shape=(jax.ShapeDtypeStruct((seq, width),...]
where the time goes in v6:
time: 187 us
  Pallas kernels  186 us (99%)
    pallas_call x1, Pallas kernels, on_this_slice(): pl.pallas_call(mega_kernel, out_shape=(jax.ShapeDtypeStruct((seq, width),...  180 us
    pallas_call x1, Pallas kernels, on_this_slice(): pl.pallas_call(finish_kernel, grid=(seq // 512,), out_shape=(f32(seq, wid...  6.45 us

profile of v6, /device:TPU:0, one launch (start us, length us, event | category | flops | bytes accessed | tf_op | source)
XLA Modules:
  0.0 187.0 jit_solution(2131164645610267702)
XLA Ops:
  0.6 179.7 %layer.1 = (bf16[1536,768]{1,0:T(8,128)(2,1)}, bf16[3,512,768]{2,1,0:T(8,128)(2,1)}, f32[96,192]{1,0:T(8,128)}, f32[96,192]{1,0:T(8,128)}, f32[96,192]{1,0:T(8,1...) custom-call(s32[1,8]{1,0:T(1,128)} %len_ref.1, ...), custom_call_target="tpu_custom_call" | custom-call | tf_op jit(solution)/shard_map/layer/pallas_call | solution.py:1270
  180.4 6.4 %finish.1 = (f32[1536,768]{1,0:T(8,128)}, bf16[1536,768]{1,0:T(8,128)(2,1)}, f32[96,192]{1,0:T(8,128)}, f32[96,192]{1,0:T(8,128)}, f32[96,192]{1,0:T(8,128)}, /*...) custom-call(bf16[1536,768]{1,0:T(8,128)(2,1)} %bitcast.13, ...), custom_call_target="tpu_custom_call" | custom-call | tf_op jit(solution)/shard_map/finish/pallas_call | solution.py:1308

commit v7 on v6

--- a/solution.py
+++ b/solution.py
@@ -713,7 +713,7 @@
     gain[...] = total
 
 
-def build_package(w, net, q_ref, k_ref, v_ref, o_ref, g_ref, u_ref, d_ref):
+def build_attn_package(w, net, q_ref, k_ref, v_ref, o_ref):
     lanes = low_lanes()
     ot = o_ref[...].T
     pad = jnp.zeros((96, 64), F32)
@@ -727,6 +727,10 @@
         last = jnp.concatenate([ref[:, 128:192], pad], axis=1)
         extra = jnp.concatenate([ot[:, 64 * j : 64 * (j + 1)], pad], axis=1)
         put(2 * j + 1, jnp.where(lanes, last, pltpu.roll(extra, 64, 1)))
+
+
+def build_ffn_package(w, net, g_ref, u_ref, d_ref):
+    at = (net.z, net.chip, net.core)
     w[at[0], at[1], at[2], :, 768:1280] = g_ref[...].astype(BF16)
     w[at[0], at[1], at[2], :, 1280:1792] = u_ref[...].astype(BF16)
     w[at[0], at[1], at[2], :, 1792:2304] = d_ref[...].astype(BF16)
@@ -831,15 +835,16 @@
     rs = Reduce(net, g, slots, zbuf, rs_sems, ok)
     rows = RowGather(net, pool, gt_send, gt_recv, gt_ok)
     mids = RowGather(net, hx, hx_send, hx_recv, None)
-    build_package(w, net, q_ref, k_ref, v_ref, o_ref, gate_ref, up_ref, down_ref)
+    build_attn_package(w, net, q_ref, k_ref, v_ref, o_ref)
+    pl.semaphore_wait(barrier, 10)
+    ag.spread(0, 0)
+    build_ffn_package(w, net, gate_ref, up_ref, down_ref)
     pad = jnp.zeros((1, 32), F32)
     mine = jnp.concatenate([
         jnp.concatenate([ga_ref[...], pad], axis=1), jnp.concatenate([gf_ref[...], pad], axis=1),
         jnp.zeros((6, 128), F32)], axis=0)
     gain_parts[net.dp] = mine.astype(BF16).astype(F32)
-    pl.semaphore_wait(barrier, 10)
     gain_copies = share_gains(net, gain_parts, gn_send, gn_recv)
-    ag.spread(0, 0)
 
     place = placement(len_ref, bins)
     lse[...] = jnp.zeros_like(lse)
@@ -1173,6 +1178,7 @@
     for i in range(4):
         rs.gather_sides(0, i)
     rs.wave(0, 0)
+    rs.wave(1, 1)
 
     def place_out(j, c):
         at = pl.ds(pl.multiple_of(j * 256, 256), 256)
@@ -1181,7 +1187,6 @@
         return c
 
     lax.fori_loop(0, seq // 256, place_out, 0)
-    rs.wave(1, 1)
 
     def place_rows(bs, first):
         def body(j, c):

time: 187 us -> 187 us (level)
  no operation moved by 1% of the time
where the time goes in v7:
time: 187 us
  Pallas kernels  186 us (99%)
    pallas_call x1, Pallas kernels, on_this_slice(): pl.pallas_call(mega_kernel, out_shape=(jax.ShapeDtypeStruct((seq, width),...  180 us
    pallas_call x1, Pallas kernels, on_this_slice(): pl.pallas_call(finish_kernel, grid=(seq // 512,), out_shape=(f32(seq, wid...  6.45 us

profile of v7, /device:TPU:0, one launch (start us, length us, event | category | flops | bytes accessed | tf_op | source)
XLA Modules:
  0.0 186.9 jit_solution(7317403535406118037)
XLA Ops:
  0.6 179.6 %layer.1 = (bf16[1536,768]{1,0:T(8,128)(2,1)}, bf16[3,512,768]{2,1,0:T(8,128)(2,1)}, f32[96,192]{1,0:T(8,128)}, f32[96,192]{1,0:T(8,128)}, f32[96,192]{1,0:T(8,1...) custom-call(s32[1,8]{1,0:T(1,128)} %len_ref.1, ...), custom_call_target="tpu_custom_call" | custom-call | tf_op jit(solution)/shard_map/layer/pallas_call | solution.py:1275
  180.3 6.4 %finish.1 = (f32[1536,768]{1,0:T(8,128)}, bf16[1536,768]{1,0:T(8,128)(2,1)}, f32[96,192]{1,0:T(8,128)}, f32[96,192]{1,0:T(8,128)}, f32[96,192]{1,0:T(8,128)}, /*...) custom-call(bf16[1536,768]{1,0:T(8,128)(2,1)} %bitcast.13, ...), custom_call_target="tpu_custom_call" | custom-call | tf_op jit(solution)/shard_map/finish/pallas_call | solution.py:1313
